TPU v7x, 256 devices: a whole 4x4x8 slice. The times are simulated.
256 devices in a mesh: segment: 8 (over x_hi, y), tp: 32 (over x_lo, z, core).
Axes of the slice: x: 4 (x_hi: 2, x_lo: 2; x = x_hi * 2 + x_lo), y: 4, z: 8, core: 2. Of those that a mesh axis runs over, the one named last changes fastest.
Arguments:
- queries: bfloat16 [256, 256, 8192], P(('segment', 'tp'))
- caption_kv: bfloat16 [256, 256, 2048], P(('segment', 'tp')), may hold values from -6 to 6
- caption_len: int32 [256], P(('segment', 'tp')), may hold values from 64 to 256
- image_kv: bfloat16 [256, 48, 2048], P(('segment', 'tp')), may hold values from -6 to 6
- patch_count: int32 [256], replicated, may hold values from 12 to 48
- image_list: int32 [32, 8], replicated, may hold values from 0 to 255, as said below
- pref_order: int32 [32, 8], replicated, may hold values from 0 to 7, each once within a row
- reward_dir: float32 [8192], replicated, may hold values from -1.8 to 1.8
Outputs:
- loss_total: float32 [], replicated
- rewards: float32 [256], P(('segment', 'tp'))
- image_grad: float32 [256, 48, 2048], P(('segment', 'tp'))
Inputs may be any that keep to these rules, and one draw needn't show every extreme that they name: `image_list`: the image in place j of a group g has its id in the block of device (section s, column (g % 4) * 8 + j) for some section s: ids run by owner, section-major, 1 per owner, so device (s, c) owns ids (s * 32 + c) * 1 onward. Group g lies in section g // 4. `pref_order`: each row is a ranking of the 8 captions of its group.
All inputs are finite; a program needn't handle non-finite values.
Results may differ from a plain program's by a relative error of at most 0.03.
Values may be sent and summed in bfloat16 or wider, within the bound.
No kernel may reach another device: no remote copies, remote signals or barrier semaphores. Data moves between devices by JAX's collectives and lax.ppermute only.
A program may use at most 128 MiB of HBM per device.

v0:
```python
import math

import jax
import jax.numpy as jnp
from jax import lax
from jax.sharding import PartitionSpec as P

D = 8192
KV_HEADS = 8
HEAD_DIM = 128
CAP_LEN = 256
PATCHES = 48
CAPS = 8
GROUP_HEADS = 8
KV_WIDTH = 2048


norm_eps = 1e-06
loss_scale = 65536.0


def partner_2(value, axis, stride):
    mask = 2**stride
    pairs = [(source, source ^ mask) for source in range(lax.axis_size(axis))]
    return lax.ppermute(value, axis, pairs)


def head_scores(query_head, key_head, key_valid, scaling):
    scores = (
        jnp.einsum("tgd,kd->gtk", query_head, key_head, preferred_element_type=jnp.float32)
        * scaling
    )
    return jnp.where(key_valid[None], scores, -jnp.inf)


def head_forward(members, key_valid, scaling):
    query_head, key_head, value_head = members
    scores = head_scores(query_head, key_head, key_valid, scaling)
    row_max = jnp.max(scores, axis=-1, keepdims=True)
    exponent = jnp.exp(scores - row_max)
    totals = jnp.sum(exponent, axis=-1, keepdims=True)
    weights = (exponent / totals).astype(jnp.bfloat16)
    output = jnp.einsum("gtk,kd->tgd", weights, value_head, preferred_element_type=jnp.float32)
    return (output, row_max, totals)


def caption_forward(query_rows, own_kv, group_images, counts, length, direction):
    scaling = 1.0 / math.sqrt(HEAD_DIM)
    query_heads = query_rows.reshape(CAP_LEN, KV_HEADS, GROUP_HEADS, HEAD_DIM).transpose(1, 0, 2, 3)
    image_tokens = group_images.reshape(CAPS * PATCHES, 2, KV_HEADS, HEAD_DIM)
    own_tokens = own_kv.reshape(CAP_LEN, 2, KV_HEADS, HEAD_DIM)
    keys_all = jnp.concatenate([image_tokens[:, 0], own_tokens[:, 0]], axis=0).transpose(1, 0, 2)
    values_all = jnp.concatenate([image_tokens[:, 1], own_tokens[:, 1]], axis=0).transpose(1, 0, 2)
    image_valid = (jnp.arange(PATCHES, dtype=jnp.int32)[None, :] < counts[:, None]).reshape(-1)
    token_pos = jnp.arange(CAP_LEN, dtype=jnp.int32)
    own_valid = token_pos[None, :] <= token_pos[:, None]
    key_valid = jnp.concatenate(
        [jnp.broadcast_to(image_valid[None, :], (CAP_LEN, CAPS * PATCHES)), own_valid], axis=1
    )
    outputs, maxima, totals = lax.map(
        lambda members: head_forward(members, key_valid, scaling),
        (query_heads, keys_all, values_all),
    )
    attended = outputs.transpose(1, 0, 2, 3).reshape(CAP_LEN, D)
    inv_rms = lax.rsqrt(jnp.mean(attended * attended, axis=-1, keepdims=True) + norm_eps)
    normed = attended * inv_rms
    per_token = jnp.sum(normed * direction[None, :], axis=-1)
    live_rows = token_pos < length
    length_f = length.astype(jnp.float32)
    reward = jnp.sum(jnp.where(live_rows, per_token, 0.0)) / length_f
    cached = (
        query_heads,
        keys_all,
        values_all,
        key_valid,
        attended,
        normed,
        inv_rms,
        maxima,
        totals,
        live_rows,
    )
    return (reward, cached)


def head_backward(members, key_valid, scaling):
    query_head, key_head, value_head, grad_head, row_max, totals, delta_head = members
    scores = head_scores(query_head, key_head, key_valid, scaling)
    probs = jnp.exp(scores - row_max) / totals
    weights = probs.astype(jnp.bfloat16)
    value_grad = jnp.einsum("gtk,tgd->kd", weights, grad_head, preferred_element_type=jnp.float32)
    weight_grad = jnp.einsum(
        "tgd,kd->gtk", grad_head, value_head, preferred_element_type=jnp.float32
    )
    score_grad = (probs * (weight_grad - delta_head[..., None])).astype(jnp.bfloat16)
    key_grad = (
        jnp.einsum("gtk,tgd->kd", score_grad, query_head, preferred_element_type=jnp.float32)
        * scaling
    )
    return (key_grad, value_grad)


def caption_backward(cached, length, direction, scaled_grad):
    scaling = 1.0 / math.sqrt(HEAD_DIM)
    (
        query_heads,
        keys_all,
        values_all,
        key_valid,
        attended,
        normed,
        inv_rms,
        maxima,
        totals,
        live_rows,
    ) = cached
    image_keys = CAPS * PATCHES
    length_f = length.astype(jnp.float32)
    normed_grad = jnp.where(live_rows[:, None], direction[None, :] * (scaled_grad / length_f), 0.0)
    att_grad = inv_rms * (
        normed_grad - normed * jnp.mean(normed_grad * normed, axis=-1, keepdims=True)
    )
    att_grad_b = att_grad.astype(jnp.bfloat16)
    grad_heads = att_grad_b.reshape(CAP_LEN, KV_HEADS, GROUP_HEADS, HEAD_DIM).transpose(1, 0, 2, 3)
    delta_rows = jnp.sum(
        (att_grad_b.astype(jnp.float32) * attended).reshape(
            CAP_LEN, KV_HEADS, GROUP_HEADS, HEAD_DIM
        ),
        axis=-1,
    ).transpose(1, 2, 0)
    image_valid = key_valid[:, :image_keys]
    key_grads, value_grads = lax.map(
        lambda members: head_backward(members, image_valid, scaling),
        (
            query_heads,
            keys_all[:, :image_keys],
            values_all[:, :image_keys],
            grad_heads,
            maxima,
            totals,
            delta_rows,
        ),
    )
    stacked = jnp.stack([key_grads, value_grads], axis=0).transpose(2, 0, 1, 3)
    return stacked.reshape(CAPS, PATCHES, KV_WIDTH)


def group_loss(group_rewards, ranking):
    ranked = jnp.take(group_rewards, ranking)
    rank_pos = jnp.arange(CAPS, dtype=jnp.int32)
    upper_pairs = rank_pos[:, None] < rank_pos[None, :]
    margins = ranked[None, :] - ranked[:, None]
    return jnp.sum(jnp.where(upper_pairs, jax.nn.softplus(margins), 0.0))


def per_device(
    queries, caption_kv, caption_len, image_kv, patch_count, image_list, pref_order, reward_dir
):
    segment_count = lax.axis_size("segment")
    tp_count = lax.axis_size("tp")
    segment_idx = lax.axis_index("segment")
    column_idx = lax.axis_index("tp")
    owned_count = image_kv.shape[0]
    groups_here = tp_count // CAPS
    group_id = segment_idx * groups_here + column_idx // CAPS
    place = column_idx % CAPS
    image_ids = lax.dynamic_index_in_dim(image_list, group_id, 0, keepdims=False)
    own_id = jnp.take(image_ids, place)
    owner_segment = own_id // (owned_count * tp_count)
    own_remainder = own_id % owned_count
    column_images = lax.all_gather(image_kv, "segment", axis=0, tiled=True)
    own_image = lax.dynamic_slice_in_dim(
        column_images, owner_segment * owned_count + own_remainder, 1, 0
    )
    group_images = own_image
    for bit_pos in range(3):
        partner = partner_2(group_images, "tp", bit_pos)
        upper_half = column_idx // (1 << bit_pos) % 2 == 1
        group_images = jnp.where(
            upper_half,
            jnp.concatenate([partner, group_images], axis=0),
            jnp.concatenate([group_images, partner], axis=0),
        )
    counts = jnp.take(patch_count, image_ids)
    length = caption_len[0]
    reward, cached = caption_forward(
        queries[0], caption_kv[0], group_images, counts, length, reward_dir
    )
    section_rewards = lax.all_gather(reward.reshape(1), "tp", axis=0, tiled=True)
    section_orders = lax.dynamic_slice_in_dim(pref_order, segment_idx * groups_here, groups_here, 0)
    section_loss = jnp.sum(
        jax.vmap(group_loss)(section_rewards.reshape(groups_here, CAPS), section_orders)
    )
    loss_total = lax.psum(section_loss, "segment")
    group_rewards = lax.dynamic_slice_in_dim(section_rewards, column_idx // CAPS * CAPS, CAPS, 0)
    ranking = lax.dynamic_index_in_dim(pref_order, group_id, 0, keepdims=False)
    reward_grad = jnp.take(jax.grad(group_loss)(group_rewards, ranking), place)
    grads = caption_backward(cached, length, reward_dir, loss_scale * reward_grad)
    partial_sum = grads
    for bit_pos in (2, 1, 0):
        half_len = partial_sum.shape[0] // 2
        upper_half = column_idx // (1 << bit_pos) % 2 == 1
        kept_part = jnp.where(upper_half, partial_sum[half_len:], partial_sum[:half_len])
        sent_part = jnp.where(upper_half, partial_sum[:half_len], partial_sum[half_len:])
        partial_sum = kept_part + partner_2(sent_part, "tp", bit_pos)
    spread_grads = lax.dynamic_update_slice_in_dim(
        jnp.zeros((segment_count * owned_count, PATCHES, KV_WIDTH), jnp.float32),
        partial_sum,
        owner_segment * owned_count + own_remainder,
        0,
    )
    image_grad = lax.psum_scatter(spread_grads, "segment", scatter_dimension=0, tiled=True)
    return (loss_total, reward.reshape(1), image_grad)


def solution(mesh):
    placed = (
        P(("segment", "tp"), None, None),
        P(("segment", "tp"), None, None),
        P(("segment", "tp")),
        P(("segment", "tp"), None, None),
        P(),
        P(),
        P(),
        P(),
    )
    return jax.shard_map(
        per_device,
        mesh=mesh,
        in_specs=placed,
        out_specs=(P(), P(("segment", "tp")), P(("segment", "tp"), None, None)),
        check_vma=False,
    )
```

profile of v0, /device:TPU:32, one launch (start us, length us, event | category | flops | bytes accessed | tf_op | source)
XLA Modules:
  0.0 517.1 jit_solution(8312509071971382826)
XLA Ops:
  13.7 54.1 %all-gather.2.cloned.1.call-done = bf16[8,48,2048]{2,1,0:T(8,128)(2,1)} async-done(((bf16[1,48,2048]{2,1,0:T(8,128)(2,1)}), bf16[8,48,2048]{2,1,0:T(8,128)(2,1)}) %all-gather.2.cloned.1.call-update) | async-done | bytes 1572880 | tf_op jit(solution)/shard_map/all_gather | solution.py:171
  72.5 6.4 %copy.58 = bf16[1,256,8192]{1,2,0:T(8,128)(2,1)} copy(bf16[1,256,8192]{2,1,0:T(8,128)(2,1)} %param.12) | data formatting | bytes 8388608 | tf_op args[0]
  78.9 6.4 %copy.62 = bf16[8,256,8,128]{3,1,2,0:T(8,128)(2,1)} copy(bf16[8,256,8,128]{1,3,2,0:T(8,128)(2,1)} %bitcast.225) | data formatting | bytes 8388608 | tf_op jit(solution)/shard_map/while | solution.py:60
  86.9 2.6 collective-permute-start.2
  89.7 33.5 %collective-permute-done.2 = bf16[4,48,2048]{2,1,0:T(8,128)(2,1)S(1)} collective-permute-done((bf16[4,48,2048]{2,1,0:T(8,128)(2,1)S(1)}, bf16[4,48,2048]{2,1,0:T(8,128)(2,1)S(1)}, u32[]{:S(2)}, u32[]{:S(2)}) %collective-permute-start.2) | collective-permute-done | bytes 786464 | tf_op jit(solution)/shard_map/ppermute | solution.py:25
  128.0 53.5 %while.29 = (s32[]{:T(128)}, f32[8,256,8,128]{1,3,2,0:T(8,128)}, f32[8,8,256,1]{2,1,3,0:T(8,128)S(1)}, f32[8,8,256,1]{2,1,3,0:T(8,128)S(1)}, bf16[8,640,128]{1,2...) while((s32[]{:T(128)}, f32[8,256,8,128]{1,3,2,0:T(8,128)}, ...), condition=%wide.region_3.4_spmd, body=%wide.region_0.3_spmd.sunk | while | flops 686813184 | bytes 18196576 | solution.py:60
  128.0 2.0 fusion.97
  131.1 3.6 fusion.99
  134.7 2.0 fusion.97
  137.8 3.6 fusion.99
  141.4 2.0 fusion.97
  144.5 3.6 fusion.99
  148.1 2.0 fusion.97
  151.2 3.6 fusion.99
  154.8 2.0 fusion.97
  157.9 3.5 fusion.99
  164.5 3.6 fusion.99
  171.2 3.6 fusion.99
  177.9 3.5 fusion.99
  181.5 4.6 fusion.59
  190.5 53.6 %all-reduce = f32[32]{0:T(128)S(1)} all-reduce(f32[32]{0:T(128)S(1)} %dynamic-update-slice.2), channel_id=1, replica_groups=mesh['segment'=8,'tp'=32] {'tp'}, use_global_device_ids=true, to_apply=%add | all-reduce | flops 32 | bytes 256
  244.9 9.1 %copy.64 = f32[8,256,8,128]{3,1,2,0:T(8,128)} copy(f32[8,256,8,128]{1,3,2,0:T(8,128)} %get-tuple-element.105) | data formatting | bytes 16777216 | tf_op jit(solution)/shard_map/while | solution.py:60
  257.3 4.3 fusion.56
  261.6 4.9 fusion.60
  266.5 3.3 multiply_convert_fusion
  271.9 58.4 %while.30 = (s32[]{:T(128)}, f32[8,384,128]{2,1,0:T(8,128)}, f32[8,384,128]{2,1,0:T(8,128)}, bf16[8,384,128]{2,1,0:T(8,128)(2,1)}, bf16[8,256,8,128]{3,1,2,0:T(8...) while((s32[]{:T(128)}, f32[8,384,128]{2,1,0:T(8,128)}, ...), condition=%wide.region_15.16_spmd.clone, body=%wide.region_14.15_spmd.clone.sunk | while | flops 811646976 | bytes 12202493 | solution.py:132
  273.9 3.0 fusion.108
  276.9 2.3 fusion.109
  281.2 3.0 fusion.108
  284.2 2.3 fusion.109
  288.5 3.0 fusion.108
  291.5 2.3 fusion.109
  295.8 3.0 fusion.108
  298.8 2.3 fusion.109
  303.1 3.0 fusion.108
  306.1 2.3 fusion.109
  310.4 3.0 fusion.108
  313.4 2.3 fusion.109
  317.7 3.0 fusion.108
  320.7 2.3 fusion.109
  324.9 3.0 fusion.108
  328.0 2.3 fusion.109
  330.3 2.1 maximum_bitcast_fusion
  336.1 64.1 %collective-permute-done.3 = f32[4,48,2048]{2,1,0:T(8,128)} collective-permute-done((f32[4,48,2048]{2,1,0:T(8,128)}, f32[4,48,2048]{2,1,0:T(8,128)}, u32[]{:S(2)}, u32[]{:S(2)}) %collective-permute-start.3) | collective-permute-done | bytes 1572896 | tf_op jit(solution)/shard_map/ppermute | solution.py:25
  402.0 4.6 collective-permute-start.4
  406.7 17.7 %collective-permute-done.4 = f32[2,48,2048]{2,1,0:T(8,128)S(1)} collective-permute-done((f32[2,48,2048]{2,1,0:T(8,128)S(1)}, f32[2,48,2048]{2,1,0:T(8,128)S(1)}, u32[]{:S(2)}, u32[]{:S(2)}) %collective-permute-start.4) | collective-permute-done | bytes 786464 | tf_op jit(solution)/shard_map/ppermute | solution.py:25
  430.4 23.0 %psum.7 = f32[]{:T(128)} all-reduce(f32[]{:T(128)} %fusion.66), channel_id=1, replica_groups=mesh['segment'=8,'tp'=32] {'segment'}, use_global_device_ids=true, to_apply=%region_8.9 | all-reduce | flops 1 | bytes 8 | tf_op jit(solution)/shard_map/psum | solution.py:194
  453.4 55.7 %reduce-scatter.2.cloned.1.call-done = f32[1,48,2048]{2,1,0:T(8,128)} async-done(((f32[8,48,2048]{2,1,0:T(8,128)}), f32[1,48,2048]{2,1,0:T(8,128)}) %reduce-scatter.2.cloned.1.call-update) | async-done | bytes 393232 | tf_op jit(solution)/shard_map/reduce_scatter | solution.py:212
  (148 shorter events, 67.3 us)
Async XLA Ops:
  7.2 78.8 %copy-start = (s32[32,8]{0,1:T(8,128)S(1)}, s32[32,8]{0,1:T(8,128)}, u32[]{:S(2)}) copy-start(s32[32,8]{0,1:T(8,128)} %param.18) | copy-start | bytes 3076
  7.2 60.6 %all-gather.2.cloned.1.call-start = ((), (), s32[]{:S(2)}) async-start(), calls=%async_computation.1 | async-start | bytes 1769472 | tf_op jit(solution)/shard_map/all_gather | solution.py:171
  7.9 501.2 %reduce-scatter.2.cloned.1.call-start = ((), (), s32[]{:S(2)}) async-start(), calls=%async_computation.2 | async-start | bytes 3538944 | tf_op jit(solution)/shard_map/reduce_scatter | solution.py:212
  68.7 1.5 collective-permute-start
  70.3 16.4 %collective-permute-start.1 = (bf16[2,48,2048]{2,1,0:T(8,128)(2,1)S(1)}, bf16[2,48,2048]{2,1,0:T(8,128)(2,1)S(1)}, u32[]{:S(2)}, u32[]{:S(2)}) collective-permute-start(bf16[2,48,2048]{2,1,0:T(8,128)(2,1)S(1)} %maximum_select_fusion.2), channel_id=1, source_target_pairs={{0,2},{1,3},{2,0},{3,1},{4,6},{5,7},{6,4},{7,5},{8,10},{9,11},{10,... | collective-permute-start | bytes 1179656 | tf_op jit(solution)/shard_map/ppermute | solution.py:25
  78.9 7.3 %copy-start.6 = (u32[256]{0:T(256)S(1)}, u32[256]{0:T(256)}, u32[]{:S(2)}) copy-start(u32[256]{0:T(256)} %constant.328) | copy-start | bytes 3076
  86.9 36.3 %collective-permute-start.2 = (bf16[4,48,2048]{2,1,0:T(8,128)(2,1)S(1)}, bf16[4,48,2048]{2,1,0:T(8,128)(2,1)S(1)}, u32[]{:S(2)}, u32[]{:S(2)}) collective-permute-start(bf16[4,48,2048]{2,1,0:T(8,128)(2,1)S(1)} %maximum_select_fusion.1), channel_id=1, source_target_pairs={{0,4},{1,5},{2,6},{3,7},{4,0},{5,1},{6,2},{7,3},{8,12},{9,13},{10,... | collective-permute-start | bytes 2359304 | tf_op jit(solution)/shard_map/ppermute | solution.py:25
  123.4 1.0 copy-start.4
  128.0 58.2 %copy-start.5 = (f32[8192]{0:T(1024)S(1)}, f32[8192]{0:T(1024)}, u32[]{:S(2)}) copy-start(f32[8192]{0:T(1024)} %param.19) | copy-start | bytes 98308
  181.5 5.8 %copy-start.1 = (f32[8,256,8,128]{1,3,2,0:T(8,128)S(1)}, f32[8,256,8,128]{1,3,2,0:T(8,128)}, u32[]{:S(2)}) copy-start(f32[8,256,8,128]{1,3,2,0:T(8,128)} %get-tuple-element.105) | copy-start | bytes 25165828
  257.3 9.2 %slice-start = ((s8[8388608]{0:T(1024)(128)(4,1)}), s8[4194304]{0:T(1024)(128)(4,1)S(1)}, s32[]{:S(2)}) async-start(s8[8388608]{0:T(1024)(128)(4,1)} %bitcast.223), calls=%async_computation.3 | async-start | bytes 8388608
  261.6 4.9 slice-start.1
  266.5 3.4 copy-start.3
  335.0 65.3 %collective-permute-start.3 = (f32[4,48,2048]{2,1,0:T(8,128)}, f32[4,48,2048]{2,1,0:T(8,128)}, u32[]{:S(2)}, u32[]{:S(2)}) collective-permute-start(f32[4,48,2048]{2,1,0:T(8,128)} %select_n.310), channel_id=1, source_target_pairs={{0,4},{1,5},{2,6},{3,7},{4,0},{5,1},{6,2},{7,3},{8,12},{9,13},{10,... | collective-permute-start | bytes 4718600 | tf_op jit(solution)/shard_map/ppermute | solution.py:25
  402.0 22.4 %collective-permute-start.4 = (f32[2,48,2048]{2,1,0:T(8,128)S(1)}, f32[2,48,2048]{2,1,0:T(8,128)S(1)}, u32[]{:S(2)}, u32[]{:S(2)}) collective-permute-start(f32[2,48,2048]{2,1,0:T(8,128)S(1)} %slice_select_fusion.2), channel_id=1, source_target_pairs={{0,2},{1,3},{2,0},{3,1},{4,6},{5,7},{6,4},{7,5},{8,10},{9,11},{10,... | collective-permute-start | bytes 2359304 | tf_op jit(solution)/shard_map/ppermute | solution.py:25
  424.6 1.8 collective-permute-start.5
  426.8 1.7 copy-start.2
Sparse Core Ops, SparseCore 0:
  10.6 57.1 all-gather.1
  428.7 80.3 reduce-scatter.1
where the time goes:
time: 519 us; the launch traced here: 517 us
  waiting for transfers between devices  229 us (44%)
  matrix products  103 us (20%)
  blocking collectives  76.6 us (15%)
  local copies, waits for them, and re-layouts  47.4 us (9%)
  other arithmetic  34.7 us (7%)
  between operations  18.3 us (4%)
  starting transfers between devices  8.1 us (2%)
    ppermute x6, waiting for transfers between devices, partner_2(): return lax.ppermute(value, axis, pairs)  118 us
    reduce_scatter x1, waiting for transfers between devices, per_device(): lax.psum_scatter(spread_grads, 'segment', scatter_dimension=0, tiled=True)  55.7 us
    all_gather x1, waiting for transfers between devices, per_device(): column_images = lax.all_gather(image_kv, 'segment', axis=0, tiled=True)  54.1 us
    unnamed x1, blocking collectives  53.6 us
    dot_general x16, matrix products, head_scores(): jnp.einsum('tgd,kd->gtk', query_head, key_head, preferred_element_type=jn...  32 us
    dot_general x8, matrix products, head_forward(): jnp.einsum('gtk,kd->tgd', weights, value_head, preferred_element_type=jnp...  28.5 us
    dot_general x8, matrix products, head_backward(): jnp.einsum('gtk,tgd->kd', score_grad, query_head, preferred_element_type=...  24 us
    psum x1, blocking collectives, per_device(): loss_total = lax.psum(section_loss, 'segment')  23 us
  transfers between devices with their start and end apart: 8, of which 7 were waited for; matrix products, arithmetic and copies ran while one was open for 5% of the time, Pallas kernels for 0%

commit v1 on v0

v1 whole, which is shorter than its diff:
```python
import math

import jax
import jax.numpy as jnp
from jax import lax
from jax.experimental import pallas as pl
from jax.experimental.pallas import tpu as pltpu
from jax.sharding import PartitionSpec as P

D = 8192
KV_HEADS = 8
HEAD_DIM = 128
CAP_LEN = 256
PATCHES = 48
CAPS = 8
GROUP_HEADS = 8
KV_WIDTH = 2048
COLUMNS = 32
IMG_SLOTS = CAPS * PATCHES
COEFS = KV_HEADS * GROUP_HEADS
WIDE = KV_WIDTH + 2 * COEFS
HALF = CAP_LEN // 2

norm_eps = 1e-06
loss_scale = 65536.0
scaling = 1.0 / math.sqrt(HEAD_DIM)
to_base2 = scaling * math.log2(math.e)

SMEM = pltpu.SMEM
VMEM = pltpu.VMEM
VMEM_LIMIT = 24 * 1024 * 1024

AT_Y, AT_SRC_Y, AT_SRC_X_SAME, AT_PARTNER_Y, AT_PLACE, AT_LEN = 0, 1, 2, 3, 4, 5
AT_COUNTS, AT_RANKING, AT_DEST = 8, 16, 24

REL = (0, 2, 4, 6, 1, 3, 5, 7)

SUM_LOW, SUM_HIGH = 2.0**-40, 2.0**60


def exact_dot(a, b, dims):
    return lax.dot_general(a, b, (dims, ((), ())), preferred_element_type=jnp.float32)


def meta_kernel(idx_ref, list_ref, count_ref, order_ref, len_ref, out_ref):
    seg = idx_ref[0]
    col = idx_ref[1]
    x = seg // 4
    y = seg % 4
    slot = col // CAPS
    place = col % CAPS

    def section_of(section):
        return list_ref[section * 4 + slot, place] // COLUMNS

    own = section_of(seg)
    partner = section_of((1 - x) * 4 + y)
    out_ref[AT_Y] = y
    out_ref[AT_SRC_Y] = own % 4
    out_ref[AT_SRC_X_SAME] = (own // 4 == x).astype(jnp.int32)
    out_ref[AT_PARTNER_Y] = partner % 4
    out_ref[AT_PLACE] = place
    out_ref[AT_LEN] = len_ref[0]
    group = seg * 4 + slot
    for i, rel in enumerate(REL):
        out_ref[AT_COUNTS + i] = count_ref[list_ref[group, place ^ rel]]
    for k in range(CAPS):
        out_ref[AT_RANKING + k] = order_ref[group, k]
    for k in range(4):
        dest = section_of(x * 4 + (y + 4 - k) % 4)
        here = (dest % 4 == y).astype(jnp.int32)
        out_ref[AT_DEST + k] = here * jnp.where(dest // 4 == x, 1, 2)


def make_meta(idx, image_list, patch_count, pref_order, caption_len):
    smem = pl.BlockSpec(memory_space=SMEM)
    return pl.pallas_call(
        meta_kernel,
        out_shape=jax.ShapeDtypeStruct((32,), jnp.int32),
        in_specs=[smem] * 5,
        out_specs=smem,
        name="meta",
    )(idx, image_list, patch_count, pref_order, caption_len)


def pick_partner_kernel(meta_ref, i0, i1, i2, i3, out_ref, sem):
    y = meta_ref[AT_Y]
    back = (y + 4 - meta_ref[AT_PARTNER_Y]) % 4
    for k, src in enumerate((i0, i1, i2, i3)):

        @pl.when(back == k)
        def _():
            copy = pltpu.make_async_copy(src, out_ref, sem)
            copy.start()
            copy.wait()


def pick_own_kernel(meta_ref, i0, i1, i2, i3, far, out_ref, sem):
    y = meta_ref[AT_Y]
    same = meta_ref[AT_SRC_X_SAME]
    back = jnp.where(same == 1, (y + 4 - meta_ref[AT_SRC_Y]) % 4, 4)
    for k, src in enumerate((i0, i1, i2, i3, far)):

        @pl.when(back == k)
        def _():
            copy = pltpu.make_async_copy(src, out_ref, sem)
            copy.start()
            copy.wait()


def pick(kernel, name, meta, *images):
    any_space = pl.BlockSpec(memory_space=pl.ANY)
    return pl.pallas_call(
        kernel,
        out_shape=jax.ShapeDtypeStruct(images[0].shape, images[0].dtype),
        in_specs=[pl.BlockSpec(memory_space=SMEM)] + [any_space] * len(images),
        out_specs=pl.BlockSpec(memory_space=VMEM),
        scratch_shapes=[pltpu.SemaphoreType.DMA],
        name=name,
    )(meta, *images)


def forward_kernel(meta_ref, q_ref, own_k_ref, own_v_ref, dir_ref, *rest):
    images = rest[:CAPS]
    p_ref, att_ref, inv_ref, stat_ref, reward_ref, ss_ref, rd_ref = rest[CAPS:]
    head = pl.program_id(0)
    key_cols = pl.ds(pl.multiple_of(head * HEAD_DIM, HEAD_DIM), HEAD_DIM)
    value_cols = pl.ds(pl.multiple_of((KV_HEADS + head) * HEAD_DIM, HEAD_DIM), HEAD_DIM)

    row = lax.broadcasted_iota(jnp.int32, (PATCHES, HEAD_DIM), 0)
    keys, values, marks = [], [], []
    for i, image in enumerate(images):
        live = row < meta_ref[AT_COUNTS + i]
        key = image[:, key_cols].astype(jnp.float32)
        keys.append(jnp.where(live, key, key[0:1, :]).astype(jnp.bfloat16))
        values.append(jnp.where(live, image[:, value_cols].astype(jnp.float32), 0.0))
        marks.append(live.astype(jnp.float32))
    image_keys = jnp.concatenate(keys, axis=0)
    own_keys = own_k_ref[...]
    values.append(own_v_ref[...].astype(jnp.float32))
    marks.append(jnp.ones((CAP_LEN, HEAD_DIM), jnp.float32))
    values_t = jnp.concatenate(values, axis=0).T
    marks_t = jnp.concatenate(marks, axis=0).T[:16]
    mixed = jnp.concatenate([values_t, marks_t], axis=0).astype(jnp.bfloat16)
    dir_t = dir_ref[...].T

    @pl.when(head == 0)
    def _():
        ss_ref[...] = jnp.zeros_like(ss_ref)
        rd_ref[...] = jnp.zeros_like(rd_ref)

    diagonal = lax.broadcasted_iota(jnp.int32, (HALF, HALF), 0) <= lax.broadcasted_iota(
        jnp.int32, (HALF, HALF), 1
    )
    minus = jnp.full((HALF, HALF), -jnp.inf, jnp.float32)

    def query(g):
        return q_ref[:, pl.ds(g * HEAD_DIM, HEAD_DIM)]

    def scores(g):
        q = query(g)
        s_img = exact_dot(image_keys, q, ((1,), (1,)))
        s_own = exact_dot(own_keys, q, ((1,), (1,)))
        return s_img, s_own

    def finish(g, p_all):
        out = exact_dot(mixed, p_all, ((1,), (0,)))
        total = out[HEAD_DIM : HEAD_DIM + 8]
        inv = 1.0 / total
        att = (out[:HEAD_DIM].reshape(16, 8, CAP_LEN) * inv[None]).reshape(HEAD_DIM, CAP_LEN)
        att_ref[pl.ds(g * HEAD_DIM, HEAD_DIM), :] = att
        inv_ref[pl.ds(g, 1), :] = inv[:1]
        return total

    def square_and_reward(g, dir_col):
        att = att_ref[pl.ds(g * HEAD_DIM, HEAD_DIM), :]
        ss = jnp.sum((att * att).reshape(16, 8, CAP_LEN), axis=0)
        rd = jnp.sum((att * dir_col).reshape(16, 8, CAP_LEN), axis=0)
        return ss, rd

    def own_block(p_a, p_b, p_c):
        return jnp.concatenate(
            [
                jnp.concatenate([p_a, p_b], axis=1),
                jnp.concatenate([jnp.zeros_like(p_c), p_c], axis=1),
            ],
            axis=0,
        )

    def plain(s, keep=None):
        s = s * to_base2
        if keep is not None:
            s = jnp.where(keep, s, minus)
        return jnp.exp2(s).astype(jnp.bfloat16)

    low = jnp.full((8, CAP_LEN), jnp.inf, jnp.float32)
    high = jnp.zeros((8, CAP_LEN), jnp.float32)
    ahead = scores(0)
    before = None
    for g in range(GROUP_HEADS + 1):
        if g < GROUP_HEADS:
            s_img, s_own = ahead
            if g + 1 < GROUP_HEADS:
                ahead = scores(g + 1)
            p_img = plain(s_img)
            p_ref[g] = p_img
            p_own = own_block(
                plain(s_own[:HALF, :HALF], diagonal),
                plain(s_own[:HALF, HALF:]),
                plain(s_own[HALF:, HALF:], diagonal),
            )
            p_all = jnp.concatenate([p_img, p_own], axis=0)
        if g > 0:
            total = finish(g - 1, before)
            low = jnp.minimum(low, total)
            high = jnp.maximum(high, total)
        before = p_all
    inside = jnp.all((low > SUM_LOW) & (high < SUM_HIGH))

    @pl.when(jnp.logical_not(inside))
    def _():
        @pl.loop(0, GROUP_HEADS)
        def _(g):
            s_img, s_own = scores(g)
            s_a = jnp.where(diagonal, s_own[:HALF, :HALF], minus)
            s_b = s_own[:HALF, HALF:]
            s_c = jnp.where(diagonal, s_own[HALF:, HALF:], minus)
            m_low = jnp.max(s_a, axis=0, keepdims=True)
            m_high = jnp.max(jnp.maximum(s_b, s_c), axis=0, keepdims=True)
            m = jnp.maximum(
                jnp.max(s_img, axis=0, keepdims=True), jnp.concatenate([m_low, m_high], axis=1)
            )
            m_low, m_high = m[:, :HALF], m[:, HALF:]
            p_img = jnp.exp2((s_img - m) * to_base2).astype(jnp.bfloat16)
            p_ref[g] = p_img
            p_own = own_block(
                jnp.exp2((s_a - m_low) * to_base2).astype(jnp.bfloat16),
                jnp.exp2((s_b - m_high) * to_base2).astype(jnp.bfloat16),
                jnp.exp2((s_c - m_high) * to_base2).astype(jnp.bfloat16),
            )
            finish(g, jnp.concatenate([p_img, p_own], axis=0))

    ss = ss_ref[...]
    rd = rd_ref[...]
    for g in range(GROUP_HEADS):
        ss_g, rd_g = square_and_reward(g, dir_t[:, g : g + 1])
        ss = ss + ss_g
        rd = rd + rd_g
    ss_ref[...] = ss
    rd_ref[...] = rd

    @pl.when(head == KV_HEADS - 1)
    def _():
        length = meta_ref[AT_LEN]
        inv_rms = lax.rsqrt(jnp.sum(ss, axis=0, keepdims=True) * (1.0 / D) + norm_eps)
        per_token = jnp.sum(rd, axis=0, keepdims=True) * inv_rms
        live = lax.broadcasted_iota(jnp.int32, (1, CAP_LEN), 1) < length
        length_f = jnp.full((1, CAP_LEN), length, jnp.int32).astype(jnp.float32)
        unit = jnp.where(live, 1.0 / length_f, 0.0)
        a = inv_rms * unit
        b = inv_rms * inv_rms * unit * per_token * (1.0 / D)
        stat_ref[...] = jnp.concatenate([a, b, jnp.zeros((6, CAP_LEN), jnp.float32)], axis=0)
        reward = jnp.sum(jnp.where(live, per_token, 0.0), axis=1, keepdims=True)
        reward_ref[...] = jnp.broadcast_to(reward / length_f[:, :1], (8, 128))


def forward(meta, q, own_kv, direction, images):
    whole = pl.BlockSpec((PATCHES, KV_WIDTH), lambda h: (0, 0))
    rows = GROUP_HEADS * HEAD_DIM
    return pl.pallas_call(
        forward_kernel,
        grid=(KV_HEADS,),
        in_specs=[
            pl.BlockSpec(memory_space=SMEM),
            pl.BlockSpec((CAP_LEN, rows), lambda h: (0, h)),
            pl.BlockSpec((CAP_LEN, HEAD_DIM), lambda h: (0, h)),
            pl.BlockSpec((CAP_LEN, HEAD_DIM), lambda h: (0, KV_HEADS + h)),
            pl.BlockSpec((GROUP_HEADS, HEAD_DIM), lambda h: (h, 0)),
        ]
        + [whole] * CAPS,
        out_specs=[
            pl.BlockSpec((GROUP_HEADS, IMG_SLOTS, CAP_LEN), lambda h: (h, 0, 0)),
            pl.BlockSpec((rows, CAP_LEN), lambda h: (h, 0)),
            pl.BlockSpec((GROUP_HEADS, CAP_LEN), lambda h: (h, 0)),
            pl.BlockSpec((8, CAP_LEN), lambda h: (0, 0)),
            pl.BlockSpec((8, 128), lambda h: (0, 0)),
        ],
        out_shape=[
            jax.ShapeDtypeStruct((KV_HEADS * GROUP_HEADS, IMG_SLOTS, CAP_LEN), jnp.bfloat16),
            jax.ShapeDtypeStruct((D, CAP_LEN), jnp.float32),
            jax.ShapeDtypeStruct((KV_HEADS * GROUP_HEADS, CAP_LEN), jnp.float32),
            jax.ShapeDtypeStruct((8, CAP_LEN), jnp.float32),
            jax.ShapeDtypeStruct((8, 128), jnp.float32),
        ],
        scratch_shapes=[VMEM((8, CAP_LEN), jnp.float32), VMEM((8, CAP_LEN), jnp.float32)],
        compiler_params=pltpu.CompilerParams(vmem_limit_bytes=VMEM_LIMIT),
        cost_estimate=pl.CostEstimate(
            flops=5_400_000_000, bytes_accessed=28_000_000, transcendentals=10_000_000
        ),
        name="forward",
    )(meta, q, own_kv, own_kv, direction, *images)


def backward_kernel(meta_ref, stat_ref, q_ref, dir_ref, p_ref, att_ref, inv_ref, *rest):
    images = rest[:CAPS]
    keep_ref, send_ref, coef_ref = rest[CAPS:]
    head = pl.program_id(0)
    key_cols = pl.ds(pl.multiple_of(head * HEAD_DIM, HEAD_DIM), HEAD_DIM)
    value_cols = pl.ds(pl.multiple_of((KV_HEADS + head) * HEAD_DIM, HEAD_DIM), HEAD_DIM)
    values = jnp.concatenate([image[:, value_cols] for image in images], axis=0)
    dir_t = dir_ref[...].T
    a = stat_ref[0:1, :]
    b = stat_ref[1:2, :]
    key_grad = jnp.zeros((IMG_SLOTS, HEAD_DIM), jnp.float32)
    value_grad = jnp.zeros((IMG_SLOTS, 2 * HEAD_DIM), jnp.float32)
    which = lax.broadcasted_iota(jnp.int32, (HEAD_DIM, CAP_LEN), 0)

    @pl.when(head == 0)
    def _():
        coef_ref[...] = jnp.zeros_like(coef_ref)

    for g in range(GROUP_HEADS):
        q = q_ref[:, g * HEAD_DIM : (g + 1) * HEAD_DIM]
        att = att_ref[g * HEAD_DIM : (g + 1) * HEAD_DIM, :]
        inv = inv_ref[g : g + 1, :]
        factor = a * inv
        rest_grad = -(b * inv) * att
        grad = (factor * dir_t[:, g : g + 1] + rest_grad).astype(jnp.bfloat16)
        delta = jnp.sum(grad.astype(jnp.float32) * att, axis=0, keepdims=True)
        factors = jnp.where(which == head * GROUP_HEADS + g, factor, 0.0)
        apart = jnp.concatenate([rest_grad, factors], axis=0).astype(jnp.bfloat16)
        p = p_ref[g]
        value_grad = value_grad + exact_dot(p, apart, ((1,), (1,)))
        weight_grad = exact_dot(values, grad, ((1,), (0,)))
        score_grad = (p.astype(jnp.float32) * (weight_grad - delta)).astype(jnp.bfloat16)
        key_grad = key_grad + exact_dot(score_grad, q, ((1,), (0,)))
    key_grad = key_grad * scaling
    row = lax.broadcasted_iota(jnp.int32, (PATCHES, HEAD_DIM), 0)
    for i in range(CAPS):
        live = row < meta_ref[AT_COUNTS + i]
        out_ref = keep_ref if i < 4 else send_ref
        part = slice(i * PATCHES, (i + 1) * PATCHES)
        out_ref[i % 4, :, key_cols] = jnp.where(live, key_grad[part], 0.0).astype(jnp.bfloat16)
        out_ref[i % 4, :, value_cols] = jnp.where(live, value_grad[part, :HEAD_DIM], 0.0).astype(jnp.bfloat16)
    coef_ref[...] += value_grad[:, HEAD_DIM:]

    @pl.when(head == KV_HEADS - 1)
    def _():
        for i in range(CAPS):
            live = row < meta_ref[AT_COUNTS + i]
            out_ref = keep_ref if i < 4 else send_ref
            coef = coef_ref[i * PATCHES : (i + 1) * PATCHES, :]
            out_ref[i % 4, :, KV_WIDTH:] = in_two(jnp.where(live, coef, 0.0))


def in_two(coef):
    first = coef.astype(jnp.bfloat16).astype(jnp.float32)
    return (first + pltpu.roll(coef - first, COEFS, 1)).astype(jnp.bfloat16)


def from_two(pair):
    pair = pair.astype(jnp.float32)
    lane = lax.broadcasted_iota(jnp.int32, pair.shape, 1)
    return jnp.where(lane < COEFS, pair + pltpu.roll(pair, COEFS, 1), 0.0)


def backward(meta, stat, q, direction, p, att, inv, images):
    whole = pl.BlockSpec((PATCHES, KV_WIDTH), lambda h: (0, 0))
    rows = GROUP_HEADS * HEAD_DIM
    half = jax.ShapeDtypeStruct((4, PATCHES, WIDE), jnp.bfloat16)
    return pl.pallas_call(
        backward_kernel,
        grid=(KV_HEADS,),
        in_specs=[
            pl.BlockSpec(memory_space=SMEM),
            pl.BlockSpec((8, CAP_LEN), lambda h: (0, 0)),
            pl.BlockSpec((CAP_LEN, rows), lambda h: (0, h)),
            pl.BlockSpec((GROUP_HEADS, HEAD_DIM), lambda h: (h, 0)),
            pl.BlockSpec((GROUP_HEADS, IMG_SLOTS, CAP_LEN), lambda h: (h, 0, 0)),
            pl.BlockSpec((rows, CAP_LEN), lambda h: (h, 0)),
            pl.BlockSpec((GROUP_HEADS, CAP_LEN), lambda h: (h, 0)),
        ]
        + [whole] * CAPS,
        out_specs=[pl.BlockSpec((4, PATCHES, WIDE), lambda h: (0, 0, 0))] * 2,
        out_shape=[half, half],
        scratch_shapes=[VMEM((IMG_SLOTS, HEAD_DIM), jnp.float32)],
        compiler_params=pltpu.CompilerParams(vmem_limit_bytes=VMEM_LIMIT),
        cost_estimate=pl.CostEstimate(
            flops=5_000_000_000, bytes_accessed=28_000_000, transcendentals=0
        ),
        name="backward",
    )(meta, stat, q, direction, p, att, inv, *images)


def scaled_sum_kernel(meta_ref, keep_ref, recv_ref, *rest):
    rewards = rest[:CAPS]
    own_ref, z1_ref, z2_ref, z3_ref, loss_ref = rest[CAPS:]
    place = meta_ref[AT_PLACE]
    lane = lax.broadcasted_iota(jnp.int32, (8, 128), 1)
    sub = lax.broadcasted_iota(jnp.int32, (8, 128), 0)
    by_lane = jnp.zeros((8, 128), jnp.float32)
    by_sub = jnp.zeros((8, 128), jnp.float32)
    for rel in range(CAPS):
        value = rewards[rel][...]
        by_lane = jnp.where(lane == (place ^ rel), value, by_lane)
        by_sub = jnp.where(sub == (place ^ rel), value, by_sub)
    rank_lane = jnp.full((8, 128), CAPS, jnp.int32)
    rank_sub = jnp.zeros((8, 128), jnp.int32)
    for k in range(CAPS):
        who = meta_ref[AT_RANKING + k]
        rank_lane = jnp.where(lane == who, k, rank_lane)
        rank_sub = jnp.where(sub == who, k, rank_sub)
    real = lane < CAPS
    better = real & (rank_sub < rank_lane)
    worse = real & (rank_sub > rank_lane)
    margin = by_lane - by_sub
    soft = jnp.maximum(margin, 0.0) + jnp.log1p(jnp.exp(-jnp.abs(margin)))
    pairs = jnp.where(better, soft, 0.0)
    loss = jnp.sum(jnp.sum(pairs, axis=0, keepdims=True), axis=1, keepdims=True)
    loss_ref[...] = jnp.broadcast_to(loss, (8, 128))
    up = 1.0 / (1.0 + jnp.exp(margin))
    down = 1.0 / (1.0 + jnp.exp(-margin))
    grads = jnp.where(worse, up, 0.0) - jnp.where(better, down, 0.0)
    grads = jnp.sum(grads, axis=1, keepdims=True) * loss_scale
    sub_col = sub[:, :1]
    mine = jnp.sum(jnp.where(sub_col == place, grads, 0.0), axis=0, keepdims=True)
    other = jnp.sum(jnp.where(sub_col == (place ^ 1), grads, 0.0), axis=0, keepdims=True)
    for i, out_ref in enumerate((own_ref, z1_ref, z2_ref, z3_ref)):
        kept, sent = keep_ref[i], recv_ref[i]
        total = kept[:, :KV_WIDTH].astype(jnp.float32) * mine
        total = total + sent[:, :KV_WIDTH].astype(jnp.float32) * other
        coef = from_two(kept[:, KV_WIDTH:]) * mine + from_two(sent[:, KV_WIDTH:]) * other
        out_ref[:, :KV_WIDTH] = total.astype(out_ref.dtype)
        out_ref[:, KV_WIDTH:] = coef if i == 0 else in_two(coef)


def scaled_sum(meta, keep, recv, rewards):
    vmem = pl.BlockSpec(memory_space=VMEM)
    wire = jax.ShapeDtypeStruct((PATCHES, WIDE), jnp.bfloat16)
    return pl.pallas_call(
        scaled_sum_kernel,
        in_specs=[pl.BlockSpec(memory_space=SMEM)] + [vmem] * (2 + CAPS),
        out_specs=[vmem] * 5,
        out_shape=[
            jax.ShapeDtypeStruct((PATCHES, WIDE), jnp.float32),
            wire,
            wire,
            wire,
            jax.ShapeDtypeStruct((8, 128), jnp.float32),
        ],
        compiler_params=pltpu.CompilerParams(vmem_limit_bytes=VMEM_LIMIT),
        name="scaled_sum",
    )(meta, keep, recv, *rewards)


def sum_kernel(own_ref, a_ref, b_ref, c_ref, dir_ref, *rest):
    losses, (out_ref, loss_ref) = rest[:2], rest[2:]
    own = own_ref[...]
    total, coef = own[:, :KV_WIDTH], own[:, KV_WIDTH:]
    for part in (a_ref, b_ref, c_ref):
        total = total + part[:, :KV_WIDTH].astype(jnp.float32)
        coef = coef + from_two(part[:, KV_WIDTH:])
    out_ref[:, : KV_WIDTH // 2] = total[:, : KV_WIDTH // 2].astype(out_ref.dtype)
    for head in range(KV_HEADS):
        cols = slice((KV_HEADS + head) * HEAD_DIM, (KV_HEADS + head + 1) * HEAD_DIM)
        value = total[:, cols]
        for j in range(head * GROUP_HEADS, (head + 1) * GROUP_HEADS):
            value = value + coef[:, j : j + 1] * dir_ref[j : j + 1, :]
        out_ref[:, cols] = value.astype(out_ref.dtype)
    loss_ref[...] = losses[0][...] + losses[1][...]


def group_sum(own, parts, direction, losses):
    vmem = pl.BlockSpec(memory_space=VMEM)
    return pl.pallas_call(
        sum_kernel,
        in_specs=[vmem] * 7,
        out_specs=[vmem] * 2,
        out_shape=[
            jax.ShapeDtypeStruct((PATCHES, KV_WIDTH), jnp.bfloat16),
            jax.ShapeDtypeStruct((8, 128), jnp.float32),
        ],
        name="group_sum",
    )(own, *parts, direction, *losses)


def sort_kernel(meta_ref, s0, s1, s2, s3, l0, l1, keep_ref, send_ref, loss_ref):
    total = jnp.zeros((PATCHES, KV_WIDTH), jnp.float32)
    kept = jnp.zeros((PATCHES, KV_WIDTH), jnp.float32)
    for k, part in enumerate((s0, s1, s2, s3)):
        dest = meta_ref[AT_DEST + k]
        value = part[...].astype(jnp.float32)
        kept = kept + jnp.where(dest == 1, value, 0.0)
        total = total + jnp.where(dest == 2, value, 0.0)
    keep_ref[...] = kept
    send_ref[...] = total.astype(send_ref.dtype)
    loss_ref[...] = l0[...] + l1[...]


def sort_by_owner(meta, parts, losses):
    vmem = pl.BlockSpec(memory_space=VMEM)
    return pl.pallas_call(
        sort_kernel,
        in_specs=[pl.BlockSpec(memory_space=SMEM)] + [vmem] * 6,
        out_specs=[vmem] * 3,
        out_shape=[
            jax.ShapeDtypeStruct((PATCHES, KV_WIDTH), jnp.float32),
            jax.ShapeDtypeStruct((PATCHES, KV_WIDTH), jnp.bfloat16),
            jax.ShapeDtypeStruct((8, 128), jnp.float32),
        ],
        name="sort_by_owner",
    )(meta, *parts, *losses)


def along_y(value, step):
    pairs = [(s, s // 4 * 4 + (s + step) % 4) for s in range(8)]
    return lax.ppermute(value, "segment", pairs)


def across(value, axis, mask):
    size = lax.axis_size(axis)
    return lax.ppermute(value, axis, [(i, i ^ mask) for i in range(size)])


def per_device(
    queries, caption_kv, caption_len, image_kv, patch_count, image_list, pref_order, reward_dir
):
    idx = jnp.stack([lax.axis_index("segment"), lax.axis_index("tp")]).astype(jnp.int32)
    image = image_kv[0]
    q = queries[0]
    direction = reward_dir.reshape(KV_HEADS * GROUP_HEADS, HEAD_DIM)
    meta = make_meta(idx, image_list, patch_count, pref_order, caption_len)

    column = [image] + [along_y(image, step) for step in (1, 2, 3)]
    far = across(pick(pick_partner_kernel, "pick_partner", meta, *column), "segment", 4)
    own = pick(pick_own_kernel, "pick_own", meta, *column, far)
    same_core = [own] + [across(own, "tp", mask) for mask in (2, 4, 6)]
    images = same_core + [across(one, "tp", 1) for one in same_core]

    p, att, inv, stat, reward = forward(meta, q, caption_kv[0], direction, images)
    rewards = [reward] + [across(reward, "tp", mask) for mask in range(1, CAPS)]
    keep, send = backward(meta, stat, q, direction, p, att, inv, images)
    recv = across(send, "tp", 1)
    mine, to_z1, to_z2, to_z3, loss = scaled_sum(meta, keep, recv, rewards)
    parts = [across(to_z1, "tp", 2), across(to_z2, "tp", 4), across(to_z3, "tp", 6)]
    loss = loss + across(loss, "tp", 8)
    total, loss = group_sum(mine, parts, direction, (loss, across(loss, "tp", 16)))
    totals = [total] + [along_y(total, step) for step in (1, 2, 3)]
    loss = loss + across(loss, "segment", 1)
    kept, away, loss = sort_by_owner(meta, totals, (loss, across(loss, "segment", 2)))
    loss = loss + across(loss, "segment", 4)
    image_grad = kept + across(away, "segment", 4).astype(jnp.float32)
    return (loss[0, 0], reward[0, :1], image_grad[None])


def solution(mesh):
    placed = (
        P(("segment", "tp"), None, None),
        P(("segment", "tp"), None, None),
        P(("segment", "tp")),
        P(("segment", "tp"), None, None),
        P(),
        P(),
        P(),
        P(),
    )
    return jax.shard_map(
        per_device,
        mesh=mesh,
        in_specs=placed,
        out_specs=(P(), P(("segment", "tp")), P(("segment", "tp"), None, None)),
        check_vma=False,
    )
```

time: 519 us -> 198 us (0.38)
  waiting for transfers between devices: 229 us -> 49.1 us
  matrix products: 103 us -> 0 us
  Pallas kernels: 0 us -> 82.2 us
  blocking collectives: 76.6 us -> 0 us
  starting transfers between devices: 8.1 us -> 45.3 us
  local copies, waits for them, and re-layouts: 47.4 us -> 14.4 us
  other arithmetic: 34.7 us -> 3.79 us
  between operations: 18.3 us -> 1.47 us
    dot_general x40 -> x0, matrix products: 103 us -> none  [the longest x16 32 us: head_scores(): jnp.einsum('tgd,kd->gtk', query_head, key_head, preferred_element_type=jn...]
    pallas_call x0 -> x8, Pallas kernels: none -> 82.2 us  [the longest x1 53.5 us: forward(): pl.pallas_call(forward_kernel, grid=(KV_HEADS,), in_specs=[pl.BlockSpec(m...]
    ppermute x6 -> x31, waiting for transfers between devices: 118 us -> 49.1 us  [the longest x25 47.3 us: across(): return lax.ppermute(value, axis, [(i, i ^ mask) for i in range(size)])]
    reduce_scatter x1 -> x0, waiting for transfers between devices: 55.7 us -> none  [per_device(): lax.psum_scatter(spread_grads, 'segment', scatter_dimension=0, tiled=True)]
    all_gather x1 -> x0, waiting for transfers between devices: 54.1 us -> none  [per_device(): column_images = lax.all_gather(image_kv, 'segment', axis=0, tiled=True)]
    unnamed x1 -> x0, blocking collectives: 53.6 us -> none
    ppermute x6 -> x31, starting transfers between devices: 8.02 us -> 45.3 us  [the longest x25 34.9 us: across(): return lax.ppermute(value, axis, [(i, i ^ mask) for i in range(size)])]
    reduce_sum x15 -> x0, other arithmetic: 25.1 us -> none  [the longest x8 8.59 us: head_forward(): totals = jnp.sum(exponent, axis=-1, keepdims=True)]
  transfers between devices with their start and end apart: 8 -> 31, of which waited for: 7 -> 14; matrix products, arithmetic and copies ran while one was open for 5% -> 3% of each run, Pallas kernels for 0% -> 1%
where the time goes in v1:
time: 198 us; the launch traced here: 196 us
  Pallas kernels  82.2 us (42%)
  waiting for transfers between devices  49.1 us (25%)
  starting transfers between devices  45.3 us (23%)
  local copies, waits for them, and re-layouts  14.4 us (7%)
  other arithmetic  3.79 us (2%)
    pallas_call x1, Pallas kernels, forward(): pl.pallas_call(forward_kernel, grid=(KV_HEADS,), in_specs=[pl.BlockSpec(m...  53.5 us
    ppermute x25, waiting for transfers between devices, across(): return lax.ppermute(value, axis, [(i, i ^ mask) for i in range(size)])  47.3 us
    ppermute x25, starting transfers between devices, across(): return lax.ppermute(value, axis, [(i, i ^ mask) for i in range(size)])  34.9 us
    pallas_call x1, Pallas kernels, backward(): pl.pallas_call(backward_kernel, grid=(KV_HEADS,), in_specs=[pl.BlockSpec(...  16.2 us
    unnamed x48, local copies, waits for them, and re-layouts  13.4 us
    ppermute x6, starting transfers between devices, along_y(): return lax.ppermute(value, 'segment', pairs)  10.4 us
    pallas_call x2, Pallas kernels, pick(): pl.pallas_call(kernel, out_shape=jax.ShapeDtypeStruct(images[0].shape, im...  4.58 us
  transfers between devices with their start and end apart: 31, of which 14 were waited for; matrix products, arithmetic and copies ran while one was open for 3% of the time, Pallas kernels for 1%

profile of v1, /device:TPU:32, one launch (start us, length us, event | category | flops | bytes accessed | tf_op | source)
XLA Modules:
  0.0 196.3 jit_solution(5376641223894590740)
XLA Ops:
  0.6 1.7 collective-permute-start
  2.3 2.9 %collective-permute-start.1 = (bf16[48,2048]{1,0:T(8,128)(2,1)}, bf16[48,2048]{1,0:T(8,128)(2,1)S(1)}, u32[]{:S(2)}, u32[]{:S(2)}) collective-permute-start(bf16[48,2048]{1,0:T(8,128)(2,1)} %bitcast.18), channel_id=1, source_target_pairs={{0,64},{32,96},{64,0},{96,32},{128,192},{160,224},{192,128},{224,1... | collective-permute-start | bytes 589832 | tf_op jit(solution)/shard_map/ppermute | solution.py:517
  5.2 1.3 collective-permute-start.2
  6.5 1.4 copy.11.list_ref
  7.9 1.4 copy.12.order_ref
  10.6 1.9 meta.1.meta_ref
  12.5 1.8 collective-permute-done.1.i2
  15.6 2.3 %pick_partner.1 = bf16[48,2048]{1,0:T(8,128)(2,1)} custom-call(s32[32]{0:T(128)} %meta.1.meta_ref, bf16[48,2048]{1,0:T(8,128)(2,1)} %bitcast.20, bf16[48,2048]{1,0:T(8,128)(2,1)} %copy-done.9, bf16[48,2048]{1,0:T(8,128)(2,1)} %copy-done.10, bf16[48,2048]{1,0:T(8,128)(2,1)} %copy-done.11), custom_call_target="tpu_custom_call" | custom-call | tf_op jit(solution)/shard_map/pick_partner/pallas_call | solution.py:113
  17.9 3.1 %collective-permute-start.3 = (bf16[48,2048]{1,0:T(8,128)(2,1)}, bf16[48,2048]{1,0:T(8,128)(2,1)S(1)}, u32[]{:S(2)}, u32[]{:S(2)}) collective-permute-start(bf16[48,2048]{1,0:T(8,128)(2,1)} %pick_partner.1), channel_id=1, source_target_pairs={{0,128},{32,160},{64,192},{96,224},{128,0},{160,32},{192,64},{224,... | collective-permute-start | bytes 589832 | tf_op jit(solution)/shard_map/ppermute | solution.py:522
  21.0 4.5 %collective-permute-done.3.far = bf16[48,2048]{1,0:T(8,128)(2,1)S(1)} collective-permute-done((bf16[48,2048]{1,0:T(8,128)(2,1)}, bf16[48,2048]{1,0:T(8,128)(2,1)S(1)}, u32[]{:S(2)}, u32[]{:S(2)}) %collective-permute-start.3) | collective-permute-done | bytes 196640 | tf_op jit(solution)/shard_map/ppermute | solution.py:522
  25.5 0.7 copy-done.18
  26.1 2.3 %pick_own.1.rest_0_ = bf16[48,2048]{1,0:T(8,128)(2,1)} custom-call(s32[32]{0:T(128)} %meta.1.meta_ref, bf16[48,2048]{1,0:T(8,128)(2,1)} %bitcast.21, bf16[48,2048]{1,0:T(8,128)(2,1)} %copy-done.9, bf16[48,2048]{1,0:T(8,128)(2,1)} %copy-done.10, bf16[48,2048]{1,0:T(8,128)(2,1)} %copy-done.11, bf16[48,2048]{1,0:T(8,128)(2,1)} %copy-done.18), custom_call_target="tpu_custom_call" | custom-call | tf_op jit(solution)/shard_map/pick_own/pallas_call | solution.py:113
  28.4 2.0 %collective-permute-start.6 = (bf16[48,2048]{1,0:T(8,128)(2,1)}, bf16[48,2048]{1,0:T(8,128)(2,1)S(1)}, u32[]{:S(2)}, u32[]{:S(2)}) collective-permute-start(bf16[48,2048]{1,0:T(8,128)(2,1)} %pick_own.1.rest_0_), channel_id=1, source_target_pairs={{0,6},{1,7},{2,4},{3,5},{4,2},{5,3},{6,0},{7,1},{8,14},{9,15},{10,... | collective-permute-start | bytes 589832 | tf_op jit(solution)/shard_map/ppermute | solution.py:522
  30.4 2.8 %collective-permute-start.4 = (bf16[48,2048]{1,0:T(8,128)(2,1)}, bf16[48,2048]{1,0:T(8,128)(2,1)S(1)}, u32[]{:S(2)}, u32[]{:S(2)}) collective-permute-start(bf16[48,2048]{1,0:T(8,128)(2,1)} %pick_own.1.rest_0_), channel_id=1, source_target_pairs={{0,2},{1,3},{2,0},{3,1},{4,6},{5,7},{6,4},{7,5},{8,10},{9,11},{10,... | collective-permute-start | bytes 589832 | tf_op jit(solution)/shard_map/ppermute | solution.py:522
  33.3 8.5 %collective-permute-done.6.rest_3_ = bf16[48,2048]{1,0:T(8,128)(2,1)S(1)} collective-permute-done((bf16[48,2048]{1,0:T(8,128)(2,1)}, bf16[48,2048]{1,0:T(8,128)(2,1)S(1)}, u32[]{:S(2)}, u32[]{:S(2)}) %collective-permute-start.6) | collective-permute-done | bytes 196640 | tf_op jit(solution)/shard_map/ppermute | solution.py:522
  41.7 1.0 collective-permute-done.4.rest_1_
  42.7 3.2 %collective-permute-done.5.rest_2_ = bf16[48,2048]{1,0:T(8,128)(2,1)S(1)} collective-permute-done((bf16[48,2048]{1,0:T(8,128)(2,1)}, bf16[48,2048]{1,0:T(8,128)(2,1)S(1)}, u32[]{:S(2)}, u32[]{:S(2)}) %collective-permute-start.5) | collective-permute-done | bytes 196640 | tf_op jit(solution)/shard_map/ppermute | solution.py:522
  46.0 1.4 collective-permute-done.9.rest_6_
  47.4 2.2 %copy-done = bf16[1,256,8192]{2,1,0:T(8,128)(2,1)S(1)} copy-done((bf16[1,256,8192]{2,1,0:T(8,128)(2,1)S(1)}, bf16[1,256,8192]{2,1,0:T(8,128)(2,1)}, u32[]{:S(2)}) %copy-start) | copy-done | bytes 4194328
  49.6 0.9 copy-done.1
  50.5 0.8 copy-done.4
  51.9 1.2 copy-done.8
  53.1 53.5 %forward.1 = (bf16[64,384,256]{2,1,0:T(8,128)(2,1)S(1)}, f32[8192,256]{1,0:T(8,128)S(1)}, f32[64,256]{1,0:T(8,128)S(1)}, f32[8,256]{1,0:T(8,128)S(1)}, f32[8,128]{1,0:T(8,128)S(1)}) custom-call(s32[32]{0:T(128)S(1)} %copy-done.6, bf16[256,8192]{1,0:T(8,128)(2,1)S(1)} %bitcast.10, bf16[256,2048]{1,0:T(8,128)(2,1)S(1)} %bitcast.15, ...), custom_call_target="tpu_custom_call" | custom-call | flops 5400000000 | bytes 28000000 | tf_op jit(solution)/shard_map/forward/pallas_call | solution.py:270
  106.6 16.2 %backward.1 = (bf16[4,48,2176]{2,1,0:T(8,128)(2,1)S(1)}, bf16[4,48,2176]{2,1,0:T(8,128)(2,1)S(1)}) custom-call(s32[32]{0:T(128)S(1)} %copy-done.7, f32[8,256]{1,0:T(8,128)S(1)} %get-tuple-element.20.stat_ref, bf16[256,8192]{1,0:T(8,128)(2,1)S(1)} %bitcast.11, f32[64,128]{1,0:T(8,128)S(1)} %bitcast.14, bf16[64,384,256]{2,1,0:T(8,128)(2,1)S(1)} %get-tuple-element.21.p_ref, ...), custom_call_target="tpu_custom_call" | custom-call | flops 5000000000 | bytes 28000000 | tf_op jit(solution)/shard_map/backward/pallas_call | solution.py:371
  123.5 1.9 collective-permute-start.13
  125.4 2.8 %collective-permute-start.15 = (f32[8,128]{1,0:T(8,128)S(1)}, f32[8,128]{1,0:T(8,128)S(1)}, u32[]{:S(2)}, u32[]{:S(2)}) collective-permute-start(f32[8,128]{1,0:T(8,128)S(1)} %get-tuple-element.26.rest_0_), channel_id=1, source_target_pairs={{0,4},{1,5},{2,6},{3,7},{4,0},{5,1},{6,2},{7,3},{8,12},{9,13},{10,... | collective-permute-start | bytes 12296 | tf_op jit(solution)/shard_map/ppermute | solution.py:522
  128.5 1.2 collective-permute-start.17
  130.0 2.1 %collective-permute-done.16.rest_5_ = f32[8,128]{1,0:T(8,128)S(1)} collective-permute-done((f32[8,128]{1,0:T(8,128)S(1)}, f32[8,128]{1,0:T(8,128)S(1)}, u32[]{:S(2)}, u32[]{:S(2)}) %collective-permute-start.16) | collective-permute-done | bytes 4128 | tf_op jit(solution)/shard_map/ppermute | solution.py:522
  132.7 1.2 scaled_sum.1
  134.0 0.8 copy-done.3
  134.7 4.7 %collective-permute-start.19 = (bf16[48,2176]{1,0:T(8,128)(2,1)S(1)}, bf16[48,2176]{1,0:T(8,128)(2,1)S(1)}, u32[]{:S(2)}, u32[]{:S(2)}) collective-permute-start(bf16[48,2176]{1,0:T(8,128)(2,1)S(1)} %get-tuple-element.28), channel_id=1, source_target_pairs={{0,2},{1,3},{2,0},{3,1},{4,6},{5,7},{6,4},{7,5},{8,10},{9,11},{10,... | collective-permute-start | bytes 626696 | tf_op jit(solution)/shard_map/ppermute | solution.py:522
  139.4 1.5 collective-permute-start.21
  140.9 5.2 %collective-permute-start.22 = (f32[8,128]{1,0:T(8,128)S(1)}, f32[8,128]{1,0:T(8,128)S(1)}, u32[]{:S(2)}, u32[]{:S(2)}) collective-permute-start(f32[8,128]{1,0:T(8,128)S(1)} %get-tuple-element.31), channel_id=1, source_target_pairs={{0,8},{1,9},{2,10},{3,11},{4,12},{5,13},{6,14},{7,15},{8,0},{9,1},... | collective-permute-start | bytes 12296 | tf_op jit(solution)/shard_map/ppermute | solution.py:522
  146.1 7.6 %collective-permute-done.22 = f32[8,128]{1,0:T(8,128)S(1)} collective-permute-done((f32[8,128]{1,0:T(8,128)S(1)}, f32[8,128]{1,0:T(8,128)S(1)}, u32[]{:S(2)}, u32[]{:S(2)}) %collective-permute-start.22) | collective-permute-done | bytes 4128 | tf_op jit(solution)/shard_map/ppermute | solution.py:522
  153.7 1.4 collective-permute-start.23
  155.1 2.2 %collective-permute-done.23.rest_1_ = f32[8,128]{1,0:T(8,128)S(1)} collective-permute-done((f32[8,128]{1,0:T(8,128)S(1)}, f32[8,128]{1,0:T(8,128)S(1)}, u32[]{:S(2)}, u32[]{:S(2)}) %collective-permute-start.23) | collective-permute-done | bytes 4128 | tf_op jit(solution)/shard_map/ppermute | solution.py:522
  157.3 2.4 %collective-permute-done.21.c_ref = bf16[48,2176]{1,0:T(8,128)(2,1)S(1)} collective-permute-done((bf16[48,2176]{1,0:T(8,128)(2,1)S(1)}, bf16[48,2176]{1,0:T(8,128)(2,1)S(1)}, u32[]{:S(2)}, u32[]{:S(2)}) %collective-permute-start.21) | collective-permute-done | bytes 208928 | tf_op jit(solution)/shard_map/ppermute | solution.py:522
  160.4 2.6 %group_sum.1 = (bf16[48,2048]{1,0:T(8,128)(2,1)}, f32[8,128]{1,0:T(8,128)}) custom-call(f32[48,2176]{1,0:T(8,128)} %copy-done.3, bf16[48,2176]{1,0:T(8,128)(2,1)} %copy-done.12, bf16[48,2176]{1,0:T(8,128)(2,1)} %copy-done.13, bf16[48,2176]{1,0:T(8,128)(2,1)} %copy-done.14, f32[64,128]{1,0:T(8,128)} %bitcast.12, f32[8,128]{1,0:T(8,128)} %copy-done.19, ...), custom_call_target="tpu_custom_call" | custom-call | tf_op jit(solution)/shard_map/group_sum/pallas_call | solution.py:475
  163.0 1.2 collective-permute-start.24
  164.2 3.3 %collective-permute-start.25 = (bf16[48,2048]{1,0:T(8,128)(2,1)}, bf16[48,2048]{1,0:T(8,128)(2,1)S(1)}, u32[]{:S(2)}, u32[]{:S(2)}) collective-permute-start(bf16[48,2048]{1,0:T(8,128)(2,1)} %get-tuple-element.32.s0), channel_id=1, source_target_pairs={{0,64},{32,96},{64,0},{96,32},{128,192},{160,224},{192,128},{224,1... | collective-permute-start | bytes 589832 | tf_op jit(solution)/shard_map/ppermute | solution.py:517
  167.5 2.0 %collective-permute-start.27 = (f32[8,128]{1,0:T(8,128)}, f32[8,128]{1,0:T(8,128)S(1)}, u32[]{:S(2)}, u32[]{:S(2)}) collective-permute-start(f32[8,128]{1,0:T(8,128)} %get-tuple-element.33), channel_id=1, source_target_pairs={{0,32},{32,0},{64,96},{96,64},{128,160},{160,128},{192,224},{224,1... | collective-permute-start | bytes 12296 | tf_op jit(solution)/shard_map/ppermute | solution.py:522
  169.5 5.9 %collective-permute-done.27 = f32[8,128]{1,0:T(8,128)S(1)} collective-permute-done((f32[8,128]{1,0:T(8,128)}, f32[8,128]{1,0:T(8,128)S(1)}, u32[]{:S(2)}, u32[]{:S(2)}) %collective-permute-start.27) | collective-permute-done | bytes 4128 | tf_op jit(solution)/shard_map/ppermute | solution.py:522
  176.1 1.4 collective-permute-start.28
  177.6 3.7 %collective-permute-done.28.l1 = f32[8,128]{1,0:T(8,128)S(1)} collective-permute-done((f32[8,128]{1,0:T(8,128)S(1)}, f32[8,128]{1,0:T(8,128)S(1)}, u32[]{:S(2)}, u32[]{:S(2)}) %collective-permute-start.28) | collective-permute-done | bytes 4128 | tf_op jit(solution)/shard_map/ppermute | solution.py:522
  182.7 2.3 %sort_by_owner.1 = (f32[48,2048]{1,0:T(8,128)}, bf16[48,2048]{1,0:T(8,128)(2,1)}, f32[8,128]{1,0:T(8,128)}) custom-call(s32[32]{0:T(128)} %meta.1.meta_ref, bf16[48,2048]{1,0:T(8,128)(2,1)} %get-tuple-element.32.s0, bf16[48,2048]{1,0:T(8,128)(2,1)} %copy-done.15, bf16[48,2048]{1,0:T(8,128)(2,1)} %copy-done.16, bf16[48,2048]{1,0:T(8,128)(2,1)} %copy-done.17, ...), custom_call_target="tpu_custom_call" | custom-call | tf_op jit(solution)/shard_map/sort_by_owner/pallas_call | solution.py:502
  185.0 3.0 %collective-permute-start.30 = (bf16[48,2048]{1,0:T(8,128)(2,1)}, bf16[48,2048]{1,0:T(8,128)(2,1)S(1)}, u32[]{:S(2)}, u32[]{:S(2)}) collective-permute-start(bf16[48,2048]{1,0:T(8,128)(2,1)} %get-tuple-element.36), channel_id=1, source_target_pairs={{0,128},{32,160},{64,192},{96,224},{128,0},{160,32},{192,64},{224,... | collective-permute-start | bytes 589832 | tf_op jit(solution)/shard_map/ppermute | solution.py:522
  189.0 4.3 %collective-permute-done.29 = f32[8,128]{1,0:T(8,128)S(1)} collective-permute-done((f32[8,128]{1,0:T(8,128)}, f32[8,128]{1,0:T(8,128)S(1)}, u32[]{:S(2)}, u32[]{:S(2)}) %collective-permute-start.29) | collective-permute-done | bytes 4128 | tf_op jit(solution)/shard_map/ppermute | solution.py:522
  194.5 1.8 add_bitcast_fusion
  (77 shorter events, 9.5 us)
Async XLA Ops:
  0.6 11.8 %collective-permute-start = (bf16[48,2048]{1,0:T(8,128)(2,1)}, bf16[48,2048]{1,0:T(8,128)(2,1)S(1)}, u32[]{:S(2)}, u32[]{:S(2)}) collective-permute-start(bf16[48,2048]{1,0:T(8,128)(2,1)} %bitcast.17), channel_id=1, source_target_pairs={{0,32},{32,64},{64,96},{96,0},{128,160},{160,192},{192,224},{224,1... | collective-permute-start | bytes 589832 | tf_op jit(solution)/shard_map/ppermute | solution.py:517
  2.3 11.9 %collective-permute-start.1 = (bf16[48,2048]{1,0:T(8,128)(2,1)}, bf16[48,2048]{1,0:T(8,128)(2,1)S(1)}, u32[]{:S(2)}, u32[]{:S(2)}) collective-permute-start(bf16[48,2048]{1,0:T(8,128)(2,1)} %bitcast.18), channel_id=1, source_target_pairs={{0,64},{32,96},{64,0},{96,32},{128,192},{160,224},{192,128},{224,1... | collective-permute-start | bytes 589832 | tf_op jit(solution)/shard_map/ppermute | solution.py:517
  5.2 9.0 %collective-permute-start.2 = (bf16[48,2048]{1,0:T(8,128)(2,1)}, bf16[48,2048]{1,0:T(8,128)(2,1)S(1)}, u32[]{:S(2)}, u32[]{:S(2)}) collective-permute-start(bf16[48,2048]{1,0:T(8,128)(2,1)} %bitcast.19), channel_id=1, source_target_pairs={{0,96},{32,0},{64,32},{96,64},{128,224},{160,128},{192,160},{224,1... | collective-permute-start | bytes 589832 | tf_op jit(solution)/shard_map/ppermute | solution.py:517
  12.4 1.8 copy-start.9
  17.9 7.6 %collective-permute-start.3 = (bf16[48,2048]{1,0:T(8,128)(2,1)}, bf16[48,2048]{1,0:T(8,128)(2,1)S(1)}, u32[]{:S(2)}, u32[]{:S(2)}) collective-permute-start(bf16[48,2048]{1,0:T(8,128)(2,1)} %pick_partner.1), channel_id=1, source_target_pairs={{0,128},{32,160},{64,192},{96,224},{128,0},{160,32},{192,64},{224,... | collective-permute-start | bytes 589832 | tf_op jit(solution)/shard_map/ppermute | solution.py:522
  25.5 0.7 copy-start.18
  28.4 13.3 %collective-permute-start.6 = (bf16[48,2048]{1,0:T(8,128)(2,1)}, bf16[48,2048]{1,0:T(8,128)(2,1)S(1)}, u32[]{:S(2)}, u32[]{:S(2)}) collective-permute-start(bf16[48,2048]{1,0:T(8,128)(2,1)} %pick_own.1.rest_0_), channel_id=1, source_target_pairs={{0,6},{1,7},{2,4},{3,5},{4,2},{5,3},{6,0},{7,1},{8,14},{9,15},{10,... | collective-permute-start | bytes 589832 | tf_op jit(solution)/shard_map/ppermute | solution.py:522
  30.4 12.3 %collective-permute-start.4 = (bf16[48,2048]{1,0:T(8,128)(2,1)}, bf16[48,2048]{1,0:T(8,128)(2,1)S(1)}, u32[]{:S(2)}, u32[]{:S(2)}) collective-permute-start(bf16[48,2048]{1,0:T(8,128)(2,1)} %pick_own.1.rest_0_), channel_id=1, source_target_pairs={{0,2},{1,3},{2,0},{3,1},{4,6},{5,7},{6,4},{7,5},{8,10},{9,11},{10,... | collective-permute-start | bytes 589832 | tf_op jit(solution)/shard_map/ppermute | solution.py:522
  33.3 12.7 %collective-permute-start.5 = (bf16[48,2048]{1,0:T(8,128)(2,1)}, bf16[48,2048]{1,0:T(8,128)(2,1)S(1)}, u32[]{:S(2)}, u32[]{:S(2)}) collective-permute-start(bf16[48,2048]{1,0:T(8,128)(2,1)} %pick_own.1.rest_0_), channel_id=1, source_target_pairs={{0,4},{1,5},{2,6},{3,7},{4,0},{5,1},{6,2},{7,3},{8,12},{9,13},{10,... | collective-permute-start | bytes 589832 | tf_op jit(solution)/shard_map/ppermute | solution.py:522
  33.3 12.7 %collective-permute-start.7 = (bf16[48,2048]{1,0:T(8,128)(2,1)}, bf16[48,2048]{1,0:T(8,128)(2,1)S(1)}, u32[]{:S(2)}, u32[]{:S(2)}) collective-permute-start(bf16[48,2048]{1,0:T(8,128)(2,1)} %pick_own.1.rest_0_), channel_id=1, source_target_pairs={{0,1},{1,0},{2,3},{3,2},{4,5},{5,4},{6,7},{7,6},{8,9},{9,8},{10,11... | collective-permute-start | bytes 589832 | tf_op jit(solution)/shard_map/ppermute | solution.py:522
  41.7 4.2 %collective-permute-start.10 = (bf16[48,2048]{1,0:T(8,128)(2,1)S(1)}, bf16[48,2048]{1,0:T(8,128)(2,1)S(1)}, u32[]{:S(2)}, u32[]{:S(2)}) collective-permute-start(bf16[48,2048]{1,0:T(8,128)(2,1)S(1)} %collective-permute-done.6.rest_3_), channel_id=1, source_target_pairs={{0,1},{1,0},{2,3},{3,2},{4,5},{5,4},{6,7},{7,6},{8,9},{9,8},{10,11... | collective-permute-start | bytes 589832 | tf_op jit(solution)/shard_map/ppermute | solution.py:522
  42.7 3.2 %collective-permute-start.8 = (bf16[48,2048]{1,0:T(8,128)(2,1)S(1)}, bf16[48,2048]{1,0:T(8,128)(2,1)S(1)}, u32[]{:S(2)}, u32[]{:S(2)}) collective-permute-start(bf16[48,2048]{1,0:T(8,128)(2,1)S(1)} %collective-permute-done.4.rest_1_), channel_id=1, source_target_pairs={{0,1},{1,0},{2,3},{3,2},{4,5},{5,4},{6,7},{7,6},{8,9},{9,8},{10,11... | collective-permute-start | bytes 589832 | tf_op jit(solution)/shard_map/ppermute | solution.py:522
  45.9 1.4 collective-permute-start.9
  47.4 2.2 %copy-start = (bf16[1,256,8192]{2,1,0:T(8,128)(2,1)S(1)}, bf16[1,256,8192]{2,1,0:T(8,128)(2,1)}, u32[]{:S(2)}) copy-start(bf16[1,256,8192]{2,1,0:T(8,128)(2,1)} %param.8) | copy-start | bytes 12582916
  49.6 0.9 copy-start.1
  50.5 0.8 copy-start.4
  51.9 1.2 copy-start.8
  53.1 53.5 %copy-start.2 = (bf16[48,2048]{1,0:T(8,128)(2,1)S(1)}, bf16[48,2048]{1,0:T(8,128)(2,1)}, u32[]{:S(2)}) copy-start(bf16[48,2048]{1,0:T(8,128)(2,1)} %pick_own.1.rest_0_) | copy-start | bytes 589828
  53.1 53.5 %copy-start.5 = (f32[8192]{0:T(1024)S(1)}, f32[8192]{0:T(1024)}, u32[]{:S(2)}) copy-start(f32[8192]{0:T(1024)} %param.15) | copy-start | bytes 98308
  53.1 53.5 %copy-start.7 = (s32[32]{0:T(128)S(1)}, s32[32]{0:T(128)}, u32[]{:S(2)}) copy-start(s32[32]{0:T(128)} %meta.1.meta_ref) | copy-start | bytes 388
  122.9 9.9 %collective-permute-start.11 = (bf16[4,48,2176]{2,1,0:T(8,128)(2,1)S(1)}, bf16[4,48,2176]{2,1,0:T(8,128)(2,1)S(1)}, u32[]{:S(2)}, u32[]{:S(2)}) collective-permute-start(bf16[4,48,2176]{2,1,0:T(8,128)(2,1)S(1)} %get-tuple-element.25), channel_id=1, source_target_pairs={{0,1},{1,0},{2,3},{3,2},{4,5},{5,4},{6,7},{7,6},{8,9},{9,8},{10,11... | collective-permute-start | bytes 2506760 | tf_op jit(solution)/shard_map/ppermute | solution.py:522
  123.1 5.1 %collective-permute-start.12 = (f32[8,128]{1,0:T(8,128)S(1)}, f32[8,128]{1,0:T(8,128)S(1)}, u32[]{:S(2)}, u32[]{:S(2)}) collective-permute-start(f32[8,128]{1,0:T(8,128)S(1)} %get-tuple-element.26.rest_0_), channel_id=1, source_target_pairs={{0,1},{1,0},{2,3},{3,2},{4,5},{5,4},{6,7},{7,6},{8,9},{9,8},{10,11... | collective-permute-start | bytes 12296 | tf_op jit(solution)/shard_map/ppermute | solution.py:522
  123.5 5.0 %collective-permute-start.13 = (f32[8,128]{1,0:T(8,128)S(1)}, f32[8,128]{1,0:T(8,128)S(1)}, u32[]{:S(2)}, u32[]{:S(2)}) collective-permute-start(f32[8,128]{1,0:T(8,128)S(1)} %get-tuple-element.26.rest_0_), channel_id=1, source_target_pairs={{0,2},{1,3},{2,0},{3,1},{4,6},{5,7},{6,4},{7,5},{8,10},{9,11},{10,... | collective-permute-start | bytes 12296 | tf_op jit(solution)/shard_map/ppermute | solution.py:522
  125.4 4.3 %collective-permute-start.14 = (f32[8,128]{1,0:T(8,128)S(1)}, f32[8,128]{1,0:T(8,128)S(1)}, u32[]{:S(2)}, u32[]{:S(2)}) collective-permute-start(f32[8,128]{1,0:T(8,128)S(1)} %get-tuple-element.26.rest_0_), channel_id=1, source_target_pairs={{0,3},{1,2},{2,1},{3,0},{4,7},{5,6},{6,5},{7,4},{8,11},{9,10},{10,... | collective-permute-start | bytes 12296 | tf_op jit(solution)/shard_map/ppermute | solution.py:522
  125.4 4.7 %collective-permute-start.15 = (f32[8,128]{1,0:T(8,128)S(1)}, f32[8,128]{1,0:T(8,128)S(1)}, u32[]{:S(2)}, u32[]{:S(2)}) collective-permute-start(f32[8,128]{1,0:T(8,128)S(1)} %get-tuple-element.26.rest_0_), channel_id=1, source_target_pairs={{0,4},{1,5},{2,6},{3,7},{4,0},{5,1},{6,2},{7,3},{8,12},{9,13},{10,... | collective-permute-start | bytes 12296 | tf_op jit(solution)/shard_map/ppermute | solution.py:522
  128.2 3.9 %collective-permute-start.16 = (f32[8,128]{1,0:T(8,128)S(1)}, f32[8,128]{1,0:T(8,128)S(1)}, u32[]{:S(2)}, u32[]{:S(2)}) collective-permute-start(f32[8,128]{1,0:T(8,128)S(1)} %get-tuple-element.26.rest_0_), channel_id=1, source_target_pairs={{0,5},{1,4},{2,7},{3,6},{4,1},{5,0},{6,3},{7,2},{8,13},{9,12},{10,... | collective-permute-start | bytes 12296 | tf_op jit(solution)/shard_map/ppermute | solution.py:522
  128.5 3.7 %collective-permute-start.17 = (f32[8,128]{1,0:T(8,128)S(1)}, f32[8,128]{1,0:T(8,128)S(1)}, u32[]{:S(2)}, u32[]{:S(2)}) collective-permute-start(f32[8,128]{1,0:T(8,128)S(1)} %get-tuple-element.26.rest_0_), channel_id=1, source_target_pairs={{0,6},{1,7},{2,4},{3,5},{4,2},{5,3},{6,0},{7,1},{8,14},{9,15},{10,... | collective-permute-start | bytes 12296 | tf_op jit(solution)/shard_map/ppermute | solution.py:522
  129.7 3.0 %collective-permute-start.18 = (f32[8,128]{1,0:T(8,128)S(1)}, f32[8,128]{1,0:T(8,128)S(1)}, u32[]{:S(2)}, u32[]{:S(2)}) collective-permute-start(f32[8,128]{1,0:T(8,128)S(1)} %get-tuple-element.26.rest_0_), channel_id=1, source_target_pairs={{0,7},{1,6},{2,5},{3,4},{4,3},{5,2},{6,1},{7,0},{8,15},{9,14},{10,... | collective-permute-start | bytes 12296 | tf_op jit(solution)/shard_map/ppermute | solution.py:522
  134.0 0.8 copy-start.3
  134.7 22.6 %collective-permute-start.19 = (bf16[48,2176]{1,0:T(8,128)(2,1)S(1)}, bf16[48,2176]{1,0:T(8,128)(2,1)S(1)}, u32[]{:S(2)}, u32[]{:S(2)}) collective-permute-start(bf16[48,2176]{1,0:T(8,128)(2,1)S(1)} %get-tuple-element.28), channel_id=1, source_target_pairs={{0,2},{1,3},{2,0},{3,1},{4,6},{5,7},{6,4},{7,5},{8,10},{9,11},{10,... | collective-permute-start | bytes 626696 | tf_op jit(solution)/shard_map/ppermute | solution.py:522
  139.4 17.9 %collective-permute-start.20 = (bf16[48,2176]{1,0:T(8,128)(2,1)S(1)}, bf16[48,2176]{1,0:T(8,128)(2,1)S(1)}, u32[]{:S(2)}, u32[]{:S(2)}) collective-permute-start(bf16[48,2176]{1,0:T(8,128)(2,1)S(1)} %get-tuple-element.29), channel_id=1, source_target_pairs={{0,4},{1,5},{2,6},{3,7},{4,0},{5,1},{6,2},{7,3},{8,12},{9,13},{10,... | collective-permute-start | bytes 626696 | tf_op jit(solution)/shard_map/ppermute | solution.py:522
  139.4 20.3 %collective-permute-start.21 = (bf16[48,2176]{1,0:T(8,128)(2,1)S(1)}, bf16[48,2176]{1,0:T(8,128)(2,1)S(1)}, u32[]{:S(2)}, u32[]{:S(2)}) collective-permute-start(bf16[48,2176]{1,0:T(8,128)(2,1)S(1)} %get-tuple-element.30), channel_id=1, source_target_pairs={{0,6},{1,7},{2,4},{3,5},{4,2},{5,3},{6,0},{7,1},{8,14},{9,15},{10,... | collective-permute-start | bytes 626696 | tf_op jit(solution)/shard_map/ppermute | solution.py:522
  140.9 12.8 %collective-permute-start.22 = (f32[8,128]{1,0:T(8,128)S(1)}, f32[8,128]{1,0:T(8,128)S(1)}, u32[]{:S(2)}, u32[]{:S(2)}) collective-permute-start(f32[8,128]{1,0:T(8,128)S(1)} %get-tuple-element.31), channel_id=1, source_target_pairs={{0,8},{1,9},{2,10},{3,11},{4,12},{5,13},{6,14},{7,15},{8,0},{9,1},... | collective-permute-start | bytes 12296 | tf_op jit(solution)/shard_map/ppermute | solution.py:522
  153.7 6.0 %copy-start.19 = (f32[8,128]{1,0:T(8,128)}, f32[8,128]{1,0:T(8,128)S(1)}, u32[]{:S(2)}) copy-start(f32[8,128]{1,0:T(8,128)S(1)} %add.12.rest_0_) | copy-start | bytes 12292
  153.7 3.6 %collective-permute-start.23 = (f32[8,128]{1,0:T(8,128)S(1)}, f32[8,128]{1,0:T(8,128)S(1)}, u32[]{:S(2)}, u32[]{:S(2)}) collective-permute-start(f32[8,128]{1,0:T(8,128)S(1)} %add.12.rest_0_), channel_id=1, source_target_pairs={{0,16},{1,17},{2,18},{3,19},{4,20},{5,21},{6,22},{7,23},{8,24},{9,... | collective-permute-start | bytes 12296 | tf_op jit(solution)/shard_map/ppermute | solution.py:522
  157.3 2.4 %copy-start.21 = (f32[8,128]{1,0:T(8,128)}, f32[8,128]{1,0:T(8,128)S(1)}, u32[]{:S(2)}) copy-start(f32[8,128]{1,0:T(8,128)S(1)} %collective-permute-done.23.rest_1_) | copy-start | bytes 12292
  157.3 2.4 %copy-start.12 = (bf16[48,2176]{1,0:T(8,128)(2,1)}, bf16[48,2176]{1,0:T(8,128)(2,1)S(1)}, u32[]{:S(2)}) copy-start(bf16[48,2176]{1,0:T(8,128)(2,1)S(1)} %collective-permute-done.19.a_ref) | copy-start | bytes 626692
  157.3 2.4 %copy-start.13 = (bf16[48,2176]{1,0:T(8,128)(2,1)}, bf16[48,2176]{1,0:T(8,128)(2,1)S(1)}, u32[]{:S(2)}) copy-start(bf16[48,2176]{1,0:T(8,128)(2,1)S(1)} %collective-permute-done.20.b_ref) | copy-start | bytes 626692
  159.7 0.7 copy-start.14
  163.0 18.3 %collective-permute-start.24 = (bf16[48,2048]{1,0:T(8,128)(2,1)}, bf16[48,2048]{1,0:T(8,128)(2,1)S(1)}, u32[]{:S(2)}, u32[]{:S(2)}) collective-permute-start(bf16[48,2048]{1,0:T(8,128)(2,1)} %get-tuple-element.32.s0), channel_id=1, source_target_pairs={{0,32},{32,64},{64,96},{96,0},{128,160},{160,192},{192,224},{224,1... | collective-permute-start | bytes 589832 | tf_op jit(solution)/shard_map/ppermute | solution.py:517
  164.2 17.1 %collective-permute-start.25 = (bf16[48,2048]{1,0:T(8,128)(2,1)}, bf16[48,2048]{1,0:T(8,128)(2,1)S(1)}, u32[]{:S(2)}, u32[]{:S(2)}) collective-permute-start(bf16[48,2048]{1,0:T(8,128)(2,1)} %get-tuple-element.32.s0), channel_id=1, source_target_pairs={{0,64},{32,96},{64,0},{96,32},{128,192},{160,224},{192,128},{224,1... | collective-permute-start | bytes 589832 | tf_op jit(solution)/shard_map/ppermute | solution.py:517
  167.5 13.8 %collective-permute-start.26 = (bf16[48,2048]{1,0:T(8,128)(2,1)}, bf16[48,2048]{1,0:T(8,128)(2,1)S(1)}, u32[]{:S(2)}, u32[]{:S(2)}) collective-permute-start(bf16[48,2048]{1,0:T(8,128)(2,1)} %get-tuple-element.32.s0), channel_id=1, source_target_pairs={{0,96},{32,0},{64,32},{96,64},{128,224},{160,128},{192,160},{224,1... | collective-permute-start | bytes 589832 | tf_op jit(solution)/shard_map/ppermute | solution.py:517
  167.5 8.0 %collective-permute-start.27 = (f32[8,128]{1,0:T(8,128)}, f32[8,128]{1,0:T(8,128)S(1)}, u32[]{:S(2)}, u32[]{:S(2)}) collective-permute-start(f32[8,128]{1,0:T(8,128)} %get-tuple-element.33), channel_id=1, source_target_pairs={{0,32},{32,0},{64,96},{96,64},{128,160},{160,128},{192,224},{224,1... | collective-permute-start | bytes 12296 | tf_op jit(solution)/shard_map/ppermute | solution.py:522
  176.1 5.2 %copy-start.20 = (f32[8,128]{1,0:T(8,128)}, f32[8,128]{1,0:T(8,128)S(1)}, u32[]{:S(2)}) copy-start(f32[8,128]{1,0:T(8,128)S(1)} %add.13.l0) | copy-start | bytes 12292
  176.1 5.1 %collective-permute-start.28 = (f32[8,128]{1,0:T(8,128)S(1)}, f32[8,128]{1,0:T(8,128)S(1)}, u32[]{:S(2)}, u32[]{:S(2)}) collective-permute-start(f32[8,128]{1,0:T(8,128)S(1)} %add.13.l0), channel_id=1, source_target_pairs={{0,64},{32,96},{64,0},{96,32},{128,192},{160,224},{192,128},{224,1... | collective-permute-start | bytes 12296 | tf_op jit(solution)/shard_map/ppermute | solution.py:522
  181.3 0.8 copy-start.16
  185.0 9.5 %collective-permute-start.30 = (bf16[48,2048]{1,0:T(8,128)(2,1)}, bf16[48,2048]{1,0:T(8,128)(2,1)S(1)}, u32[]{:S(2)}, u32[]{:S(2)}) collective-permute-start(bf16[48,2048]{1,0:T(8,128)(2,1)} %get-tuple-element.36), channel_id=1, source_target_pairs={{0,128},{32,160},{64,192},{96,224},{128,0},{160,32},{192,64},{224,... | collective-permute-start | bytes 589832 | tf_op jit(solution)/shard_map/ppermute | solution.py:522
  188.0 5.3 %collective-permute-start.29 = (f32[8,128]{1,0:T(8,128)}, f32[8,128]{1,0:T(8,128)S(1)}, u32[]{:S(2)}, u32[]{:S(2)}) collective-permute-start(f32[8,128]{1,0:T(8,128)} %get-tuple-element.34), channel_id=1, source_target_pairs={{0,128},{32,160},{64,192},{96,224},{128,0},{160,32},{192,64},{224,... | collective-permute-start | bytes 12296 | tf_op jit(solution)/shard_map/ppermute | solution.py:522
  (6 other events, 4.0 us)

commit v2 on v1

v2 whole, which is shorter than its diff:
```python
import functools
import math

import jax
import jax.numpy as jnp
from jax import lax
from jax.experimental import pallas as pl
from jax.experimental.pallas import tpu as pltpu
from jax.sharding import PartitionSpec as P

D = 8192
KV_HEADS = 8
HEAD_DIM = 128
CAP_LEN = 256
PATCHES = 48
CAPS = 8
GROUP_HEADS = 8
KV_WIDTH = 2048
COLUMNS = 32
IMG_SLOTS = CAPS * PATCHES
COEFS = KV_HEADS * GROUP_HEADS
WIDE = KV_WIDTH + 2 * COEFS
HALF = CAP_LEN // 2

norm_eps = 1e-06
loss_scale = 65536.0
scaling = 1.0 / math.sqrt(HEAD_DIM)
to_base2 = scaling * math.log2(math.e)

SMEM = pltpu.SMEM
VMEM = pltpu.VMEM
VMEM_LIMIT = 16 * 1024 * 1024
BIG_LIMIT = 56 * 1024 * 1024

AT_Y, AT_SRC_Y, AT_SRC_X_SAME, AT_PARTNER_Y, AT_PLACE, AT_LEN = 0, 1, 2, 3, 4, 5
AT_COUNTS, AT_RANKING, AT_DEST = 8, 16, 24

REL = (0, 2, 4, 6, 1, 3, 5, 7)

SUM_HIGH = 2.0**60
TOGETHER = 2


def exact_dot(a, b, dims):
    return lax.dot_general(a, b, (dims, ((), ())), preferred_element_type=jnp.float32)


def meta_kernel(idx_ref, list_ref, count_ref, order_ref, len_ref, out_ref):
    seg = idx_ref[0]
    col = idx_ref[1]
    x = seg // 4
    y = seg % 4
    slot = col // CAPS
    place = col % CAPS

    def section_of(section):
        return list_ref[section * 4 + slot, place] // COLUMNS

    own = section_of(seg)
    partner = section_of((1 - x) * 4 + y)
    out_ref[AT_Y] = y
    out_ref[AT_SRC_Y] = own % 4
    out_ref[AT_SRC_X_SAME] = (own // 4 == x).astype(jnp.int32)
    out_ref[AT_PARTNER_Y] = partner % 4
    out_ref[AT_PLACE] = place
    out_ref[AT_LEN] = len_ref[0]
    group = seg * 4 + slot
    for i, rel in enumerate(REL):
        out_ref[AT_COUNTS + i] = count_ref[list_ref[group, place ^ rel]]
    for k in range(CAPS):
        out_ref[AT_RANKING + k] = order_ref[group, k]
    for k in range(4):
        dest = section_of(x * 4 + (y + 4 - k) % 4)
        here = (dest % 4 == y).astype(jnp.int32)
        out_ref[AT_DEST + k] = here * jnp.where(dest // 4 == x, 1, 2)


def make_meta(idx, image_list, patch_count, pref_order, caption_len):
    smem = pl.BlockSpec(memory_space=SMEM)
    return pl.pallas_call(
        meta_kernel,
        out_shape=jax.ShapeDtypeStruct((32,), jnp.int32),
        in_specs=[smem] * 5,
        out_specs=smem,
        name="meta",
    )(idx, image_list, patch_count, pref_order, caption_len)


def pick_partner_kernel(meta_ref, i0, i1, i2, i3, out_ref, sem):
    y = meta_ref[AT_Y]
    back = (y + 4 - meta_ref[AT_PARTNER_Y]) % 4
    for k, src in enumerate((i0, i1, i2, i3)):

        @pl.when(back == k)
        def _():
            copy = pltpu.make_async_copy(src, out_ref, sem)
            copy.start()
            copy.wait()


def pick_own_kernel(meta_ref, i0, i1, i2, i3, far, out_ref, sem):
    y = meta_ref[AT_Y]
    same = meta_ref[AT_SRC_X_SAME]
    back = jnp.where(same == 1, (y + 4 - meta_ref[AT_SRC_Y]) % 4, 4)
    for k, src in enumerate((i0, i1, i2, i3, far)):

        @pl.when(back == k)
        def _():
            copy = pltpu.make_async_copy(src, out_ref, sem)
            copy.start()
            copy.wait()


def pick(kernel, name, meta, *images):
    any_space = pl.BlockSpec(memory_space=pl.ANY)
    return pl.pallas_call(
        kernel,
        out_shape=jax.ShapeDtypeStruct(images[0].shape, images[0].dtype),
        in_specs=[pl.BlockSpec(memory_space=SMEM)] + [any_space] * len(images),
        out_specs=pl.BlockSpec(memory_space=VMEM),
        scratch_shapes=[pltpu.SemaphoreType.DMA],
        name=name,
    )(meta, *images)


def head_columns(head):
    keys = pl.ds(pl.multiple_of(head * HEAD_DIM, HEAD_DIM), HEAD_DIM)
    values = pl.ds(pl.multiple_of((KV_HEADS + head) * HEAD_DIM, HEAD_DIM), HEAD_DIM)
    return keys, values


def with_marks(values, marks):
    values_t = jnp.concatenate(values, axis=0).T
    marks_t = jnp.concatenate(marks, axis=0).T[:16]
    return jnp.concatenate([values_t, marks_t], axis=0).astype(jnp.bfloat16)


def pipelined(count, start, finish):
    ahead = start(0)
    done = []
    for g in range(count):
        now = ahead
        if g + 1 < count:
            ahead = start(g + 1)
        done.append(finish(g, now))
    return done


def column(g):
    return slice(g * HEAD_DIM, (g + 1) * HEAD_DIM)


def own_kernel(q_ref, key_ref, value_ref, acc_ref, max_ref, sum_ref):
    keys = key_ref[...]
    mixed = with_marks(
        [value_ref[...].astype(jnp.float32)], [jnp.ones((CAP_LEN, HEAD_DIM), jnp.float32)]
    )
    diagonal = lax.broadcasted_iota(jnp.int32, (HALF, HALF), 0) <= lax.broadcasted_iota(
        jnp.int32, (HALF, HALF), 1
    )
    minus = jnp.full((HALF, HALF), -jnp.inf, jnp.float32)

    def start(g):
        return exact_dot(keys, q_ref[:, column(g)], ((1,), (1,)))

    def finish(g, s):
        s_a = jnp.where(diagonal, s[:HALF, :HALF], minus)
        s_b = s[:HALF, HALF:]
        s_c = jnp.where(diagonal, s[HALF:, HALF:], minus)
        m_low = jnp.max(s_a, axis=0, keepdims=True) * to_base2
        m_high = jnp.max(jnp.maximum(s_b, s_c), axis=0, keepdims=True) * to_base2
        p_a = jnp.exp2(s_a * to_base2 - m_low).astype(jnp.bfloat16)
        p_b = jnp.exp2(s_b * to_base2 - m_high).astype(jnp.bfloat16)
        p_c = jnp.exp2(s_c * to_base2 - m_high).astype(jnp.bfloat16)
        p = jnp.concatenate(
            [
                jnp.concatenate([p_a, p_b], axis=1),
                jnp.concatenate([jnp.zeros_like(p_c), p_c], axis=1),
            ],
            axis=0,
        )
        out = exact_dot(mixed, p, ((1,), (0,)))
        acc_ref[column(g), :] = out[:HEAD_DIM]
        max_ref[g : g + 1, :] = jnp.concatenate([m_low, m_high], axis=1)
        sum_ref[g : g + 1, :] = out[HEAD_DIM : HEAD_DIM + 1]

    pipelined(GROUP_HEADS, start, finish)


def image_parts(meta_ref, images, key_cols, value_cols):
    row = lax.broadcasted_iota(jnp.int32, (PATCHES, HEAD_DIM), 0)
    keys, values, marks = [], [], []
    for i, image in enumerate(images):
        live = row < meta_ref[AT_COUNTS + i]
        key = image[:, key_cols].astype(jnp.float32)
        keys.append(jnp.where(live, key, key[0:1, :]).astype(jnp.bfloat16))
        values.append(jnp.where(live, image[:, value_cols].astype(jnp.float32), 0.0))
        marks.append(live.astype(jnp.float32))
    return jnp.concatenate(keys, axis=0), with_marks(values, marks)


def forward_step(head, meta_ref, q_ref, dir_ref, state, images, kept, stat_ref, reward_ref, sum_refs):
    acc_in, max_in, sum_in = state
    p_ref, att_ref, inv_ref = kept
    ss_ref, rd_ref = sum_refs
    keys, mixed = image_parts(meta_ref, images, *head_columns(head))
    dir_t = dir_ref[...].T

    @pl.when(head == 0)
    def _():
        ss_ref[...] = jnp.zeros_like(ss_ref)
        rd_ref[...] = jnp.zeros_like(rd_ref)

    def start(g):
        return exact_dot(keys, q_ref[:, column(g)], ((1,), (1,)))

    def attended(p, acc, total):
        out = exact_dot(mixed, p, ((1,), (0,)))
        total = total + out[HEAD_DIM : HEAD_DIM + 1]
        return (acc + out[:HEAD_DIM]) * (1.0 / total), total

    def square_and_reward(att, dir_col):
        ss = jnp.sum((att * att).reshape(16, 8, CAP_LEN), axis=0)
        return ss, jnp.sum((att * dir_col).reshape(16, 8, CAP_LEN), axis=0)

    zero = jnp.zeros((8, CAP_LEN), jnp.float32)
    sums = [zero, zero, jnp.zeros((1, CAP_LEN), jnp.float32)]

    def finish(g, s):
        p = jnp.exp2(s * to_base2 - max_in[g : g + 1, :]).astype(jnp.bfloat16)
        p_ref[g] = p
        att, total = attended(p, acc_in[column(g), :], sum_in[g : g + 1, :])
        att_ref[column(g), :] = att
        inv_ref[g : g + 1, :] = 1.0 / total
        ss, rd = square_and_reward(att, dir_t[:, g : g + 1])
        sums[0] += ss
        sums[1] += rd
        sums[2] = jnp.maximum(sums[2], total)

    pipelined(GROUP_HEADS, start, finish)
    inside = jnp.max(sums[2]) < SUM_HIGH

    @pl.when(inside)
    def _():
        ss_ref[...] += sums[0]
        rd_ref[...] += sums[1]

    @pl.when(jnp.logical_not(inside))
    def _():
        for g in range(GROUP_HEADS):
            s = start(g)
            old = max_in[g : g + 1, :]
            new = jnp.maximum(old, jnp.max(s, axis=0, keepdims=True) * to_base2)
            shrink = jnp.exp2(old - new)
            p = jnp.exp2(s * to_base2 - new).astype(jnp.bfloat16)
            p_ref[g] = p
            att, total = attended(p, acc_in[column(g), :] * shrink, sum_in[g : g + 1, :] * shrink)
            att_ref[column(g), :] = att
            inv_ref[g : g + 1, :] = 1.0 / total
            ss, rd = square_and_reward(att, dir_t[:, g : g + 1])
            ss_ref[...] += ss
            rd_ref[...] += rd

    @pl.when(head == KV_HEADS - 1)
    def _():
        ss = ss_ref[...]
        rd = rd_ref[...]
        length = meta_ref[AT_LEN]
        inv_rms = lax.rsqrt(jnp.sum(ss, axis=0, keepdims=True) * (1.0 / D) + norm_eps)
        per_token = jnp.sum(rd, axis=0, keepdims=True) * inv_rms
        live = lax.broadcasted_iota(jnp.int32, (1, CAP_LEN), 1) < length
        length_f = jnp.full((1, CAP_LEN), length, jnp.int32).astype(jnp.float32)
        unit = jnp.where(live, 1.0 / length_f, 0.0)
        a = inv_rms * unit
        b = inv_rms * inv_rms * unit * per_token * (1.0 / D)
        stat_ref[...] = jnp.concatenate([a, b, jnp.zeros((6, CAP_LEN), jnp.float32)], axis=0)
        reward = jnp.sum(jnp.where(live, per_token, 0.0), axis=1, keepdims=True)
        reward_ref[...] = jnp.broadcast_to(reward / length_f[:, :1], (8, 128))


ROWS = GROUP_HEADS * HEAD_DIM
Q_SPEC = pl.BlockSpec((CAP_LEN, ROWS), lambda h: (0, h))
ACC_SPEC = pl.BlockSpec((ROWS, CAP_LEN), lambda h: (h, 0))
ROW_SPEC = pl.BlockSpec((GROUP_HEADS, CAP_LEN), lambda h: (h, 0))
SMEM_SPEC = pl.BlockSpec(memory_space=SMEM)
ACC = jax.ShapeDtypeStruct((D, CAP_LEN), jnp.float32)
ROW = jax.ShapeDtypeStruct((COEFS, CAP_LEN), jnp.float32)
TILE = jax.ShapeDtypeStruct((8, 128), jnp.float32)


def by_head(kernel, name, in_specs, out_specs, out_shape, scratch=(), flops=2_000_000_000):
    return pl.pallas_call(
        kernel,
        grid=(KV_HEADS,),
        in_specs=in_specs,
        out_specs=out_specs,
        out_shape=out_shape,
        scratch_shapes=scratch,
        compiler_params=pltpu.CompilerParams(vmem_limit_bytes=BIG_LIMIT),
        cost_estimate=pl.CostEstimate(
            flops=flops, bytes_accessed=16_000_000, transcendentals=4_000_000
        ),
        name=name,
    )


def attend_own(q, own_kv):
    key = pl.BlockSpec((CAP_LEN, HEAD_DIM), lambda h: (0, h))
    value = pl.BlockSpec((CAP_LEN, HEAD_DIM), lambda h: (0, KV_HEADS + h))
    call = by_head(
        own_kernel, "attend_own", [Q_SPEC, key, value], [ACC_SPEC, ROW_SPEC, ROW_SPEC], [ACC, ROW, ROW]
    )
    return call(q, own_kv, own_kv)


def backward_step(head, meta_ref, q_ref, dir_ref, images, kept, stat_ref, outs, coef_ref):
    p_ref, att_ref, inv_ref = kept
    keep_ref, send_ref = outs
    key_cols, value_cols = head_columns(head)
    values = jnp.concatenate([image[:, value_cols] for image in images], axis=0)
    dir_t = dir_ref[...].T
    a = stat_ref[0:1, :]
    b = stat_ref[1:2, :]
    which = lax.broadcasted_iota(jnp.int32, (HEAD_DIM, CAP_LEN), 0)

    @pl.when(head == 0)
    def _():
        coef_ref[...] = jnp.zeros_like(coef_ref)

    key_grad = jnp.zeros((IMG_SLOTS, HEAD_DIM), jnp.float32)
    value_grad = jnp.zeros((IMG_SLOTS, 2 * HEAD_DIM), jnp.float32)

    def start(g):
        att = att_ref[column(g), :]
        inv = inv_ref[g : g + 1, :]
        factor = a * inv
        rest_grad = -(b * inv) * att
        grad = (factor * dir_t[:, g : g + 1] + rest_grad).astype(jnp.bfloat16)
        delta = jnp.sum(grad.astype(jnp.float32) * att, axis=0, keepdims=True)
        factors = jnp.where(which == head * GROUP_HEADS + g, factor, 0.0)
        apart = jnp.concatenate([rest_grad, factors], axis=0).astype(jnp.bfloat16)
        return exact_dot(values, grad, ((1,), (0,))), delta, apart

    def finish(g, started):
        weight_grad, delta, apart = started
        p = p_ref[g]
        return p, (p.astype(jnp.float32) * (weight_grad - delta)).astype(jnp.bfloat16), apart

    for first in range(0, GROUP_HEADS, TOGETHER):
        done = pipelined(TOGETHER, lambda g: start(first + g), lambda g, x: finish(first + g, x))
        p, score_grad, apart = (jnp.concatenate(part, axis=1) for part in zip(*done))
        q = jnp.concatenate([q_ref[:, column(first + g)] for g in range(TOGETHER)], axis=0)
        value_grad = value_grad + exact_dot(p, apart, ((1,), (1,)))
        key_grad = key_grad + exact_dot(score_grad, q, ((1,), (0,)))
    key_grad = key_grad * scaling
    row = lax.broadcasted_iota(jnp.int32, (PATCHES, HEAD_DIM), 0)
    for i in range(CAPS):
        live = row < meta_ref[AT_COUNTS + i]
        out_ref = keep_ref if i < 4 else send_ref
        part = slice(i * PATCHES, (i + 1) * PATCHES)
        out_ref[i % 4, :, key_cols] = jnp.where(live, key_grad[part], 0.0).astype(jnp.bfloat16)
        out_ref[i % 4, :, value_cols] = jnp.where(
            live, value_grad[part, :HEAD_DIM], 0.0
        ).astype(jnp.bfloat16)
    coef_ref[...] += value_grad[:, HEAD_DIM:]

    @pl.when(head == KV_HEADS - 1)
    def _():
        for i in range(CAPS):
            live = row < meta_ref[AT_COUNTS + i]
            out_ref = keep_ref if i < 4 else send_ref
            coef = coef_ref[i * PATCHES : (i + 1) * PATCHES, :]
            out_ref[i % 4, :, KV_WIDTH:] = in_two(jnp.where(live, coef, 0.0))


def in_two(coef):
    first = coef.astype(jnp.bfloat16).astype(jnp.float32)
    return (first + pltpu.roll(coef - first, COEFS, 1)).astype(jnp.bfloat16)


def from_two(pair):
    pair = pair.astype(jnp.float32)
    lane = lax.broadcasted_iota(jnp.int32, pair.shape, 1)
    return jnp.where(lane < COEFS, pair + pltpu.roll(pair, COEFS, 1), 0.0)


def image_kernel(meta_ref, q_ref, dir_ref, acc_in, max_in, sum_in, *rest):
    images = rest[:CAPS]
    keep_ref, send_ref, reward_ref = rest[CAPS : CAPS + 3]
    p_all, att_all, inv_all, stat_ref, ss_ref, rd_ref, coef_ref = rest[CAPS + 3 :]
    step = pl.program_id(0)
    head = step % KV_HEADS
    kept = (p_all.at[head], att_all.at[head], inv_all.at[head])

    @pl.when(step < KV_HEADS)
    def _():
        state = (acc_in, max_in, sum_in)
        sums = (ss_ref, rd_ref)
        forward_step(
            head, meta_ref, q_ref, dir_ref, state, images, kept, stat_ref, reward_ref, sums
        )

    @pl.when(step >= KV_HEADS)
    def _():
        outs = (keep_ref, send_ref)
        backward_step(head, meta_ref, q_ref, dir_ref, images, kept, stat_ref, outs, coef_ref)


def attend_images(meta, q, direction, state, images):
    half = jax.ShapeDtypeStruct((4, PATCHES, WIDE), jnp.bfloat16)
    half_spec = pl.BlockSpec((4, PATCHES, WIDE), lambda s: (0, 0, 0))

    def once(s):
        return (jnp.minimum(s, KV_HEADS - 1), 0)

    row_spec = pl.BlockSpec((GROUP_HEADS, CAP_LEN), once)
    call = pl.pallas_call(
        image_kernel,
        grid=(2 * KV_HEADS,),
        in_specs=[
            SMEM_SPEC,
            pl.BlockSpec((CAP_LEN, ROWS), lambda s: (0, s % KV_HEADS)),
            pl.BlockSpec((GROUP_HEADS, HEAD_DIM), lambda s: (s % KV_HEADS, 0)),
            pl.BlockSpec((ROWS, CAP_LEN), once),
            row_spec,
            row_spec,
        ]
        + [pl.BlockSpec((PATCHES, KV_WIDTH), lambda s: (0, 0))] * CAPS,
        out_specs=[half_spec, half_spec, pl.BlockSpec((8, 128), lambda s: (0, 0))],
        out_shape=[half, half, TILE],
        scratch_shapes=[
            VMEM((KV_HEADS, GROUP_HEADS, IMG_SLOTS, CAP_LEN), jnp.bfloat16),
            VMEM((KV_HEADS, ROWS, CAP_LEN), jnp.float32),
            VMEM((KV_HEADS, GROUP_HEADS, CAP_LEN), jnp.float32),
            VMEM((8, CAP_LEN), jnp.float32),
            VMEM((8, CAP_LEN), jnp.float32),
            VMEM((8, CAP_LEN), jnp.float32),
            VMEM((IMG_SLOTS, HEAD_DIM), jnp.float32),
        ],
        compiler_params=pltpu.CompilerParams(vmem_limit_bytes=BIG_LIMIT),
        cost_estimate=pl.CostEstimate(
            flops=8_000_000_000, bytes_accessed=18_000_000, transcendentals=6_000_000
        ),
        name="attend_images",
    )
    return call(meta, q, direction, *state, *images)


def group_loss(place, rewards, meta_ref):
    lane = lax.broadcasted_iota(jnp.int32, (8, 128), 1)
    sub = lax.broadcasted_iota(jnp.int32, (8, 128), 0)
    by_lane = jnp.zeros((8, 128), jnp.float32)
    by_sub = jnp.zeros((8, 128), jnp.float32)
    for rel in range(CAPS):
        tile = rewards[rel // 2][...]
        value = jnp.where((place ^ rel) % 2 == 0, tile[0:1, :], tile[1:2, :])
        by_lane = jnp.where(lane == (place ^ rel), value, by_lane)
        by_sub = jnp.where(sub == (place ^ rel), value, by_sub)
    rank_lane = jnp.full((8, 128), CAPS, jnp.int32)
    rank_sub = jnp.zeros((8, 128), jnp.int32)
    for k in range(CAPS):
        who = meta_ref[AT_RANKING + k]
        rank_lane = jnp.where(lane == who, k, rank_lane)
        rank_sub = jnp.where(sub == who, k, rank_sub)
    real = lane < CAPS
    better = real & (rank_sub < rank_lane)
    worse = real & (rank_sub > rank_lane)
    margin = by_lane - by_sub
    soft = jnp.maximum(margin, 0.0) + jnp.log1p(jnp.exp(-jnp.abs(margin)))
    pairs = jnp.where(better, soft, 0.0)
    loss = jnp.sum(jnp.sum(pairs, axis=0, keepdims=True), axis=1, keepdims=True)
    up = 1.0 / (1.0 + jnp.exp(margin))
    down = 1.0 / (1.0 + jnp.exp(-margin))
    grads = jnp.where(worse, up, 0.0) - jnp.where(better, down, 0.0)
    grads = jnp.sum(grads, axis=1, keepdims=True) * loss_scale
    sub_col = sub[:, :1]
    mine = jnp.sum(jnp.where(sub_col == place, grads, 0.0), axis=0, keepdims=True)
    other = jnp.sum(jnp.where(sub_col == (place ^ 1), grads, 0.0), axis=0, keepdims=True)
    return loss, mine, other


def scaled_sum_kernel(meta_ref, keep_ref, recv_ref, *rest):
    rewards = rest[:4]
    *outs, loss_ref = rest[4:]
    loss, mine, other = group_loss(meta_ref[AT_PLACE], rewards, meta_ref)
    loss_ref[...] = jnp.broadcast_to(loss, (8, 128))
    for i, out_ref in enumerate(outs):
        kept, sent = keep_ref[i], recv_ref[i]
        total = kept[:, :KV_WIDTH].astype(jnp.float32) * mine
        total = total + sent[:, :KV_WIDTH].astype(jnp.float32) * other
        coef = from_two(kept[:, KV_WIDTH:]) * mine + from_two(sent[:, KV_WIDTH:]) * other
        out_ref[:, :KV_WIDTH] = total.astype(out_ref.dtype)
        wide = out_ref.dtype == jnp.float32
        out_ref[:, KV_WIDTH:] = coef if wide else in_two(coef)


def in_vmem(kernel, name, count, out_shape, meta=True):
    vmem = pl.BlockSpec(memory_space=VMEM)
    return pl.pallas_call(
        kernel,
        in_specs=[SMEM_SPEC] * meta + [vmem] * count,
        out_specs=[vmem] * len(out_shape),
        out_shape=out_shape,
        compiler_params=pltpu.CompilerParams(vmem_limit_bytes=VMEM_LIMIT),
        name=name,
    )


WIRE = jax.ShapeDtypeStruct((PATCHES, WIDE), jnp.bfloat16)
TOTAL = jax.ShapeDtypeStruct((PATCHES, WIDE), jnp.float32)


def scaled_sum(meta, keep, recv, rewards):
    outs = [TOTAL, WIRE, WIRE, WIRE, TILE]
    call = in_vmem(scaled_sum_kernel, "scaled_sum", 6, outs)
    return call(meta, keep, recv, *rewards)


def in_three(value):
    terms = []
    for _ in range(3):
        term = value.astype(jnp.bfloat16).astype(jnp.float32)
        terms.append(term)
        value = value - term
    return terms


def store_loss(ref, loss):
    lane = lax.broadcasted_iota(jnp.int32, (PATCHES, 128), 1)
    first, second, third = (term[:1] for term in in_three(loss))
    row = jnp.where(lane == 0, first, jnp.where(lane == 1, second, third))
    ref[:, KV_WIDTH:] = row.astype(jnp.bfloat16)


def read_loss(ref):
    row = ref[:8, KV_WIDTH:].astype(jnp.float32)
    return jnp.broadcast_to(row[:, 0:1] + row[:, 1:2] + row[:, 2:3], (8, 128))


def sum_kernel(own_ref, a_ref, b_ref, c_ref, dir_ref, l0_ref, l1_ref, out_ref):
    own = own_ref[...]
    total, coef = own[:, :KV_WIDTH], own[:, KV_WIDTH:]
    for part in (a_ref, b_ref, c_ref):
        total = total + part[:, :KV_WIDTH].astype(jnp.float32)
        coef = coef + from_two(part[:, KV_WIDTH:])
    out_ref[:, : KV_WIDTH // 2] = total[:, : KV_WIDTH // 2].astype(out_ref.dtype)
    for head in range(KV_HEADS):
        cols = column(KV_HEADS + head)
        value = total[:, cols]
        for j in range(head * GROUP_HEADS, (head + 1) * GROUP_HEADS):
            value = value + coef[:, j : j + 1] * dir_ref[j : j + 1, :]
        out_ref[:, cols] = value.astype(out_ref.dtype)
    store_loss(out_ref, l0_ref[...] + l1_ref[...])


def group_sum(own, parts, direction, losses):
    call = in_vmem(sum_kernel, "group_sum", 7, [WIRE], meta=False)
    return call(own, *parts, direction, *losses)[0]


def sort_kernel(meta_ref, s0, s1, s2, s3, keep_ref, send_ref, loss_ref):
    total = jnp.zeros((PATCHES, KV_WIDTH), jnp.float32)
    kept = jnp.zeros((PATCHES, KV_WIDTH), jnp.float32)
    for k, part in enumerate((s0, s1, s2, s3)):
        dest = meta_ref[AT_DEST + k]
        value = part[:, :KV_WIDTH].astype(jnp.float32)
        kept = kept + jnp.where(dest == 1, value, 0.0)
        total = total + jnp.where(dest == 2, value, 0.0)
    keep_ref[...] = kept
    send_ref[:, :KV_WIDTH] = total.astype(send_ref.dtype)
    loss = (read_loss(s0) + read_loss(s2)) + (read_loss(s1) + read_loss(s3))
    store_loss(send_ref, loss)
    loss_ref[...] = loss


def sort_by_owner(meta, parts):
    grad = jax.ShapeDtypeStruct((PATCHES, KV_WIDTH), jnp.float32)
    return in_vmem(sort_kernel, "sort_by_owner", 4, [grad, WIRE, TILE])(meta, *parts)


def last_kernel(keep_ref, recv_ref, l0_ref, l2_ref, l3_ref, out_ref, loss_ref):
    out_ref[0] = keep_ref[...] + recv_ref[:, :KV_WIDTH].astype(jnp.float32)
    loss_ref[...] = (l0_ref[...] + read_loss(recv_ref)) + (l2_ref[...] + l3_ref[...])


def last_sum(kept, recv, losses):
    grad = jax.ShapeDtypeStruct((1, PATCHES, KV_WIDTH), jnp.float32)
    call = in_vmem(last_kernel, "last_sum", 5, [grad, TILE], meta=False)
    return call(kept, recv, *losses)


def along_y(value, step):
    pairs = [(s, s // 4 * 4 + (s + step) % 4) for s in range(8)]
    return lax.ppermute(value, "segment", pairs)


def across(value, axis, mask):
    size = lax.axis_size(axis)
    return lax.ppermute(value, axis, [(i, i ^ mask) for i in range(size)])


def per_device(
    queries, caption_kv, caption_len, image_kv, patch_count, image_list, pref_order, reward_dir
):
    idx = jnp.stack([lax.axis_index("segment"), lax.axis_index("tp")]).astype(jnp.int32)
    image = image_kv[0]
    q = queries[0]
    direction = reward_dir.reshape(KV_HEADS * GROUP_HEADS, HEAD_DIM)
    meta = make_meta(idx, image_list, patch_count, pref_order, caption_len)

    seen = [image] + [along_y(image, step) for step in (1, 2, 3)]
    wanted = pick(pick_partner_kernel, "pick_partner", meta, *seen)
    own = pick(pick_own_kernel, "pick_own", meta, *seen, across(wanted, "segment", 4))
    acc, top, total = attend_own(q, caption_kv[0])
    others = [across(own, "tp", mask) for mask in (2, 4, 6)]
    *others, top = lax.optimization_barrier((*others, top))
    same_core = [own, *others]
    images = same_core + [across(one, "tp", 1) for one in same_core]

    keep, send, reward = attend_images(meta, q, direction, (acc, top, total), images)
    recv = across(send, "tp", 1)
    other = across(reward, "tp", 1)
    second = lax.axis_index("tp") % 2 == 1
    row = lax.broadcasted_iota(jnp.int32, reward.shape, 0)
    pair = jnp.where((row == 1) == second, reward, other)
    rewards = [pair] + [across(pair, "tp", mask) for mask in (2, 4, 6)]
    mine, to_z1, to_z2, to_z3, loss = scaled_sum(meta, keep, recv, rewards)
    parts = [across(to_z1, "tp", 2), across(to_z2, "tp", 4), across(to_z3, "tp", 6)]
    total = group_sum(mine, parts, direction, (loss, across(loss, "tp", 8)))
    totals = [total] + [along_y(total, step) for step in (1, 2, 3)]
    kept, away, loss = sort_by_owner(meta, totals)
    both = [(i, i ^ (4 * COLUMNS + 16)) for i in range(8 * COLUMNS)]
    diagonal = lax.ppermute(loss, ("segment", "tp"), both)
    losses = (loss, across(loss, "tp", 16), diagonal)
    image_grad, loss = last_sum(kept, across(away, "segment", 4), losses)
    return (loss[0, 0], reward[0, :1], image_grad)


def solution(mesh):
    placed = (
        P(("segment", "tp"), None, None),
        P(("segment", "tp"), None, None),
        P(("segment", "tp")),
        P(("segment", "tp"), None, None),
        P(),
        P(),
        P(),
        P(),
    )
    return jax.shard_map(
        per_device,
        mesh=mesh,
        in_specs=placed,
        out_specs=(P(), P(("segment", "tp")), P(("segment", "tp"), None, None)),
        check_vma=False,
    )
```

time: 198 us -> 165 us (0.83)
  starting transfers between devices: 45.3 us -> 34.8 us
  waiting for transfers between devices: 49.1 us -> 40.6 us
  local copies, waits for them, and re-layouts: 14.4 us -> 7.61 us
  Pallas kernels: 82.2 us -> 78 us
  other arithmetic: 3.79 us -> 1.41 us
    ppermute x25 -> x19, waiting for transfers between devices: 47.3 us -> 24.4 us  [across(): return lax.ppermute(value, axis, [(i, i ^ mask) for i in range(size)])]
    ppermute x6, waiting for transfers between devices: 1.78 us -> 13.8 us  [along_y(): return lax.ppermute(value, 'segment', pairs)]
    ppermute x25 -> x19, starting transfers between devices: 34.9 us -> 26.7 us  [across(): return lax.ppermute(value, axis, [(i, i ^ mask) for i in range(size)])]
    unnamed x48 -> x30, local copies, waits for them, and re-layouts: 13.4 us -> 5.91 us
    pallas_call x5 -> x6, Pallas kernels: 75.8 us -> 71.6 us  [the longest x1 55.4 us: attend_images(): return call(meta, q, direction, *state, *images)]
    ppermute x6, starting transfers between devices: 10.4 us -> 6.82 us  [along_y(): return lax.ppermute(value, 'segment', pairs)]
    ppermute x0 -> x1, waiting for transfers between devices: none -> 2.37 us  [per_device(): diagonal = lax.ppermute(loss, ('segment', 'tp'), both)]
  transfers between devices with their start and end apart: 31 -> 26, of which waited for: 14 -> 18; matrix products, arithmetic and copies ran while one was open for 3% -> 3% of each run, Pallas kernels for 1% -> 9%
where the time goes in v2:
time: 165 us; the launch traced here: 164 us
  Pallas kernels  78 us (47%)
  waiting for transfers between devices  40.6 us (25%)
  starting transfers between devices  34.8 us (21%)
  local copies, waits for them, and re-layouts  7.61 us (5%)
    pallas_call x1, Pallas kernels, attend_images(): return call(meta, q, direction, *state, *images)  55.4 us
    ppermute x19, starting transfers between devices, across(): return lax.ppermute(value, axis, [(i, i ^ mask) for i in range(size)])  26.7 us
    ppermute x19, waiting for transfers between devices, across(): return lax.ppermute(value, axis, [(i, i ^ mask) for i in range(size)])  24.4 us
    ppermute x6, waiting for transfers between devices, along_y(): return lax.ppermute(value, 'segment', pairs)  13.8 us
    pallas_call x1, Pallas kernels, attend_own(): return call(q, own_kv, own_kv)  12.4 us
    ppermute x6, starting transfers between devices, along_y(): return lax.ppermute(value, 'segment', pairs)  6.82 us
    unnamed x30, local copies, waits for them, and re-layouts  5.91 us
    pallas_call x2, Pallas kernels, pick(): pl.pallas_call(kernel, out_shape=jax.ShapeDtypeStruct(images[0].shape, im...  4.59 us
  transfers between devices with their start and end apart: 26, of which 18 were waited for; matrix products, arithmetic and copies ran while one was open for 3% of the time, Pallas kernels for 9%

profile of v2, /device:TPU:32, one launch (start us, length us, event | category | flops | bytes accessed | tf_op | source)
XLA Modules:
  0.0 163.8 jit_solution(14807640400736179480)
XLA Ops:
  0.6 3.1 %collective-permute-start.2 = (bf16[48,2048]{1,0:T(8,128)(2,1)}, bf16[48,2048]{1,0:T(8,128)(2,1)S(1)}, u32[]{:S(2)}, u32[]{:S(2)}) collective-permute-start(bf16[48,2048]{1,0:T(8,128)(2,1)} %bitcast.10), channel_id=1, source_target_pairs={{0,96},{32,0},{64,32},{96,64},{128,224},{160,128},{192,160},{224,1... | collective-permute-start | bytes 589832 | tf_op jit(solution)/shard_map/ppermute | solution.py:594
  3.7 0.6 collective-permute-start.1
  4.4 1.0 collective-permute-start
  6.0 1.4 copy.11.list_ref
  7.3 1.4 copy.12.order_ref
  8.7 0.6 pad_add_fusion.idx_ref
  9.3 1.9 %meta.1.meta_ref = s32[32]{0:T(128)} custom-call(s32[2]{0:T(128)} %pad_add_fusion.idx_ref, s32[32,8]{1,0:T(8,128)} %copy.11.list_ref, s32[256]{0:T(256)} %count_ref.1, s32[32,8]{1,0:T(8,128)} %copy.12.order_ref, s32[1]{0:T(128)S(6)} %copy.13.len_ref), custom_call_target="tpu_custom_call" | custom-call | tf_op jit(solution)/shard_map/meta/pallas_call | solution.py:80
  11.2 1.2 collective-permute-done.2.i3
  12.4 0.9 collective-permute-done.1.i2
  13.3 2.7 %collective-permute-done.i1 = bf16[48,2048]{1,0:T(8,128)(2,1)S(1)} collective-permute-done((bf16[48,2048]{1,0:T(8,128)(2,1)}, bf16[48,2048]{1,0:T(8,128)(2,1)S(1)}, u32[]{:S(2)}, u32[]{:S(2)}) %collective-permute-start) | collective-permute-done | bytes 196640 | tf_op jit(solution)/shard_map/ppermute | solution.py:594
  16.0 0.7 copy-done.5
  16.7 2.3 %pick_partner.1 = bf16[48,2048]{1,0:T(8,128)(2,1)} custom-call(s32[32]{0:T(128)} %meta.1.meta_ref, bf16[48,2048]{1,0:T(8,128)(2,1)} %bitcast.13, bf16[48,2048]{1,0:T(8,128)(2,1)} %copy-done.5, bf16[48,2048]{1,0:T(8,128)(2,1)} %copy-done.4, bf16[48,2048]{1,0:T(8,128)(2,1)} %copy-done.3), custom_call_target="tpu_custom_call" | custom-call | tf_op jit(solution)/shard_map/pick_partner/pallas_call | solution.py:116
  19.0 3.1 %collective-permute-start.3 = (bf16[48,2048]{1,0:T(8,128)(2,1)}, bf16[48,2048]{1,0:T(8,128)(2,1)S(1)}, u32[]{:S(2)}, u32[]{:S(2)}) collective-permute-start(bf16[48,2048]{1,0:T(8,128)(2,1)} %pick_partner.1), channel_id=1, source_target_pairs={{0,128},{32,160},{64,192},{96,224},{128,0},{160,32},{192,64},{224,... | collective-permute-start | bytes 589832 | tf_op jit(solution)/shard_map/ppermute | solution.py:599
  22.1 5.5 %collective-permute-done.3.far = bf16[48,2048]{1,0:T(8,128)(2,1)S(1)} collective-permute-done((bf16[48,2048]{1,0:T(8,128)(2,1)}, bf16[48,2048]{1,0:T(8,128)(2,1)S(1)}, u32[]{:S(2)}, u32[]{:S(2)}) %collective-permute-start.3) | collective-permute-done | bytes 196640 | tf_op jit(solution)/shard_map/ppermute | solution.py:599
  27.6 0.7 copy-done.6
  28.3 2.3 %pick_own.1.rest_0_ = bf16[48,2048]{1,0:T(8,128)(2,1)} custom-call(s32[32]{0:T(128)} %meta.1.meta_ref, bf16[48,2048]{1,0:T(8,128)(2,1)} %bitcast.14, bf16[48,2048]{1,0:T(8,128)(2,1)} %copy-done.5, bf16[48,2048]{1,0:T(8,128)(2,1)} %copy-done.4, bf16[48,2048]{1,0:T(8,128)(2,1)} %copy-done.3, bf16[48,2048]{1,0:T(8,128)(2,1)} %copy-done.6), custom_call_target="tpu_custom_call" | custom-call | tf_op jit(solution)/shard_map/pick_own/pallas_call | solution.py:116
  30.6 2.0 %collective-permute-start.6 = (bf16[48,2048]{1,0:T(8,128)(2,1)}, bf16[48,2048]{1,0:T(8,128)(2,1)S(1)}, u32[]{:S(2)}, u32[]{:S(2)}) collective-permute-start(bf16[48,2048]{1,0:T(8,128)(2,1)} %pick_own.1.rest_0_), channel_id=1, source_target_pairs={{0,6},{1,7},{2,4},{3,5},{4,2},{5,3},{6,0},{7,1},{8,14},{9,15},{10,... | collective-permute-start | bytes 589832 | tf_op jit(solution)/shard_map/ppermute | solution.py:599
  32.6 1.4 collective-permute-start.5
  34.1 1.4 collective-permute-start.4
  35.4 12.4 %attend_own.1 = (f32[8192,256]{1,0:T(8,128)}, f32[64,256]{1,0:T(8,128)}, f32[64,256]{1,0:T(8,128)}) custom-call(bf16[256,8192]{1,0:T(8,128)(2,1)} %bitcast.15, bf16[256,2048]{1,0:T(8,128)(2,1)} %bitcast.17, bf16[256,2048]{1,0:T(8,128)(2,1)} %bitcast.18), custom_call_target="tpu_custom_call" | custom-call | flops 2000000000 | bytes 16000000 | tf_op jit(solution)/shard_map/attend_own/pallas_call | solution.py:313
  47.8 1.3 collective-permute-done.5.rest_2_
  49.7 0.8 collective-permute-done.8.rest_5_
  51.8 55.4 %attend_images.1 = (bf16[4,48,2176]{2,1,0:T(8,128)(2,1)}, bf16[4,48,2176]{2,1,0:T(8,128)(2,1)}, f32[8,128]{1,0:T(8,128)}) custom-call(s32[32]{0:T(128)} %meta.1.meta_ref, bf16[256,8192]{1,0:T(8,128)(2,1)} %bitcast.16, f32[64,128]{1,0:T(8,128)} %bitcast.8, f32[8192,256]{1,0:T(8,128)} %get-tuple-element.23.acc_in, f32[64,256]{1,0:T(8,128)} %get-tuple-element.25.max_in, ...), custom_call_target="tpu_custom_call" | custom-call | flops 8000000000 | bytes 18000000 | tf_op jit(solution)/shard_map/attend_images/pallas_call | solution.py:446
  107.8 2.1 %collective-permute-done.12 = f32[8,128]{1,0:T(8,128)S(1)} collective-permute-done((f32[8,128]{1,0:T(8,128)}, f32[8,128]{1,0:T(8,128)S(1)}, u32[]{:S(2)}, u32[]{:S(2)}) %collective-permute-start.12) | collective-permute-done | bytes 4128 | tf_op jit(solution)/shard_map/ppermute | solution.py:599
  109.9 0.8 broadcast_select_fusion.rest_0_
  111.1 4.0 %collective-permute-start.14 = (f32[8,128]{1,0:T(8,128)S(1)}, f32[8,128]{1,0:T(8,128)S(1)}, u32[]{:S(2)}, u32[]{:S(2)}) collective-permute-start(f32[8,128]{1,0:T(8,128)S(1)} %broadcast_select_fusion.rest_0_), channel_id=1, source_target_pairs={{0,4},{1,5},{2,6},{3,7},{4,0},{5,1},{6,2},{7,3},{8,12},{9,13},{10,... | collective-permute-start | bytes 12296 | tf_op jit(solution)/shard_map/ppermute | solution.py:599
  115.4 1.3 collective-permute-done.14.rest_2_
  116.7 2.0 %collective-permute-done.13.rest_1_ = f32[8,128]{1,0:T(8,128)S(1)} collective-permute-done((f32[8,128]{1,0:T(8,128)S(1)}, f32[8,128]{1,0:T(8,128)S(1)}, u32[]{:S(2)}, u32[]{:S(2)}) %collective-permute-start.13) | collective-permute-done | bytes 4128 | tf_op jit(solution)/shard_map/ppermute | solution.py:599
  118.7 1.1 copy-done
  119.9 1.2 scaled_sum.1
  121.1 1.3 collective-permute-start.16
  122.4 2.0 %collective-permute-start.17 = (bf16[48,2176]{1,0:T(8,128)(2,1)S(1)}, bf16[48,2176]{1,0:T(8,128)(2,1)S(1)}, u32[]{:S(2)}, u32[]{:S(2)}) collective-permute-start(bf16[48,2176]{1,0:T(8,128)(2,1)S(1)} %get-tuple-element.35), channel_id=1, source_target_pairs={{0,4},{1,5},{2,6},{3,7},{4,0},{5,1},{6,2},{7,3},{8,12},{9,13},{10,... | collective-permute-start | bytes 626696 | tf_op jit(solution)/shard_map/ppermute | solution.py:599
  124.7 6.1 %collective-permute-start.19 = (f32[8,128]{1,0:T(8,128)S(1)}, f32[8,128]{1,0:T(8,128)S(1)}, u32[]{:S(2)}, u32[]{:S(2)}) collective-permute-start(f32[8,128]{1,0:T(8,128)S(1)} %get-tuple-element.37.l0_ref), channel_id=1, source_target_pairs={{0,8},{1,9},{2,10},{3,11},{4,12},{5,13},{6,14},{7,15},{8,0},{9,1},... | collective-permute-start | bytes 12296 | tf_op jit(solution)/shard_map/ppermute | solution.py:599
  130.8 4.6 %collective-permute-done.19.l1_ref = f32[8,128]{1,0:T(8,128)S(1)} collective-permute-done((f32[8,128]{1,0:T(8,128)S(1)}, f32[8,128]{1,0:T(8,128)S(1)}, u32[]{:S(2)}, u32[]{:S(2)}) %collective-permute-start.19) | collective-permute-done | bytes 4128 | tf_op jit(solution)/shard_map/ppermute | solution.py:599
  135.4 2.7 %collective-permute-done.17.b_ref = bf16[48,2176]{1,0:T(8,128)(2,1)S(1)} collective-permute-done((bf16[48,2176]{1,0:T(8,128)(2,1)S(1)}, bf16[48,2176]{1,0:T(8,128)(2,1)S(1)}, u32[]{:S(2)}, u32[]{:S(2)}) %collective-permute-start.17) | collective-permute-done | bytes 208928 | tf_op jit(solution)/shard_map/ppermute | solution.py:599
  138.0 3.6 %collective-permute-done.18.c_ref = bf16[48,2176]{1,0:T(8,128)(2,1)S(1)} collective-permute-done((bf16[48,2176]{1,0:T(8,128)(2,1)S(1)}, bf16[48,2176]{1,0:T(8,128)(2,1)S(1)}, u32[]{:S(2)}, u32[]{:S(2)}) %collective-permute-start.18) | collective-permute-done | bytes 208928 | tf_op jit(solution)/shard_map/ppermute | solution.py:599
  141.6 0.7 group_sum.1.s0
  142.4 0.9 collective-permute-start.21
  143.3 1.1 collective-permute-start.20
  144.4 5.0 %collective-permute-done.22.s3 = bf16[48,2176]{1,0:T(8,128)(2,1)S(1)} collective-permute-done((bf16[48,2176]{1,0:T(8,128)(2,1)S(1)}, bf16[48,2176]{1,0:T(8,128)(2,1)S(1)}, u32[]{:S(2)}, u32[]{:S(2)}) %collective-permute-start.22) | collective-permute-done | bytes 208928 | tf_op jit(solution)/shard_map/ppermute | solution.py:594
  149.4 1.9 %collective-permute-done.21.s2 = bf16[48,2176]{1,0:T(8,128)(2,1)S(1)} collective-permute-done((bf16[48,2176]{1,0:T(8,128)(2,1)S(1)}, bf16[48,2176]{1,0:T(8,128)(2,1)S(1)}, u32[]{:S(2)}, u32[]{:S(2)}) %collective-permute-start.21) | collective-permute-done | bytes 208928 | tf_op jit(solution)/shard_map/ppermute | solution.py:594
  151.3 2.2 %collective-permute-done.20.s1 = bf16[48,2176]{1,0:T(8,128)(2,1)S(1)} collective-permute-done((bf16[48,2176]{1,0:T(8,128)(2,1)S(1)}, bf16[48,2176]{1,0:T(8,128)(2,1)S(1)}, u32[]{:S(2)}, u32[]{:S(2)}) %collective-permute-start.20) | collective-permute-done | bytes 208928 | tf_op jit(solution)/shard_map/ppermute | solution.py:594
  153.4 1.1 sort_by_owner.1
  154.5 3.1 %collective-permute-start.23 = (bf16[48,2176]{1,0:T(8,128)(2,1)S(1)}, bf16[48,2176]{1,0:T(8,128)(2,1)S(1)}, u32[]{:S(2)}, u32[]{:S(2)}) collective-permute-start(bf16[48,2176]{1,0:T(8,128)(2,1)S(1)} %get-tuple-element.39), channel_id=1, source_target_pairs={{0,128},{32,160},{64,192},{96,224},{128,0},{160,32},{192,64},{224,... | collective-permute-start | bytes 626696 | tf_op jit(solution)/shard_map/ppermute | solution.py:599
  157.6 1.3 collective-permute-start.25
  158.8 1.2 slice.7
  160.0 2.4 %collective-permute-done.25.l3_ref = f32[8,128]{1,0:T(8,128)S(1)} collective-permute-done((f32[8,128]{1,0:T(8,128)S(1)}, f32[8,128]{1,0:T(8,128)S(1)}, u32[]{:S(2)}, u32[]{:S(2)}) %collective-permute-start.25) | collective-permute-done | bytes 4128 | tf_op jit(solution)/shard_map/ppermute | solution.py:633
  162.4 0.8 last_sum.1
  (48 shorter events, 4.2 us)
Async XLA Ops:
  0.6 11.8 %collective-permute-start.2 = (bf16[48,2048]{1,0:T(8,128)(2,1)}, bf16[48,2048]{1,0:T(8,128)(2,1)S(1)}, u32[]{:S(2)}, u32[]{:S(2)}) collective-permute-start(bf16[48,2048]{1,0:T(8,128)(2,1)} %bitcast.10), channel_id=1, source_target_pairs={{0,96},{32,0},{64,32},{96,64},{128,224},{160,128},{192,160},{224,1... | collective-permute-start | bytes 589832 | tf_op jit(solution)/shard_map/ppermute | solution.py:594
  3.7 9.6 %collective-permute-start.1 = (bf16[48,2048]{1,0:T(8,128)(2,1)}, bf16[48,2048]{1,0:T(8,128)(2,1)S(1)}, u32[]{:S(2)}, u32[]{:S(2)}) collective-permute-start(bf16[48,2048]{1,0:T(8,128)(2,1)} %bitcast.11), channel_id=1, source_target_pairs={{0,64},{32,96},{64,0},{96,32},{128,192},{160,224},{192,128},{224,1... | collective-permute-start | bytes 589832 | tf_op jit(solution)/shard_map/ppermute | solution.py:594
  4.4 11.7 %collective-permute-start = (bf16[48,2048]{1,0:T(8,128)(2,1)}, bf16[48,2048]{1,0:T(8,128)(2,1)S(1)}, u32[]{:S(2)}, u32[]{:S(2)}) collective-permute-start(bf16[48,2048]{1,0:T(8,128)(2,1)} %bitcast.12), channel_id=1, source_target_pairs={{0,32},{32,64},{64,96},{96,0},{128,160},{160,192},{192,224},{224,1... | collective-permute-start | bytes 589832 | tf_op jit(solution)/shard_map/ppermute | solution.py:594
  12.4 3.6 %copy-start.3 = (bf16[48,2048]{1,0:T(8,128)(2,1)}, bf16[48,2048]{1,0:T(8,128)(2,1)S(1)}, u32[]{:S(2)}) copy-start(bf16[48,2048]{1,0:T(8,128)(2,1)S(1)} %collective-permute-done.2.i3) | copy-start | bytes 589828
  13.3 2.7 %copy-start.4 = (bf16[48,2048]{1,0:T(8,128)(2,1)}, bf16[48,2048]{1,0:T(8,128)(2,1)S(1)}, u32[]{:S(2)}) copy-start(bf16[48,2048]{1,0:T(8,128)(2,1)S(1)} %collective-permute-done.1.i2) | copy-start | bytes 589828
  16.0 0.7 copy-start.5
  19.0 8.6 %collective-permute-start.3 = (bf16[48,2048]{1,0:T(8,128)(2,1)}, bf16[48,2048]{1,0:T(8,128)(2,1)S(1)}, u32[]{:S(2)}, u32[]{:S(2)}) collective-permute-start(bf16[48,2048]{1,0:T(8,128)(2,1)} %pick_partner.1), channel_id=1, source_target_pairs={{0,128},{32,160},{64,192},{96,224},{128,0},{160,32},{192,64},{224,... | collective-permute-start | bytes 589832 | tf_op jit(solution)/shard_map/ppermute | solution.py:599
  27.6 0.7 copy-start.6
  30.6 17.2 %collective-permute-start.6 = (bf16[48,2048]{1,0:T(8,128)(2,1)}, bf16[48,2048]{1,0:T(8,128)(2,1)S(1)}, u32[]{:S(2)}, u32[]{:S(2)}) collective-permute-start(bf16[48,2048]{1,0:T(8,128)(2,1)} %pick_own.1.rest_0_), channel_id=1, source_target_pairs={{0,6},{1,7},{2,4},{3,5},{4,2},{5,3},{6,0},{7,1},{8,14},{9,15},{10,... | collective-permute-start | bytes 589832 | tf_op jit(solution)/shard_map/ppermute | solution.py:599
  32.6 16.5 %collective-permute-start.5 = (bf16[48,2048]{1,0:T(8,128)(2,1)}, bf16[48,2048]{1,0:T(8,128)(2,1)S(1)}, u32[]{:S(2)}, u32[]{:S(2)}) collective-permute-start(bf16[48,2048]{1,0:T(8,128)(2,1)} %pick_own.1.rest_0_), channel_id=1, source_target_pairs={{0,4},{1,5},{2,6},{3,7},{4,0},{5,1},{6,2},{7,3},{8,12},{9,13},{10,... | collective-permute-start | bytes 589832 | tf_op jit(solution)/shard_map/ppermute | solution.py:599
  34.1 15.0 %collective-permute-start.4 = (bf16[48,2048]{1,0:T(8,128)(2,1)}, bf16[48,2048]{1,0:T(8,128)(2,1)S(1)}, u32[]{:S(2)}, u32[]{:S(2)}) collective-permute-start(bf16[48,2048]{1,0:T(8,128)(2,1)} %pick_own.1.rest_0_), channel_id=1, source_target_pairs={{0,2},{1,3},{2,0},{3,1},{4,6},{5,7},{6,4},{7,5},{8,10},{9,11},{10,... | collective-permute-start | bytes 589832 | tf_op jit(solution)/shard_map/ppermute | solution.py:599
  47.8 1.9 %collective-permute-start.7 = (bf16[48,2048]{1,0:T(8,128)(2,1)}, bf16[48,2048]{1,0:T(8,128)(2,1)S(1)}, u32[]{:S(2)}, u32[]{:S(2)}) collective-permute-start(bf16[48,2048]{1,0:T(8,128)(2,1)} %pick_own.1.rest_0_), channel_id=1, source_target_pairs={{0,1},{1,0},{2,3},{3,2},{4,5},{5,4},{6,7},{7,6},{8,9},{9,8},{10,11... | collective-permute-start | bytes 589832 | tf_op jit(solution)/shard_map/ppermute | solution.py:599
  47.8 3.3 %copy-start.7 = (bf16[48,2048]{1,0:T(8,128)(2,1)}, bf16[48,2048]{1,0:T(8,128)(2,1)S(1)}, u32[]{:S(2)}) copy-start(bf16[48,2048]{1,0:T(8,128)(2,1)S(1)} %collective-permute-done.6.rest_3_) | copy-start | bytes 589828
  49.1 2.0 %copy-start.8 = (bf16[48,2048]{1,0:T(8,128)(2,1)}, bf16[48,2048]{1,0:T(8,128)(2,1)S(1)}, u32[]{:S(2)}) copy-start(bf16[48,2048]{1,0:T(8,128)(2,1)S(1)} %collective-permute-done.5.rest_2_) | copy-start | bytes 589828
  49.1 2.0 %copy-start.9 = (bf16[48,2048]{1,0:T(8,128)(2,1)}, bf16[48,2048]{1,0:T(8,128)(2,1)S(1)}, u32[]{:S(2)}) copy-start(bf16[48,2048]{1,0:T(8,128)(2,1)S(1)} %collective-permute-done.4.rest_1_) | copy-start | bytes 589828
  49.1 1.4 collective-permute-start.8
  49.1 1.7 %collective-permute-start.9 = (bf16[48,2048]{1,0:T(8,128)(2,1)S(1)}, bf16[48,2048]{1,0:T(8,128)(2,1)S(1)}, u32[]{:S(2)}, u32[]{:S(2)}) collective-permute-start(bf16[48,2048]{1,0:T(8,128)(2,1)S(1)} %collective-permute-done.5.rest_2_), channel_id=1, source_target_pairs={{0,1},{1,0},{2,3},{3,2},{4,5},{5,4},{6,7},{7,6},{8,9},{9,8},{10,11... | collective-permute-start | bytes 589832 | tf_op jit(solution)/shard_map/ppermute | solution.py:599
  49.6 1.5 collective-permute-start.10
  49.7 1.4 copy-start.10
  50.6 0.7 copy-start.11
  50.8 0.7 copy-start.12
  51.1 0.7 copy-start.13
  51.8 66.9 %copy-start.2 = (s32[32]{0:T(128)S(1)}, s32[32]{0:T(128)}, u32[]{:S(2)}) copy-start(s32[32]{0:T(128)} %meta.1.meta_ref) | copy-start | bytes 388
  51.8 89.8 %copy-start.1 = (f32[8192]{0:T(1024)S(1)}, f32[8192]{0:T(1024)}, u32[]{:S(2)}) copy-start(f32[8192]{0:T(1024)} %param.15) | copy-start | bytes 98308
  107.2 11.5 %collective-permute-start.11 = (bf16[4,48,2176]{2,1,0:T(8,128)(2,1)}, bf16[4,48,2176]{2,1,0:T(8,128)(2,1)S(1)}, u32[]{:S(2)}, u32[]{:S(2)}) collective-permute-start(bf16[4,48,2176]{2,1,0:T(8,128)(2,1)} %get-tuple-element.31), channel_id=1, source_target_pairs={{0,1},{1,0},{2,3},{3,2},{4,5},{5,4},{6,7},{7,6},{8,9},{9,8},{10,11... | collective-permute-start | bytes 2506760 | tf_op jit(solution)/shard_map/ppermute | solution.py:599
  107.5 2.3 %collective-permute-start.12 = (f32[8,128]{1,0:T(8,128)}, f32[8,128]{1,0:T(8,128)S(1)}, u32[]{:S(2)}, u32[]{:S(2)}) collective-permute-start(f32[8,128]{1,0:T(8,128)} %get-tuple-element.32), channel_id=1, source_target_pairs={{0,1},{1,0},{2,3},{3,2},{4,5},{5,4},{6,7},{7,6},{8,9},{9,8},{10,11... | collective-permute-start | bytes 12296 | tf_op jit(solution)/shard_map/ppermute | solution.py:599
  110.6 4.8 %collective-permute-start.15 = (f32[8,128]{1,0:T(8,128)S(1)}, f32[8,128]{1,0:T(8,128)S(1)}, u32[]{:S(2)}, u32[]{:S(2)}) collective-permute-start(f32[8,128]{1,0:T(8,128)S(1)} %broadcast_select_fusion.rest_0_), channel_id=1, source_target_pairs={{0,6},{1,7},{2,4},{3,5},{4,2},{5,3},{6,0},{7,1},{8,14},{9,15},{10,... | collective-permute-start | bytes 12296 | tf_op jit(solution)/shard_map/ppermute | solution.py:599
  111.1 5.6 %collective-permute-start.14 = (f32[8,128]{1,0:T(8,128)S(1)}, f32[8,128]{1,0:T(8,128)S(1)}, u32[]{:S(2)}, u32[]{:S(2)}) collective-permute-start(f32[8,128]{1,0:T(8,128)S(1)} %broadcast_select_fusion.rest_0_), channel_id=1, source_target_pairs={{0,4},{1,5},{2,6},{3,7},{4,0},{5,1},{6,2},{7,3},{8,12},{9,13},{10,... | collective-permute-start | bytes 12296 | tf_op jit(solution)/shard_map/ppermute | solution.py:599
  115.1 3.6 %collective-permute-start.13 = (f32[8,128]{1,0:T(8,128)S(1)}, f32[8,128]{1,0:T(8,128)S(1)}, u32[]{:S(2)}, u32[]{:S(2)}) collective-permute-start(f32[8,128]{1,0:T(8,128)S(1)} %broadcast_select_fusion.rest_0_), channel_id=1, source_target_pairs={{0,2},{1,3},{2,0},{3,1},{4,6},{5,7},{6,4},{7,5},{8,10},{9,11},{10,... | collective-permute-start | bytes 12296 | tf_op jit(solution)/shard_map/ppermute | solution.py:599
  118.7 1.2 copy-start
  121.1 14.3 %collective-permute-start.16 = (bf16[48,2176]{1,0:T(8,128)(2,1)S(1)}, bf16[48,2176]{1,0:T(8,128)(2,1)S(1)}, u32[]{:S(2)}, u32[]{:S(2)}) collective-permute-start(bf16[48,2176]{1,0:T(8,128)(2,1)S(1)} %get-tuple-element.34), channel_id=1, source_target_pairs={{0,2},{1,3},{2,0},{3,1},{4,6},{5,7},{6,4},{7,5},{8,10},{9,11},{10,... | collective-permute-start | bytes 626696 | tf_op jit(solution)/shard_map/ppermute | solution.py:599
  122.4 15.6 %collective-permute-start.17 = (bf16[48,2176]{1,0:T(8,128)(2,1)S(1)}, bf16[48,2176]{1,0:T(8,128)(2,1)S(1)}, u32[]{:S(2)}, u32[]{:S(2)}) collective-permute-start(bf16[48,2176]{1,0:T(8,128)(2,1)S(1)} %get-tuple-element.35), channel_id=1, source_target_pairs={{0,4},{1,5},{2,6},{3,7},{4,0},{5,1},{6,2},{7,3},{8,12},{9,13},{10,... | collective-permute-start | bytes 626696 | tf_op jit(solution)/shard_map/ppermute | solution.py:599
  124.4 17.2 %collective-permute-start.18 = (bf16[48,2176]{1,0:T(8,128)(2,1)S(1)}, bf16[48,2176]{1,0:T(8,128)(2,1)S(1)}, u32[]{:S(2)}, u32[]{:S(2)}) collective-permute-start(bf16[48,2176]{1,0:T(8,128)(2,1)S(1)} %get-tuple-element.36), channel_id=1, source_target_pairs={{0,6},{1,7},{2,4},{3,5},{4,2},{5,3},{6,0},{7,1},{8,14},{9,15},{10,... | collective-permute-start | bytes 626696 | tf_op jit(solution)/shard_map/ppermute | solution.py:599
  124.7 10.7 %collective-permute-start.19 = (f32[8,128]{1,0:T(8,128)S(1)}, f32[8,128]{1,0:T(8,128)S(1)}, u32[]{:S(2)}, u32[]{:S(2)}) collective-permute-start(f32[8,128]{1,0:T(8,128)S(1)} %get-tuple-element.37.l0_ref), channel_id=1, source_target_pairs={{0,8},{1,9},{2,10},{3,11},{4,12},{5,13},{6,14},{7,15},{8,0},{9,1},... | collective-permute-start | bytes 12296 | tf_op jit(solution)/shard_map/ppermute | solution.py:599
  142.3 7.1 %collective-permute-start.22 = (bf16[48,2176]{1,0:T(8,128)(2,1)S(1)}, bf16[48,2176]{1,0:T(8,128)(2,1)S(1)}, u32[]{:S(2)}, u32[]{:S(2)}) collective-permute-start(bf16[48,2176]{1,0:T(8,128)(2,1)S(1)} %group_sum.1.s0), channel_id=1, source_target_pairs={{0,96},{32,0},{64,32},{96,64},{128,224},{160,128},{192,160},{224,1... | collective-permute-start | bytes 626696 | tf_op jit(solution)/shard_map/ppermute | solution.py:594
  142.4 8.9 %collective-permute-start.21 = (bf16[48,2176]{1,0:T(8,128)(2,1)S(1)}, bf16[48,2176]{1,0:T(8,128)(2,1)S(1)}, u32[]{:S(2)}, u32[]{:S(2)}) collective-permute-start(bf16[48,2176]{1,0:T(8,128)(2,1)S(1)} %group_sum.1.s0), channel_id=1, source_target_pairs={{0,64},{32,96},{64,0},{96,32},{128,192},{160,224},{192,128},{224,1... | collective-permute-start | bytes 626696 | tf_op jit(solution)/shard_map/ppermute | solution.py:594
  143.3 10.1 %collective-permute-start.20 = (bf16[48,2176]{1,0:T(8,128)(2,1)S(1)}, bf16[48,2176]{1,0:T(8,128)(2,1)S(1)}, u32[]{:S(2)}, u32[]{:S(2)}) collective-permute-start(bf16[48,2176]{1,0:T(8,128)(2,1)S(1)} %group_sum.1.s0), channel_id=1, source_target_pairs={{0,32},{32,64},{64,96},{96,0},{128,160},{160,192},{192,224},{224,1... | collective-permute-start | bytes 626696 | tf_op jit(solution)/shard_map/ppermute | solution.py:594
  154.5 7.9 %collective-permute-start.23 = (bf16[48,2176]{1,0:T(8,128)(2,1)S(1)}, bf16[48,2176]{1,0:T(8,128)(2,1)S(1)}, u32[]{:S(2)}, u32[]{:S(2)}) collective-permute-start(bf16[48,2176]{1,0:T(8,128)(2,1)S(1)} %get-tuple-element.39), channel_id=1, source_target_pairs={{0,128},{32,160},{64,192},{96,224},{128,0},{160,32},{192,64},{224,... | collective-permute-start | bytes 626696 | tf_op jit(solution)/shard_map/ppermute | solution.py:599
  157.6 4.8 %collective-permute-start.25 = (f32[8,128]{1,0:T(8,128)S(1)}, f32[8,128]{1,0:T(8,128)S(1)}, u32[]{:S(2)}, u32[]{:S(2)}) collective-permute-start(f32[8,128]{1,0:T(8,128)S(1)} %get-tuple-element.40.l0_ref), channel_id=1, source_target_pairs={{0,144},{1,145},{2,146},{3,147},{4,148},{5,149},{6,150},{7,151},{8... | collective-permute-start | bytes 12296 | tf_op jit(solution)/shard_map/ppermute | solution.py:633
  158.8 3.6 %collective-permute-start.24 = (f32[8,128]{1,0:T(8,128)S(1)}, f32[8,128]{1,0:T(8,128)S(1)}, u32[]{:S(2)}, u32[]{:S(2)}) collective-permute-start(f32[8,128]{1,0:T(8,128)S(1)} %get-tuple-element.40.l0_ref), channel_id=1, source_target_pairs={{0,16},{1,17},{2,18},{3,19},{4,20},{5,21},{6,22},{7,23},{8,24},{9,... | collective-permute-start | bytes 12296 | tf_op jit(solution)/shard_map/ppermute | solution.py:599

commit v3 on v2

--- a/solution.py
+++ b/solution.py
@@ -32,13 +32,12 @@
 VMEM_LIMIT = 16 * 1024 * 1024
 BIG_LIMIT = 56 * 1024 * 1024
 
-AT_Y, AT_SRC_Y, AT_SRC_X_SAME, AT_PARTNER_Y, AT_PLACE, AT_LEN = 0, 1, 2, 3, 4, 5
+AT_FOR_PARTNER, AT_OWN, AT_PLACE, AT_LEN = 0, 1, 2, 3
 AT_COUNTS, AT_RANKING, AT_DEST = 8, 16, 24
 
 REL = (0, 2, 4, 6, 1, 3, 5, 7)
 
 SUM_HIGH = 2.0**60
-TOGETHER = 2
 
 
 def exact_dot(a, b, dims):
@@ -58,10 +57,8 @@
 
     own = section_of(seg)
     partner = section_of((1 - x) * 4 + y)
-    out_ref[AT_Y] = y
-    out_ref[AT_SRC_Y] = own % 4
-    out_ref[AT_SRC_X_SAME] = (own // 4 == x).astype(jnp.int32)
-    out_ref[AT_PARTNER_Y] = partner % 4
+    out_ref[AT_FOR_PARTNER] = (y + 4 - partner % 4) % 4
+    out_ref[AT_OWN] = jnp.where(own // 4 == x, (y + 4 - own % 4) % 4, 4)
     out_ref[AT_PLACE] = place
     out_ref[AT_LEN] = len_ref[0]
     group = seg * 4 + slot
@@ -86,41 +83,11 @@
     )(idx, image_list, patch_count, pref_order, caption_len)
 
 
-def pick_partner_kernel(meta_ref, i0, i1, i2, i3, out_ref, sem):
-    y = meta_ref[AT_Y]
-    back = (y + 4 - meta_ref[AT_PARTNER_Y]) % 4
-    for k, src in enumerate((i0, i1, i2, i3)):
-
-        @pl.when(back == k)
-        def _():
-            copy = pltpu.make_async_copy(src, out_ref, sem)
-            copy.start()
-            copy.wait()
-
-
-def pick_own_kernel(meta_ref, i0, i1, i2, i3, far, out_ref, sem):
-    y = meta_ref[AT_Y]
-    same = meta_ref[AT_SRC_X_SAME]
-    back = jnp.where(same == 1, (y + 4 - meta_ref[AT_SRC_Y]) % 4, 4)
-    for k, src in enumerate((i0, i1, i2, i3, far)):
-
-        @pl.when(back == k)
-        def _():
-            copy = pltpu.make_async_copy(src, out_ref, sem)
-            copy.start()
-            copy.wait()
-
-
-def pick(kernel, name, meta, *images):
-    any_space = pl.BlockSpec(memory_space=pl.ANY)
-    return pl.pallas_call(
-        kernel,
-        out_shape=jax.ShapeDtypeStruct(images[0].shape, images[0].dtype),
-        in_specs=[pl.BlockSpec(memory_space=SMEM)] + [any_space] * len(images),
-        out_specs=pl.BlockSpec(memory_space=VMEM),
-        scratch_shapes=[pltpu.SemaphoreType.DMA],
-        name=name,
-    )(meta, *images)
+def pick(which, images):
+    chosen = images[-1]
+    for k in reversed(range(len(images) - 1)):
+        chosen = jnp.where(which == k, images[k], chosen)
+    return chosen
 
 
 def head_columns(head):
@@ -135,15 +102,15 @@
     return jnp.concatenate([values_t, marks_t], axis=0).astype(jnp.bfloat16)
 
 
-def pipelined(count, start, finish):
-    ahead = start(0)
-    done = []
-    for g in range(count):
-        now = ahead
-        if g + 1 < count:
-            ahead = start(g + 1)
-        done.append(finish(g, now))
-    return done
+def pipelined(count, *stages):
+    results = [{} for _ in stages]
+    for step in range(count + len(stages) - 1):
+        for depth, stage in enumerate(stages):
+            g = step - depth
+            if 0 <= g < count:
+                before = results[depth - 1].pop(g) if depth else None
+                results[depth][g] = stage(g, before)
+    return [results[-1][g] for g in range(count)]
 
 
 def column(g):
@@ -160,10 +127,10 @@
     )
     minus = jnp.full((HALF, HALF), -jnp.inf, jnp.float32)
 
-    def start(g):
+    def start(g, _):
         return exact_dot(keys, q_ref[:, column(g)], ((1,), (1,)))
 
-    def finish(g, s):
+    def soft(g, s):
         s_a = jnp.where(diagonal, s[:HALF, :HALF], minus)
         s_b = s[:HALF, HALF:]
         s_c = jnp.where(diagonal, s[HALF:, HALF:], minus)
@@ -179,12 +146,15 @@
             ],
             axis=0,
         )
+        max_ref[g : g + 1, :] = jnp.concatenate([m_low, m_high], axis=1)
+        return p
+
+    def finish(g, p):
         out = exact_dot(mixed, p, ((1,), (0,)))
         acc_ref[column(g), :] = out[:HEAD_DIM]
-        max_ref[g : g + 1, :] = jnp.concatenate([m_low, m_high], axis=1)
         sum_ref[g : g + 1, :] = out[HEAD_DIM : HEAD_DIM + 1]
 
-    pipelined(GROUP_HEADS, start, finish)
+    pipelined(GROUP_HEADS, start, soft, finish)
 
 
 def image_parts(meta_ref, images, key_cols, value_cols):
@@ -206,12 +176,7 @@
     keys, mixed = image_parts(meta_ref, images, *head_columns(head))
     dir_t = dir_ref[...].T
 
-    @pl.when(head == 0)
-    def _():
-        ss_ref[...] = jnp.zeros_like(ss_ref)
-        rd_ref[...] = jnp.zeros_like(rd_ref)
-
-    def start(g):
+    def start(g, _):
         return exact_dot(keys, q_ref[:, column(g)], ((1,), (1,)))
 
     def attended(p, acc, total):
@@ -226,9 +191,12 @@
     zero = jnp.zeros((8, CAP_LEN), jnp.float32)
     sums = [zero, zero, jnp.zeros((1, CAP_LEN), jnp.float32)]
 
-    def finish(g, s):
+    def soft(g, s):
         p = jnp.exp2(s * to_base2 - max_in[g : g + 1, :]).astype(jnp.bfloat16)
         p_ref[g] = p
+        return p
+
+    def finish(g, p):
         att, total = attended(p, acc_in[column(g), :], sum_in[g : g + 1, :])
         att_ref[column(g), :] = att
         inv_ref[g : g + 1, :] = 1.0 / total
@@ -237,7 +205,7 @@
         sums[1] += rd
         sums[2] = jnp.maximum(sums[2], total)
 
-    pipelined(GROUP_HEADS, start, finish)
+    pipelined(GROUP_HEADS, start, soft, finish)
     inside = jnp.max(sums[2]) < SUM_HIGH
 
     @pl.when(inside)
@@ -248,7 +216,7 @@
     @pl.when(jnp.logical_not(inside))
     def _():
         for g in range(GROUP_HEADS):
-            s = start(g)
+            s = start(g, None)
             old = max_in[g : g + 1, :]
             new = jnp.maximum(old, jnp.max(s, axis=0, keepdims=True) * to_base2)
             shrink = jnp.exp2(old - new)
@@ -323,14 +291,10 @@
     b = stat_ref[1:2, :]
     which = lax.broadcasted_iota(jnp.int32, (HEAD_DIM, CAP_LEN), 0)
 
-    @pl.when(head == 0)
-    def _():
-        coef_ref[...] = jnp.zeros_like(coef_ref)
-
     key_grad = jnp.zeros((IMG_SLOTS, HEAD_DIM), jnp.float32)
     value_grad = jnp.zeros((IMG_SLOTS, 2 * HEAD_DIM), jnp.float32)
 
-    def start(g):
+    def prepare(g, _):
         att = att_ref[column(g), :]
         inv = inv_ref[g : g + 1, :]
         factor = a * inv
@@ -338,20 +302,27 @@
         grad = (factor * dir_t[:, g : g + 1] + rest_grad).astype(jnp.bfloat16)
         delta = jnp.sum(grad.astype(jnp.float32) * att, axis=0, keepdims=True)
         factors = jnp.where(which == head * GROUP_HEADS + g, factor, 0.0)
-        apart = jnp.concatenate([rest_grad, factors], axis=0).astype(jnp.bfloat16)
+        return grad, delta, jnp.concatenate([rest_grad, factors], axis=0).astype(jnp.bfloat16)
+
+    def weights(g, before):
+        grad, delta, apart = before
         return exact_dot(values, grad, ((1,), (0,))), delta, apart
 
-    def finish(g, started):
-        weight_grad, delta, apart = started
+    def scores(g, before):
+        weight_grad, delta, apart = before
         p = p_ref[g]
-        return p, (p.astype(jnp.float32) * (weight_grad - delta)).astype(jnp.bfloat16), apart
-
-    for first in range(0, GROUP_HEADS, TOGETHER):
-        done = pipelined(TOGETHER, lambda g: start(first + g), lambda g, x: finish(first + g, x))
-        p, score_grad, apart = (jnp.concatenate(part, axis=1) for part in zip(*done))
-        q = jnp.concatenate([q_ref[:, column(first + g)] for g in range(TOGETHER)], axis=0)
-        value_grad = value_grad + exact_dot(p, apart, ((1,), (1,)))
-        key_grad = key_grad + exact_dot(score_grad, q, ((1,), (0,)))
+        score_grad = (p.astype(jnp.float32) * (weight_grad - delta)).astype(jnp.bfloat16)
+        return score_grad, apart
+
+    sums = [key_grad, value_grad]
+
+    def add(g, before):
+        score_grad, apart = before
+        sums[1] += exact_dot(p_ref[g], apart, ((1,), (1,)))
+        sums[0] += exact_dot(score_grad, q_ref[:, column(g)], ((1,), (0,)))
+
+    pipelined(GROUP_HEADS, prepare, weights, scores, add)
+    key_grad, value_grad = sums
     key_grad = key_grad * scaling
     row = lax.broadcasted_iota(jnp.int32, (PATCHES, HEAD_DIM), 0)
     for i in range(CAPS):
@@ -384,58 +355,88 @@
     return jnp.where(lane < COEFS, pair + pltpu.roll(pair, COEFS, 1), 0.0)
 
 
-def image_kernel(meta_ref, q_ref, dir_ref, acc_in, max_in, sum_in, *rest):
-    images = rest[:CAPS]
+def image_kernel(meta_ref, q_hbm, dir_ref, acc_hbm, max_ref, sum_ref, *rest):
+    sources = rest[:CAPS]
     keep_ref, send_ref, reward_ref = rest[CAPS : CAPS + 3]
-    p_all, att_all, inv_all, stat_ref, ss_ref, rd_ref, coef_ref = rest[CAPS + 3 :]
-    step = pl.program_id(0)
-    head = step % KV_HEADS
-    kept = (p_all.at[head], att_all.at[head], inv_all.at[head])
-
-    @pl.when(step < KV_HEADS)
-    def _():
-        state = (acc_in, max_in, sum_in)
+    q_all, acc_all, image_all, p_all, att_all, inv_all = rest[CAPS + 3 : CAPS + 9]
+    stat_ref, ss_ref, rd_ref, coef_ref, q_sem, acc_sem, image_sem = rest[CAPS + 9 :]
+
+    def q_copy(head):
+        cols = pl.ds(pl.multiple_of(head * ROWS, ROWS), ROWS)
+        return pltpu.make_async_copy(q_hbm.at[:, cols], q_all.at[head], q_sem.at[head])
+
+    def acc_copy(head):
+        rows = pl.ds(pl.multiple_of(head * ROWS, ROWS), ROWS)
+        return pltpu.make_async_copy(acc_hbm.at[rows, :], acc_all.at[head], acc_sem.at[head])
+
+    copies = [
+        pltpu.make_async_copy(source, image_all.at[i], image_sem.at[i])
+        for i, source in enumerate(sources)
+    ]
+    q_copy(0).start()
+    for copy in copies:
+        copy.start()
+    acc_copy(0).start()
+    q_copy(1).start()
+    acc_copy(1).start()
+    ss_ref[...] = jnp.zeros_like(ss_ref)
+    rd_ref[...] = jnp.zeros_like(rd_ref)
+    coef_ref[...] = jnp.zeros_like(coef_ref)
+    for copy in copies:
+        copy.wait()
+    images = [image_all.at[i] for i in range(CAPS)]
+
+    def of_head(head):
+        rows = pl.ds(pl.multiple_of(head * GROUP_HEADS, GROUP_HEADS), GROUP_HEADS)
+        kept = (p_all.at[head], att_all.at[head], inv_all.at[head])
+        return rows, q_all.at[head], dir_ref.at[rows, :], kept
+
+    @pl.loop(0, KV_HEADS)
+    def _(head):
+        q_copy(head).wait()
+        acc_copy(head).wait()
+
+        @pl.when(head + 2 < KV_HEADS)
+        def _():
+            q_copy(head + 2).start()
+            acc_copy(head + 2).start()
+
+        rows, q_ref, dirs, kept = of_head(head)
+        state = (acc_all.at[head], max_ref.at[rows, :], sum_ref.at[rows, :])
         sums = (ss_ref, rd_ref)
-        forward_step(
-            head, meta_ref, q_ref, dir_ref, state, images, kept, stat_ref, reward_ref, sums
-        )
-
-    @pl.when(step >= KV_HEADS)
-    def _():
+        forward_step(head, meta_ref, q_ref, dirs, state, images, kept, stat_ref, reward_ref, sums)
+
+    @pl.loop(0, KV_HEADS)
+    def _(head):
+        rows, q_ref, dirs, kept = of_head(head)
         outs = (keep_ref, send_ref)
-        backward_step(head, meta_ref, q_ref, dir_ref, images, kept, stat_ref, outs, coef_ref)
+        backward_step(head, meta_ref, q_ref, dirs, images, kept, stat_ref, outs, coef_ref)
 
 
 def attend_images(meta, q, direction, state, images):
     half = jax.ShapeDtypeStruct((4, PATCHES, WIDE), jnp.bfloat16)
-    half_spec = pl.BlockSpec((4, PATCHES, WIDE), lambda s: (0, 0, 0))
-
-    def once(s):
-        return (jnp.minimum(s, KV_HEADS - 1), 0)
-
-    row_spec = pl.BlockSpec((GROUP_HEADS, CAP_LEN), once)
+    any_space = pl.BlockSpec(memory_space=pl.ANY)
+    vmem = pl.BlockSpec(memory_space=VMEM)
+    row = VMEM((8, CAP_LEN), jnp.float32)
     call = pl.pallas_call(
         image_kernel,
-        grid=(2 * KV_HEADS,),
-        in_specs=[
-            SMEM_SPEC,
-            pl.BlockSpec((CAP_LEN, ROWS), lambda s: (0, s % KV_HEADS)),
-            pl.BlockSpec((GROUP_HEADS, HEAD_DIM), lambda s: (s % KV_HEADS, 0)),
-            pl.BlockSpec((ROWS, CAP_LEN), once),
-            row_spec,
-            row_spec,
-        ]
-        + [pl.BlockSpec((PATCHES, KV_WIDTH), lambda s: (0, 0))] * CAPS,
-        out_specs=[half_spec, half_spec, pl.BlockSpec((8, 128), lambda s: (0, 0))],
+        in_specs=[SMEM_SPEC, any_space, vmem, any_space, vmem, vmem] + [any_space] * CAPS,
+        out_specs=[vmem] * 3,
         out_shape=[half, half, TILE],
         scratch_shapes=[
+            VMEM((KV_HEADS, CAP_LEN, ROWS), jnp.bfloat16),
+            VMEM((KV_HEADS, ROWS, CAP_LEN), jnp.float32),
+            VMEM((CAPS, PATCHES, KV_WIDTH), jnp.bfloat16),
             VMEM((KV_HEADS, GROUP_HEADS, IMG_SLOTS, CAP_LEN), jnp.bfloat16),
             VMEM((KV_HEADS, ROWS, CAP_LEN), jnp.float32),
             VMEM((KV_HEADS, GROUP_HEADS, CAP_LEN), jnp.float32),
-            VMEM((8, CAP_LEN), jnp.float32),
-            VMEM((8, CAP_LEN), jnp.float32),
-            VMEM((8, CAP_LEN), jnp.float32),
+            row,
+            row,
+            row,
             VMEM((IMG_SLOTS, HEAD_DIM), jnp.float32),
+            pltpu.SemaphoreType.DMA((KV_HEADS,)),
+            pltpu.SemaphoreType.DMA((KV_HEADS,)),
+            pltpu.SemaphoreType.DMA((CAPS,)),
         ],
         compiler_params=pltpu.CompilerParams(vmem_limit_bytes=BIG_LIMIT),
         cost_estimate=pl.CostEstimate(
@@ -578,15 +579,14 @@
     return in_vmem(sort_kernel, "sort_by_owner", 4, [grad, WIRE, TILE])(meta, *parts)
 
 
-def last_kernel(keep_ref, recv_ref, l0_ref, l2_ref, l3_ref, out_ref, loss_ref):
+def last_kernel(keep_ref, recv_ref, loss_in_ref, out_ref, loss_ref):
     out_ref[0] = keep_ref[...] + recv_ref[:, :KV_WIDTH].astype(jnp.float32)
-    loss_ref[...] = (l0_ref[...] + read_loss(recv_ref)) + (l2_ref[...] + l3_ref[...])
-
-
-def last_sum(kept, recv, losses):
+    loss_ref[...] = loss_in_ref[...] + read_loss(recv_ref)
+
+
+def last_sum(kept, recv, loss):
     grad = jax.ShapeDtypeStruct((1, PATCHES, KV_WIDTH), jnp.float32)
-    call = in_vmem(last_kernel, "last_sum", 5, [grad, TILE], meta=False)
-    return call(kept, recv, *losses)
+    return in_vmem(last_kernel, "last_sum", 3, [grad, TILE], meta=False)(kept, recv, loss)
 
 
 def along_y(value, step):
@@ -609,8 +609,8 @@
     meta = make_meta(idx, image_list, patch_count, pref_order, caption_len)
 
     seen = [image] + [along_y(image, step) for step in (1, 2, 3)]
-    wanted = pick(pick_partner_kernel, "pick_partner", meta, *seen)
-    own = pick(pick_own_kernel, "pick_own", meta, *seen, across(wanted, "segment", 4))
+    wanted = pick(meta[AT_FOR_PARTNER], seen)
+    own = pick(meta[AT_OWN], [*seen, across(wanted, "segment", 4)])
     acc, top, total = attend_own(q, caption_kv[0])
     others = [across(own, "tp", mask) for mask in (2, 4, 6)]
     *others, top = lax.optimization_barrier((*others, top))
@@ -626,13 +626,12 @@
     rewards = [pair] + [across(pair, "tp", mask) for mask in (2, 4, 6)]
     mine, to_z1, to_z2, to_z3, loss = scaled_sum(meta, keep, recv, rewards)
     parts = [across(to_z1, "tp", 2), across(to_z2, "tp", 4), across(to_z3, "tp", 6)]
-    total = group_sum(mine, parts, direction, (loss, across(loss, "tp", 8)))
+    loss = loss + across(loss, "tp", 16)
+    losses = (loss, across(loss, "tp", 8))
+    total = group_sum(mine, parts, direction, losses)
     totals = [total] + [along_y(total, step) for step in (1, 2, 3)]
     kept, away, loss = sort_by_owner(meta, totals)
-    both = [(i, i ^ (4 * COLUMNS + 16)) for i in range(8 * COLUMNS)]
-    diagonal = lax.ppermute(loss, ("segment", "tp"), both)
-    losses = (loss, across(loss, "tp", 16), diagonal)
-    image_grad, loss = last_sum(kept, across(away, "segment", 4), losses)
+    image_grad, loss = last_sum(kept, across(away, "segment", 4), loss)
     return (loss[0, 0], reward[0, :1], image_grad)
 
 

time: 165 us -> 159 us (0.964)
  Pallas kernels: 78 us -> 70.9 us
  waiting for transfers between devices: 40.6 us -> 33.7 us
  between operations: 1.41 us -> 5.94 us
  other arithmetic: 1.41 us -> 3.32 us
    pallas_call x3 -> x1, Pallas kernels: 5.43 us -> 0.83 us  [last_sum(): in_vmem(last_kernel, 'last_sum', 3, [grad, TILE], meta=False)]
    ppermute x6, waiting for transfers between devices: 13.8 us -> 10.4 us  [along_y(): return lax.ppermute(value, 'segment', pairs)]
    ppermute x1 -> x0, waiting for transfers between devices: 2.37 us -> none  [per_device(): diagonal = lax.ppermute(loss, ('segment', 'tp'), both)]
    pallas_call x1, Pallas kernels: 55.4 us -> 53.2 us  [attend_images(): return call(meta, q, direction, *state, *images)]
    select_n x0 -> x2, other arithmetic: none -> 1.96 us  [pick(): chosen = jnp.where(which == k, images[k], chosen)]
    unnamed x30 -> x24, local copies, waits for them, and re-layouts: 5.91 us -> 4.54 us
  transfers between devices with their start and end apart: 26 -> 25, of which waited for: 18 -> 17; matrix products, arithmetic and copies ran while one was open for 3% -> 4% of each run, Pallas kernels for 9% -> 9%
where the time goes in v3:
time: 159 us; the launch traced here: 157 us
  Pallas kernels  70.9 us (45%)
  starting transfers between devices  35.3 us (22%)
  waiting for transfers between devices  33.7 us (21%)
  local copies, waits for them, and re-layouts  7.56 us (5%)
  between operations  5.94 us (4%)
  other arithmetic  3.32 us (2%)
    pallas_call x1, Pallas kernels, attend_images(): return call(meta, q, direction, *state, *images)  53.2 us
    ppermute x19, starting transfers between devices, across(): return lax.ppermute(value, axis, [(i, i ^ mask) for i in range(size)])  28.3 us
    ppermute x19, waiting for transfers between devices, across(): return lax.ppermute(value, axis, [(i, i ^ mask) for i in range(size)])  23.3 us
    pallas_call x1, Pallas kernels, attend_own(): return call(q, own_kv, own_kv)  12 us
    ppermute x6, waiting for transfers between devices, along_y(): return lax.ppermute(value, 'segment', pairs)  10.4 us
    ppermute x6, starting transfers between devices, along_y(): return lax.ppermute(value, 'segment', pairs)  7.05 us
    unnamed x24, local copies, waits for them, and re-layouts  4.54 us
  transfers between devices with their start and end apart: 25, of which 17 were waited for; matrix products, arithmetic and copies ran while one was open for 4% of the time, Pallas kernels for 9%

profile of v3, /device:TPU:32, one launch (start us, length us, event | category | flops | bytes accessed | tf_op | source)
XLA Modules:
  0.0 156.7 jit_solution(2708974910096725777)
XLA Ops:
  0.6 3.1 %collective-permute-start.2 = (bf16[48,2048]{1,0:T(8,128)(2,1)}, bf16[48,2048]{1,0:T(8,128)(2,1)S(1)}, u32[]{:S(2)}, u32[]{:S(2)}) collective-permute-start(bf16[48,2048]{1,0:T(8,128)(2,1)} %bitcast.19), channel_id=1, source_target_pairs={{0,96},{32,0},{64,32},{96,64},{128,224},{160,128},{192,160},{224,1... | collective-permute-start | bytes 589832 | tf_op jit(solution)/shard_map/ppermute | solution.py:594
  3.7 0.6 collective-permute-start.1
  4.4 1.0 collective-permute-start
  6.0 1.4 copy.11.list_ref
  7.3 1.4 copy.12.order_ref
  8.7 0.6 pad_add_fusion.idx_ref
  9.3 1.9 %meta.1.meta_ref = s32[32]{0:T(128)} custom-call(s32[2]{0:T(128)} %pad_add_fusion.idx_ref, s32[32,8]{1,0:T(8,128)} %copy.11.list_ref, s32[256]{0:T(256)} %count_ref.1, s32[32,8]{1,0:T(8,128)} %copy.12.order_ref, s32[1]{0:T(128)S(6)} %copy.13.len_ref), custom_call_target="tpu_custom_call" | custom-call | tf_op jit(solution)/shard_map/meta/pallas_call | solution.py:77
  11.2 1.3 fusion
  14.4 1.6 %collective-permute-done = bf16[48,2048]{1,0:T(8,128)(2,1)S(1)} collective-permute-done((bf16[48,2048]{1,0:T(8,128)(2,1)}, bf16[48,2048]{1,0:T(8,128)(2,1)S(1)}, u32[]{:S(2)}, u32[]{:S(2)}) %collective-permute-start) | collective-permute-done | bytes 196640 | tf_op jit(solution)/shard_map/ppermute | solution.py:594
  16.0 1.0 select_select_fusion.1
  17.0 3.1 %collective-permute-start.3 = (bf16[48,2048]{1,0:T(8,128)(2,1)S(1)}, bf16[48,2048]{1,0:T(8,128)(2,1)S(1)}, u32[]{:S(2)}, u32[]{:S(2)}) collective-permute-start(bf16[48,2048]{1,0:T(8,128)(2,1)S(1)} %select_select_fusion.1), channel_id=1, source_target_pairs={{0,128},{32,160},{64,192},{96,224},{128,0},{160,32},{192,64},{224,... | collective-permute-start | bytes 589832 | tf_op jit(solution)/shard_map/ppermute | solution.py:599
  22.7 2.7 %collective-permute-done.3 = bf16[48,2048]{1,0:T(8,128)(2,1)S(1)} collective-permute-done((bf16[48,2048]{1,0:T(8,128)(2,1)S(1)}, bf16[48,2048]{1,0:T(8,128)(2,1)S(1)}, u32[]{:S(2)}, u32[]{:S(2)}) %collective-permute-start.3) | collective-permute-done | bytes 196640 | tf_op jit(solution)/shard_map/ppermute | solution.py:599
  25.4 1.0 select_select_fusion.rest_0_
  26.4 2.0 %collective-permute-start.6 = (bf16[48,2048]{1,0:T(8,128)(2,1)S(1)}, bf16[48,2048]{1,0:T(8,128)(2,1)S(1)}, u32[]{:S(2)}, u32[]{:S(2)}) collective-permute-start(bf16[48,2048]{1,0:T(8,128)(2,1)S(1)} %select_select_fusion.rest_0_), channel_id=1, source_target_pairs={{0,6},{1,7},{2,4},{3,5},{4,2},{5,3},{6,0},{7,1},{8,14},{9,15},{10,... | collective-permute-start | bytes 589832 | tf_op jit(solution)/shard_map/ppermute | solution.py:599
  28.4 1.5 collective-permute-start.5
  29.9 1.4 collective-permute-start.4
  31.2 12.0 %attend_own.1 = (f32[8192,256]{1,0:T(8,128)}, f32[64,256]{1,0:T(8,128)}, f32[64,256]{1,0:T(8,128)}) custom-call(bf16[256,8192]{1,0:T(8,128)(2,1)} %bitcast.22, bf16[256,2048]{1,0:T(8,128)(2,1)} %bitcast.24, bf16[256,2048]{1,0:T(8,128)(2,1)} %bitcast.25), custom_call_target="tpu_custom_call" | custom-call | flops 2000000000 | bytes 16000000 | tf_op jit(solution)/shard_map/attend_own/pallas_call | solution.py:281
  43.2 1.3 collective-permute-done.5.rest_2_
  44.6 0.5 collective-permute-start.9
  45.2 0.8 collective-permute-done.8.rest_5_
  47.3 53.2 %attend_images.1 = (bf16[4,48,2176]{2,1,0:T(8,128)(2,1)}, bf16[4,48,2176]{2,1,0:T(8,128)(2,1)}, f32[8,128]{1,0:T(8,128)}) custom-call(s32[32]{0:T(128)} %meta.1.meta_ref, bf16[256,8192]{1,0:T(8,128)(2,1)} %bitcast.23, f32[64,128]{1,0:T(8,128)} %bitcast.17, f32[8192,256]{1,0:T(8,128)} %get-tuple-element.23.acc_hbm, f32[64,256]{1,0:T(8,128)} %get-tuple-element.25.max_ref, ...), custom_call_target="tpu_custom_call" | custom-call | flops 8000000000 | bytes 18000000 | tf_op jit(solution)/shard_map/attend_images/pallas_call | solution.py:447
  101.1 2.1 %collective-permute-done.12 = f32[8,128]{1,0:T(8,128)S(1)} collective-permute-done((f32[8,128]{1,0:T(8,128)}, f32[8,128]{1,0:T(8,128)S(1)}, u32[]{:S(2)}, u32[]{:S(2)}) %collective-permute-start.12) | collective-permute-done | bytes 4128 | tf_op jit(solution)/shard_map/ppermute | solution.py:599
  103.1 0.8 broadcast_select_fusion.rest_0_
  104.4 4.2 %collective-permute-start.14 = (f32[8,128]{1,0:T(8,128)S(1)}, f32[8,128]{1,0:T(8,128)S(1)}, u32[]{:S(2)}, u32[]{:S(2)}) collective-permute-start(f32[8,128]{1,0:T(8,128)S(1)} %broadcast_select_fusion.rest_0_), channel_id=1, source_target_pairs={{0,4},{1,5},{2,6},{3,7},{4,0},{5,1},{6,2},{7,3},{8,12},{9,13},{10,... | collective-permute-start | bytes 12296 | tf_op jit(solution)/shard_map/ppermute | solution.py:599
  108.8 1.3 collective-permute-done.14.rest_2_
  110.2 2.0 %collective-permute-done.13.rest_1_ = f32[8,128]{1,0:T(8,128)S(1)} collective-permute-done((f32[8,128]{1,0:T(8,128)S(1)}, f32[8,128]{1,0:T(8,128)S(1)}, u32[]{:S(2)}, u32[]{:S(2)}) %collective-permute-start.13) | collective-permute-done | bytes 4128 | tf_op jit(solution)/shard_map/ppermute | solution.py:599
  112.1 1.1 copy-done
  113.3 1.2 scaled_sum.1
  114.5 1.3 collective-permute-start.16
  115.8 2.0 %collective-permute-start.17 = (bf16[48,2176]{1,0:T(8,128)(2,1)S(1)}, bf16[48,2176]{1,0:T(8,128)(2,1)S(1)}, u32[]{:S(2)}, u32[]{:S(2)}) collective-permute-start(bf16[48,2176]{1,0:T(8,128)(2,1)S(1)} %get-tuple-element.35), channel_id=1, source_target_pairs={{0,4},{1,5},{2,6},{3,7},{4,0},{5,1},{6,2},{7,3},{8,12},{9,13},{10,... | collective-permute-start | bytes 626696 | tf_op jit(solution)/shard_map/ppermute | solution.py:599
  118.1 1.5 collective-permute-start.19
  119.6 2.1 %collective-permute-done.19 = f32[8,128]{1,0:T(8,128)S(1)} collective-permute-done((f32[8,128]{1,0:T(8,128)S(1)}, f32[8,128]{1,0:T(8,128)S(1)}, u32[]{:S(2)}, u32[]{:S(2)}) %collective-permute-start.19) | collective-permute-done | bytes 4128 | tf_op jit(solution)/shard_map/ppermute | solution.py:599
  121.7 6.0 %collective-permute-start.20 = (f32[8,128]{1,0:T(8,128)S(1)}, f32[8,128]{1,0:T(8,128)S(1)}, u32[]{:S(2)}, u32[]{:S(2)}) collective-permute-start(f32[8,128]{1,0:T(8,128)S(1)} %add.8.l0_ref), channel_id=1, source_target_pairs={{0,8},{1,9},{2,10},{3,11},{4,12},{5,13},{6,14},{7,15},{8,0},{9,1},... | collective-permute-start | bytes 12296 | tf_op jit(solution)/shard_map/ppermute | solution.py:599
  127.7 1.6 %collective-permute-done.20.l1_ref = f32[8,128]{1,0:T(8,128)S(1)} collective-permute-done((f32[8,128]{1,0:T(8,128)S(1)}, f32[8,128]{1,0:T(8,128)S(1)}, u32[]{:S(2)}, u32[]{:S(2)}) %collective-permute-start.20) | collective-permute-done | bytes 4128 | tf_op jit(solution)/shard_map/ppermute | solution.py:599
  129.3 2.1 %collective-permute-done.17.b_ref = bf16[48,2176]{1,0:T(8,128)(2,1)S(1)} collective-permute-done((bf16[48,2176]{1,0:T(8,128)(2,1)S(1)}, bf16[48,2176]{1,0:T(8,128)(2,1)S(1)}, u32[]{:S(2)}, u32[]{:S(2)}) %collective-permute-start.17) | collective-permute-done | bytes 208928 | tf_op jit(solution)/shard_map/ppermute | solution.py:599
  131.4 3.6 %collective-permute-done.18.c_ref = bf16[48,2176]{1,0:T(8,128)(2,1)S(1)} collective-permute-done((bf16[48,2176]{1,0:T(8,128)(2,1)S(1)}, bf16[48,2176]{1,0:T(8,128)(2,1)S(1)}, u32[]{:S(2)}, u32[]{:S(2)}) %collective-permute-start.18) | collective-permute-done | bytes 208928 | tf_op jit(solution)/shard_map/ppermute | solution.py:599
  135.0 0.7 group_sum.1.s0
  136.0 0.7 collective-permute-start.22
  136.7 1.3 collective-permute-start.21
  138.1 5.0 %collective-permute-done.23.s3 = bf16[48,2176]{1,0:T(8,128)(2,1)S(1)} collective-permute-done((bf16[48,2176]{1,0:T(8,128)(2,1)S(1)}, bf16[48,2176]{1,0:T(8,128)(2,1)S(1)}, u32[]{:S(2)}, u32[]{:S(2)}) %collective-permute-start.23) | collective-permute-done | bytes 208928 | tf_op jit(solution)/shard_map/ppermute | solution.py:594
  143.1 1.6 %collective-permute-done.22.s2 = bf16[48,2176]{1,0:T(8,128)(2,1)S(1)} collective-permute-done((bf16[48,2176]{1,0:T(8,128)(2,1)S(1)}, bf16[48,2176]{1,0:T(8,128)(2,1)S(1)}, u32[]{:S(2)}, u32[]{:S(2)}) %collective-permute-start.22) | collective-permute-done | bytes 208928 | tf_op jit(solution)/shard_map/ppermute | solution.py:594
  144.7 2.2 %collective-permute-done.21.s1 = bf16[48,2176]{1,0:T(8,128)(2,1)S(1)} collective-permute-done((bf16[48,2176]{1,0:T(8,128)(2,1)S(1)}, bf16[48,2176]{1,0:T(8,128)(2,1)S(1)}, u32[]{:S(2)}, u32[]{:S(2)}) %collective-permute-start.21) | collective-permute-done | bytes 208928 | tf_op jit(solution)/shard_map/ppermute | solution.py:594
  146.9 1.1 sort_by_owner.1
  147.9 3.2 %collective-permute-start.24 = (bf16[48,2176]{1,0:T(8,128)(2,1)S(1)}, bf16[48,2176]{1,0:T(8,128)(2,1)S(1)}, u32[]{:S(2)}, u32[]{:S(2)}) collective-permute-start(bf16[48,2176]{1,0:T(8,128)(2,1)S(1)} %get-tuple-element.39), channel_id=1, source_target_pairs={{0,128},{32,160},{64,192},{96,224},{128,0},{160,32},{192,64},{224,... | collective-permute-start | bytes 626696 | tf_op jit(solution)/shard_map/ppermute | solution.py:599
  151.1 1.2 slice.15
  152.3 3.0 %collective-permute-done.24.recv_ref = bf16[48,2176]{1,0:T(8,128)(2,1)S(1)} collective-permute-done((bf16[48,2176]{1,0:T(8,128)(2,1)S(1)}, bf16[48,2176]{1,0:T(8,128)(2,1)S(1)}, u32[]{:S(2)}, u32[]{:S(2)}) %collective-permute-start.24) | collective-permute-done | bytes 208928 | tf_op jit(solution)/shard_map/ppermute | solution.py:599
  155.3 0.8 last_sum.1
  156.2 0.5 slice.14
  (42 shorter events, 3.3 us)
Async XLA Ops:
  0.6 13.8 %collective-permute-start.2 = (bf16[48,2048]{1,0:T(8,128)(2,1)}, bf16[48,2048]{1,0:T(8,128)(2,1)S(1)}, u32[]{:S(2)}, u32[]{:S(2)}) collective-permute-start(bf16[48,2048]{1,0:T(8,128)(2,1)} %bitcast.19), channel_id=1, source_target_pairs={{0,96},{32,0},{64,32},{96,64},{128,224},{160,128},{192,160},{224,1... | collective-permute-start | bytes 589832 | tf_op jit(solution)/shard_map/ppermute | solution.py:594
  3.7 10.7 %collective-permute-start.1 = (bf16[48,2048]{1,0:T(8,128)(2,1)}, bf16[48,2048]{1,0:T(8,128)(2,1)S(1)}, u32[]{:S(2)}, u32[]{:S(2)}) collective-permute-start(bf16[48,2048]{1,0:T(8,128)(2,1)} %bitcast.20), channel_id=1, source_target_pairs={{0,64},{32,96},{64,0},{96,32},{128,192},{160,224},{192,128},{224,1... | collective-permute-start | bytes 589832 | tf_op jit(solution)/shard_map/ppermute | solution.py:594
  4.4 11.7 %collective-permute-start = (bf16[48,2048]{1,0:T(8,128)(2,1)}, bf16[48,2048]{1,0:T(8,128)(2,1)S(1)}, u32[]{:S(2)}, u32[]{:S(2)}) collective-permute-start(bf16[48,2048]{1,0:T(8,128)(2,1)} %bitcast.21), channel_id=1, source_target_pairs={{0,32},{32,64},{64,96},{96,0},{128,160},{160,192},{192,224},{224,1... | collective-permute-start | bytes 589832 | tf_op jit(solution)/shard_map/ppermute | solution.py:594
  17.0 8.4 %collective-permute-start.3 = (bf16[48,2048]{1,0:T(8,128)(2,1)S(1)}, bf16[48,2048]{1,0:T(8,128)(2,1)S(1)}, u32[]{:S(2)}, u32[]{:S(2)}) collective-permute-start(bf16[48,2048]{1,0:T(8,128)(2,1)S(1)} %select_select_fusion.1), channel_id=1, source_target_pairs={{0,128},{32,160},{64,192},{96,224},{128,0},{160,32},{192,64},{224,... | collective-permute-start | bytes 589832 | tf_op jit(solution)/shard_map/ppermute | solution.py:599
  26.4 20.2 %copy-start.3 = (bf16[48,2048]{1,0:T(8,128)(2,1)}, bf16[48,2048]{1,0:T(8,128)(2,1)S(1)}, u32[]{:S(2)}) copy-start(bf16[48,2048]{1,0:T(8,128)(2,1)S(1)} %select_select_fusion.rest_0_) | copy-start | bytes 589828
  26.4 16.8 %collective-permute-start.6 = (bf16[48,2048]{1,0:T(8,128)(2,1)S(1)}, bf16[48,2048]{1,0:T(8,128)(2,1)S(1)}, u32[]{:S(2)}, u32[]{:S(2)}) collective-permute-start(bf16[48,2048]{1,0:T(8,128)(2,1)S(1)} %select_select_fusion.rest_0_), channel_id=1, source_target_pairs={{0,6},{1,7},{2,4},{3,5},{4,2},{5,3},{6,0},{7,1},{8,14},{9,15},{10,... | collective-permute-start | bytes 589832 | tf_op jit(solution)/shard_map/ppermute | solution.py:599
  28.4 16.2 %collective-permute-start.5 = (bf16[48,2048]{1,0:T(8,128)(2,1)S(1)}, bf16[48,2048]{1,0:T(8,128)(2,1)S(1)}, u32[]{:S(2)}, u32[]{:S(2)}) collective-permute-start(bf16[48,2048]{1,0:T(8,128)(2,1)S(1)} %select_select_fusion.rest_0_), channel_id=1, source_target_pairs={{0,4},{1,5},{2,6},{3,7},{4,0},{5,1},{6,2},{7,3},{8,12},{9,13},{10,... | collective-permute-start | bytes 589832 | tf_op jit(solution)/shard_map/ppermute | solution.py:599
  29.9 14.7 %collective-permute-start.4 = (bf16[48,2048]{1,0:T(8,128)(2,1)S(1)}, bf16[48,2048]{1,0:T(8,128)(2,1)S(1)}, u32[]{:S(2)}, u32[]{:S(2)}) collective-permute-start(bf16[48,2048]{1,0:T(8,128)(2,1)S(1)} %select_select_fusion.rest_0_), channel_id=1, source_target_pairs={{0,2},{1,3},{2,0},{3,1},{4,6},{5,7},{6,4},{7,5},{8,10},{9,11},{10,... | collective-permute-start | bytes 589832 | tf_op jit(solution)/shard_map/ppermute | solution.py:599
  43.2 2.0 %collective-permute-start.7 = (bf16[48,2048]{1,0:T(8,128)(2,1)S(1)}, bf16[48,2048]{1,0:T(8,128)(2,1)S(1)}, u32[]{:S(2)}, u32[]{:S(2)}) collective-permute-start(bf16[48,2048]{1,0:T(8,128)(2,1)S(1)} %select_select_fusion.rest_0_), channel_id=1, source_target_pairs={{0,1},{1,0},{2,3},{3,2},{4,5},{5,4},{6,7},{7,6},{8,9},{9,8},{10,11... | collective-permute-start | bytes 589832 | tf_op jit(solution)/shard_map/ppermute | solution.py:599
  43.2 3.4 %copy-start.4 = (bf16[48,2048]{1,0:T(8,128)(2,1)}, bf16[48,2048]{1,0:T(8,128)(2,1)S(1)}, u32[]{:S(2)}) copy-start(bf16[48,2048]{1,0:T(8,128)(2,1)S(1)} %collective-permute-done.6.rest_3_) | copy-start | bytes 589828
  44.6 2.0 %copy-start.5 = (bf16[48,2048]{1,0:T(8,128)(2,1)}, bf16[48,2048]{1,0:T(8,128)(2,1)S(1)}, u32[]{:S(2)}) copy-start(bf16[48,2048]{1,0:T(8,128)(2,1)S(1)} %collective-permute-done.5.rest_2_) | copy-start | bytes 589828
  44.6 2.0 %copy-start.6 = (bf16[48,2048]{1,0:T(8,128)(2,1)}, bf16[48,2048]{1,0:T(8,128)(2,1)S(1)}, u32[]{:S(2)}) copy-start(bf16[48,2048]{1,0:T(8,128)(2,1)S(1)} %collective-permute-done.4.rest_1_) | copy-start | bytes 589828
  44.6 1.4 collective-permute-start.8
  44.6 1.7 %collective-permute-start.9 = (bf16[48,2048]{1,0:T(8,128)(2,1)S(1)}, bf16[48,2048]{1,0:T(8,128)(2,1)S(1)}, u32[]{:S(2)}, u32[]{:S(2)}) collective-permute-start(bf16[48,2048]{1,0:T(8,128)(2,1)S(1)} %collective-permute-done.5.rest_2_), channel_id=1, source_target_pairs={{0,1},{1,0},{2,3},{3,2},{4,5},{5,4},{6,7},{7,6},{8,9},{9,8},{10,11... | collective-permute-start | bytes 589832 | tf_op jit(solution)/shard_map/ppermute | solution.py:599
  45.1 1.5 collective-permute-start.10
  45.2 1.4 copy-start.7
  46.0 0.7 copy-start.8
  46.3 0.7 copy-start.9
  46.6 0.7 copy-start.10
  47.3 64.9 %copy-start.2 = (s32[32]{0:T(128)S(1)}, s32[32]{0:T(128)}, u32[]{:S(2)}) copy-start(s32[32]{0:T(128)} %meta.1.meta_ref) | copy-start | bytes 388
  47.3 87.7 %copy-start.1 = (f32[8192]{0:T(1024)S(1)}, f32[8192]{0:T(1024)}, u32[]{:S(2)}) copy-start(f32[8192]{0:T(1024)} %param.15) | copy-start | bytes 98308
  100.5 11.6 %collective-permute-start.11 = (bf16[4,48,2176]{2,1,0:T(8,128)(2,1)}, bf16[4,48,2176]{2,1,0:T(8,128)(2,1)S(1)}, u32[]{:S(2)}, u32[]{:S(2)}) collective-permute-start(bf16[4,48,2176]{2,1,0:T(8,128)(2,1)} %get-tuple-element.31), channel_id=1, source_target_pairs={{0,1},{1,0},{2,3},{3,2},{4,5},{5,4},{6,7},{7,6},{8,9},{9,8},{10,11... | collective-permute-start | bytes 2506760 | tf_op jit(solution)/shard_map/ppermute | solution.py:599
  100.8 2.3 %collective-permute-start.12 = (f32[8,128]{1,0:T(8,128)}, f32[8,128]{1,0:T(8,128)S(1)}, u32[]{:S(2)}, u32[]{:S(2)}) collective-permute-start(f32[8,128]{1,0:T(8,128)} %get-tuple-element.32), channel_id=1, source_target_pairs={{0,1},{1,0},{2,3},{3,2},{4,5},{5,4},{6,7},{7,6},{8,9},{9,8},{10,11... | collective-permute-start | bytes 12296 | tf_op jit(solution)/shard_map/ppermute | solution.py:599
  103.9 4.9 %collective-permute-start.15 = (f32[8,128]{1,0:T(8,128)S(1)}, f32[8,128]{1,0:T(8,128)S(1)}, u32[]{:S(2)}, u32[]{:S(2)}) collective-permute-start(f32[8,128]{1,0:T(8,128)S(1)} %broadcast_select_fusion.rest_0_), channel_id=1, source_target_pairs={{0,6},{1,7},{2,4},{3,5},{4,2},{5,3},{6,0},{7,1},{8,14},{9,15},{10,... | collective-permute-start | bytes 12296 | tf_op jit(solution)/shard_map/ppermute | solution.py:599
  104.4 5.8 %collective-permute-start.14 = (f32[8,128]{1,0:T(8,128)S(1)}, f32[8,128]{1,0:T(8,128)S(1)}, u32[]{:S(2)}, u32[]{:S(2)}) collective-permute-start(f32[8,128]{1,0:T(8,128)S(1)} %broadcast_select_fusion.rest_0_), channel_id=1, source_target_pairs={{0,4},{1,5},{2,6},{3,7},{4,0},{5,1},{6,2},{7,3},{8,12},{9,13},{10,... | collective-permute-start | bytes 12296 | tf_op jit(solution)/shard_map/ppermute | solution.py:599
  108.5 3.6 %collective-permute-start.13 = (f32[8,128]{1,0:T(8,128)S(1)}, f32[8,128]{1,0:T(8,128)S(1)}, u32[]{:S(2)}, u32[]{:S(2)}) collective-permute-start(f32[8,128]{1,0:T(8,128)S(1)} %broadcast_select_fusion.rest_0_), channel_id=1, source_target_pairs={{0,2},{1,3},{2,0},{3,1},{4,6},{5,7},{6,4},{7,5},{8,10},{9,11},{10,... | collective-permute-start | bytes 12296 | tf_op jit(solution)/shard_map/ppermute | solution.py:599
  112.1 1.2 copy-start
  114.5 14.8 %collective-permute-start.16 = (bf16[48,2176]{1,0:T(8,128)(2,1)S(1)}, bf16[48,2176]{1,0:T(8,128)(2,1)S(1)}, u32[]{:S(2)}, u32[]{:S(2)}) collective-permute-start(bf16[48,2176]{1,0:T(8,128)(2,1)S(1)} %get-tuple-element.34), channel_id=1, source_target_pairs={{0,2},{1,3},{2,0},{3,1},{4,6},{5,7},{6,4},{7,5},{8,10},{9,11},{10,... | collective-permute-start | bytes 626696 | tf_op jit(solution)/shard_map/ppermute | solution.py:599
  115.8 15.6 %collective-permute-start.17 = (bf16[48,2176]{1,0:T(8,128)(2,1)S(1)}, bf16[48,2176]{1,0:T(8,128)(2,1)S(1)}, u32[]{:S(2)}, u32[]{:S(2)}) collective-permute-start(bf16[48,2176]{1,0:T(8,128)(2,1)S(1)} %get-tuple-element.35), channel_id=1, source_target_pairs={{0,4},{1,5},{2,6},{3,7},{4,0},{5,1},{6,2},{7,3},{8,12},{9,13},{10,... | collective-permute-start | bytes 626696 | tf_op jit(solution)/shard_map/ppermute | solution.py:599
  117.8 17.2 %collective-permute-start.18 = (bf16[48,2176]{1,0:T(8,128)(2,1)S(1)}, bf16[48,2176]{1,0:T(8,128)(2,1)S(1)}, u32[]{:S(2)}, u32[]{:S(2)}) collective-permute-start(bf16[48,2176]{1,0:T(8,128)(2,1)S(1)} %get-tuple-element.36), channel_id=1, source_target_pairs={{0,6},{1,7},{2,4},{3,5},{4,2},{5,3},{6,0},{7,1},{8,14},{9,15},{10,... | collective-permute-start | bytes 626696 | tf_op jit(solution)/shard_map/ppermute | solution.py:599
  118.1 3.6 %collective-permute-start.19 = (f32[8,128]{1,0:T(8,128)S(1)}, f32[8,128]{1,0:T(8,128)S(1)}, u32[]{:S(2)}, u32[]{:S(2)}) collective-permute-start(f32[8,128]{1,0:T(8,128)S(1)} %get-tuple-element.37), channel_id=1, source_target_pairs={{0,16},{1,17},{2,18},{3,19},{4,20},{5,21},{6,22},{7,23},{8,24},{9,... | collective-permute-start | bytes 12296 | tf_op jit(solution)/shard_map/ppermute | solution.py:599
  121.7 7.6 %collective-permute-start.20 = (f32[8,128]{1,0:T(8,128)S(1)}, f32[8,128]{1,0:T(8,128)S(1)}, u32[]{:S(2)}, u32[]{:S(2)}) collective-permute-start(f32[8,128]{1,0:T(8,128)S(1)} %add.8.l0_ref), channel_id=1, source_target_pairs={{0,8},{1,9},{2,10},{3,11},{4,12},{5,13},{6,14},{7,15},{8,0},{9,1},... | collective-permute-start | bytes 12296 | tf_op jit(solution)/shard_map/ppermute | solution.py:599
  135.7 7.4 %collective-permute-start.23 = (bf16[48,2176]{1,0:T(8,128)(2,1)S(1)}, bf16[48,2176]{1,0:T(8,128)(2,1)S(1)}, u32[]{:S(2)}, u32[]{:S(2)}) collective-permute-start(bf16[48,2176]{1,0:T(8,128)(2,1)S(1)} %group_sum.1.s0), channel_id=1, source_target_pairs={{0,96},{32,0},{64,32},{96,64},{128,224},{160,128},{192,160},{224,1... | collective-permute-start | bytes 626696 | tf_op jit(solution)/shard_map/ppermute | solution.py:594
  136.0 8.7 %collective-permute-start.22 = (bf16[48,2176]{1,0:T(8,128)(2,1)S(1)}, bf16[48,2176]{1,0:T(8,128)(2,1)S(1)}, u32[]{:S(2)}, u32[]{:S(2)}) collective-permute-start(bf16[48,2176]{1,0:T(8,128)(2,1)S(1)} %group_sum.1.s0), channel_id=1, source_target_pairs={{0,64},{32,96},{64,0},{96,32},{128,192},{160,224},{192,128},{224,1... | collective-permute-start | bytes 626696 | tf_op jit(solution)/shard_map/ppermute | solution.py:594
  136.7 10.1 %collective-permute-start.21 = (bf16[48,2176]{1,0:T(8,128)(2,1)S(1)}, bf16[48,2176]{1,0:T(8,128)(2,1)S(1)}, u32[]{:S(2)}, u32[]{:S(2)}) collective-permute-start(bf16[48,2176]{1,0:T(8,128)(2,1)S(1)} %group_sum.1.s0), channel_id=1, source_target_pairs={{0,32},{32,64},{64,96},{96,0},{128,160},{160,192},{192,224},{224,1... | collective-permute-start | bytes 626696 | tf_op jit(solution)/shard_map/ppermute | solution.py:594
  147.9 7.4 %collective-permute-start.24 = (bf16[48,2176]{1,0:T(8,128)(2,1)S(1)}, bf16[48,2176]{1,0:T(8,128)(2,1)S(1)}, u32[]{:S(2)}, u32[]{:S(2)}) collective-permute-start(bf16[48,2176]{1,0:T(8,128)(2,1)S(1)} %get-tuple-element.39), channel_id=1, source_target_pairs={{0,128},{32,160},{64,192},{96,224},{128,0},{160,32},{192,64},{224,... | collective-permute-start | bytes 626696 | tf_op jit(solution)/shard_map/ppermute | solution.py:599

commit v4 on v3

--- a/solution.py
+++ b/solution.py
@@ -30,7 +30,7 @@
 SMEM = pltpu.SMEM
 VMEM = pltpu.VMEM
 VMEM_LIMIT = 16 * 1024 * 1024
-BIG_LIMIT = 56 * 1024 * 1024
+BIG_LIMIT = 48 * 1024 * 1024
 
 AT_FOR_PARTNER, AT_OWN, AT_PLACE, AT_LEN = 0, 1, 2, 3
 AT_COUNTS, AT_RANKING, AT_DEST = 8, 16, 24
@@ -169,81 +169,58 @@
     return jnp.concatenate(keys, axis=0), with_marks(values, marks)
 
 
-def forward_step(head, meta_ref, q_ref, dir_ref, state, images, kept, stat_ref, reward_ref, sum_refs):
+def forward_step(head, exact, meta_ref, q_ref, dir_ref, state, images, kept, sum_refs):
     acc_in, max_in, sum_in = state
     p_ref, att_ref, inv_ref = kept
-    ss_ref, rd_ref = sum_refs
+    ss_ref, rd_ref, top_ref = sum_refs
     keys, mixed = image_parts(meta_ref, images, *head_columns(head))
     dir_t = dir_ref[...].T
+    sums = [ss_ref[...], rd_ref[...], top_ref[...]]
 
     def start(g, _):
         return exact_dot(keys, q_ref[:, column(g)], ((1,), (1,)))
 
-    def attended(p, acc, total):
+    def soft(g, s):
+        old = max_in[g : g + 1, :]
+        shrink = None
+        if exact:
+            new = jnp.maximum(old, jnp.max(s, axis=0, keepdims=True) * to_base2)
+            shrink, old = jnp.exp2(old - new), new
+        p = jnp.exp2(s * to_base2 - old).astype(jnp.bfloat16)
+        p_ref[g] = p
+        return p, shrink
+
+    def finish(g, before):
+        p, shrink = before
+        acc, total = acc_in[column(g), :], sum_in[g : g + 1, :]
+        if exact:
+            acc, total = acc * shrink, total * shrink
         out = exact_dot(mixed, p, ((1,), (0,)))
         total = total + out[HEAD_DIM : HEAD_DIM + 1]
-        return (acc + out[:HEAD_DIM]) * (1.0 / total), total
-
-    def square_and_reward(att, dir_col):
-        ss = jnp.sum((att * att).reshape(16, 8, CAP_LEN), axis=0)
-        return ss, jnp.sum((att * dir_col).reshape(16, 8, CAP_LEN), axis=0)
-
-    zero = jnp.zeros((8, CAP_LEN), jnp.float32)
-    sums = [zero, zero, jnp.zeros((1, CAP_LEN), jnp.float32)]
-
-    def soft(g, s):
-        p = jnp.exp2(s * to_base2 - max_in[g : g + 1, :]).astype(jnp.bfloat16)
-        p_ref[g] = p
-        return p
-
-    def finish(g, p):
-        att, total = attended(p, acc_in[column(g), :], sum_in[g : g + 1, :])
+        inv = 1.0 / total
+        att = (acc + out[:HEAD_DIM]) * inv
         att_ref[column(g), :] = att
-        inv_ref[g : g + 1, :] = 1.0 / total
-        ss, rd = square_and_reward(att, dir_t[:, g : g + 1])
-        sums[0] += ss
-        sums[1] += rd
+        inv_ref[g : g + 1, :] = inv
+        sums[0] += jnp.sum((att * att).reshape(16, 8, CAP_LEN), axis=0)
+        sums[1] += jnp.sum((att * dir_t[:, g : g + 1]).reshape(16, 8, CAP_LEN), axis=0)
         sums[2] = jnp.maximum(sums[2], total)
 
     pipelined(GROUP_HEADS, start, soft, finish)
-    inside = jnp.max(sums[2]) < SUM_HIGH
-
-    @pl.when(inside)
-    def _():
-        ss_ref[...] += sums[0]
-        rd_ref[...] += sums[1]
-
-    @pl.when(jnp.logical_not(inside))
-    def _():
-        for g in range(GROUP_HEADS):
-            s = start(g, None)
-            old = max_in[g : g + 1, :]
-            new = jnp.maximum(old, jnp.max(s, axis=0, keepdims=True) * to_base2)
-            shrink = jnp.exp2(old - new)
-            p = jnp.exp2(s * to_base2 - new).astype(jnp.bfloat16)
-            p_ref[g] = p
-            att, total = attended(p, acc_in[column(g), :] * shrink, sum_in[g : g + 1, :] * shrink)
-            att_ref[column(g), :] = att
-            inv_ref[g : g + 1, :] = 1.0 / total
-            ss, rd = square_and_reward(att, dir_t[:, g : g + 1])
-            ss_ref[...] += ss
-            rd_ref[...] += rd
-
-    @pl.when(head == KV_HEADS - 1)
-    def _():
-        ss = ss_ref[...]
-        rd = rd_ref[...]
-        length = meta_ref[AT_LEN]
-        inv_rms = lax.rsqrt(jnp.sum(ss, axis=0, keepdims=True) * (1.0 / D) + norm_eps)
-        per_token = jnp.sum(rd, axis=0, keepdims=True) * inv_rms
-        live = lax.broadcasted_iota(jnp.int32, (1, CAP_LEN), 1) < length
-        length_f = jnp.full((1, CAP_LEN), length, jnp.int32).astype(jnp.float32)
-        unit = jnp.where(live, 1.0 / length_f, 0.0)
-        a = inv_rms * unit
-        b = inv_rms * inv_rms * unit * per_token * (1.0 / D)
-        stat_ref[...] = jnp.concatenate([a, b, jnp.zeros((6, CAP_LEN), jnp.float32)], axis=0)
-        reward = jnp.sum(jnp.where(live, per_token, 0.0), axis=1, keepdims=True)
-        reward_ref[...] = jnp.broadcast_to(reward / length_f[:, :1], (8, 128))
+    ss_ref[...], rd_ref[...], top_ref[...] = sums
+
+
+def token_factors(meta_ref, ss_ref, rd_ref, stat_ref, reward_ref):
+    length = meta_ref[AT_LEN]
+    inv_rms = lax.rsqrt(jnp.sum(ss_ref[...], axis=0, keepdims=True) * (1.0 / D) + norm_eps)
+    per_token = jnp.sum(rd_ref[...], axis=0, keepdims=True) * inv_rms
+    live = lax.broadcasted_iota(jnp.int32, (1, CAP_LEN), 1) < length
+    length_f = jnp.full((1, CAP_LEN), length, jnp.int32).astype(jnp.float32)
+    unit = jnp.where(live, 1.0 / length_f, 0.0)
+    a = inv_rms * unit
+    b = inv_rms * inv_rms * unit * per_token * (1.0 / D)
+    stat_ref[...] = jnp.concatenate([a, b, jnp.zeros((6, CAP_LEN), jnp.float32)], axis=0)
+    reward = jnp.sum(jnp.where(live, per_token, 0.0), axis=1, keepdims=True)
+    reward_ref[...] = jnp.broadcast_to(reward / length_f[:, :1], (8, 128))
 
 
 ROWS = GROUP_HEADS * HEAD_DIM
@@ -264,7 +241,7 @@
         out_specs=out_specs,
         out_shape=out_shape,
         scratch_shapes=scratch,
-        compiler_params=pltpu.CompilerParams(vmem_limit_bytes=BIG_LIMIT),
+        compiler_params=pltpu.CompilerParams(vmem_limit_bytes=VMEM_LIMIT),
         cost_estimate=pl.CostEstimate(
             flops=flops, bytes_accessed=16_000_000, transcendentals=4_000_000
         ),
@@ -359,7 +336,7 @@
     sources = rest[:CAPS]
     keep_ref, send_ref, reward_ref = rest[CAPS : CAPS + 3]
     q_all, acc_all, image_all, p_all, att_all, inv_all = rest[CAPS + 3 : CAPS + 9]
-    stat_ref, ss_ref, rd_ref, coef_ref, q_sem, acc_sem, image_sem = rest[CAPS + 9 :]
+    stat_ref, ss_ref, rd_ref, top_ref, coef_ref, q_sem, acc_sem, image_sem = rest[CAPS + 9 :]
 
     def q_copy(head):
         cols = pl.ds(pl.multiple_of(head * ROWS, ROWS), ROWS)
@@ -379,9 +356,9 @@
     acc_copy(0).start()
     q_copy(1).start()
     acc_copy(1).start()
-    ss_ref[...] = jnp.zeros_like(ss_ref)
-    rd_ref[...] = jnp.zeros_like(rd_ref)
-    coef_ref[...] = jnp.zeros_like(coef_ref)
+    sums = (ss_ref, rd_ref, top_ref)
+    for ref in (*sums, coef_ref):
+        ref[...] = jnp.zeros_like(ref)
     for copy in copies:
         copy.wait()
     images = [image_all.at[i] for i in range(CAPS)]
@@ -391,6 +368,11 @@
         kept = (p_all.at[head], att_all.at[head], inv_all.at[head])
         return rows, q_all.at[head], dir_ref.at[rows, :], kept
 
+    def forward_head(head, exact):
+        rows, q_ref, dirs, kept = of_head(head)
+        state = (acc_all.at[head], max_ref.at[rows, :], sum_ref.at[rows, :])
+        forward_step(head, exact, meta_ref, q_ref, dirs, state, images, kept, sums)
+
     @pl.loop(0, KV_HEADS)
     def _(head):
         q_copy(head).wait()
@@ -401,10 +383,18 @@
             q_copy(head + 2).start()
             acc_copy(head + 2).start()
 
-        rows, q_ref, dirs, kept = of_head(head)
-        state = (acc_all.at[head], max_ref.at[rows, :], sum_ref.at[rows, :])
-        sums = (ss_ref, rd_ref)
-        forward_step(head, meta_ref, q_ref, dirs, state, images, kept, stat_ref, reward_ref, sums)
+        forward_head(head, False)
+
+    @pl.when(jnp.logical_not(jnp.max(top_ref[...]) < SUM_HIGH))
+    def _():
+        for ref in sums:
+            ref[...] = jnp.zeros_like(ref)
+
+        @pl.loop(0, KV_HEADS)
+        def _(head):
+            forward_head(head, True)
+
+    token_factors(meta_ref, ss_ref, rd_ref, stat_ref, reward_ref)
 
     @pl.loop(0, KV_HEADS)
     def _(head):
@@ -433,6 +423,7 @@
             row,
             row,
             row,
+            VMEM((1, CAP_LEN), jnp.float32),
             VMEM((IMG_SLOTS, HEAD_DIM), jnp.float32),
             pltpu.SemaphoreType.DMA((KV_HEADS,)),
             pltpu.SemaphoreType.DMA((KV_HEADS,)),
@@ -581,12 +572,13 @@
 
 def last_kernel(keep_ref, recv_ref, loss_in_ref, out_ref, loss_ref):
     out_ref[0] = keep_ref[...] + recv_ref[:, :KV_WIDTH].astype(jnp.float32)
-    loss_ref[...] = loss_in_ref[...] + read_loss(recv_ref)
+    loss_ref[...] = (loss_in_ref[...] + read_loss(recv_ref))[:1, :1]
 
 
 def last_sum(kept, recv, loss):
     grad = jax.ShapeDtypeStruct((1, PATCHES, KV_WIDTH), jnp.float32)
-    return in_vmem(last_kernel, "last_sum", 3, [grad, TILE], meta=False)(kept, recv, loss)
+    one = jax.ShapeDtypeStruct((1, 1), jnp.float32)
+    return in_vmem(last_kernel, "last_sum", 3, [grad, one], meta=False)(kept, recv, loss)
 
 
 def along_y(value, step):
@@ -632,7 +624,7 @@
     totals = [total] + [along_y(total, step) for step in (1, 2, 3)]
     kept, away, loss = sort_by_owner(meta, totals)
     image_grad, loss = last_sum(kept, across(away, "segment", 4), loss)
-    return (loss[0, 0], reward[0, :1], image_grad)
+    return (loss.reshape(()), reward[0, :1], image_grad)
 
 
 def solution(mesh):

time: 159 us -> 144 us (0.906); the launches traced: 157 us -> 143 us
  Pallas kernels: 70.9 us -> 55.7 us
  local copies, waits for them, and re-layouts: 7.56 us -> 11.3 us
    pallas_call x1, Pallas kernels: 53.2 us -> 40.8 us  [attend_images(): return call(meta, q, direction, *state, *images)]
    unnamed x24 -> x12, local copies, waits for them, and re-layouts: 4.54 us -> 9.4 us
    pallas_call x1, Pallas kernels: 12 us -> 9.2 us  [attend_own(): return call(q, own_kv, own_kv)]
  transfers between devices with their start and end apart: 25 -> 25, of which waited for: 17 -> 17; matrix products, arithmetic and copies ran while one was open for 4% -> 4% of each run, Pallas kernels for 9% -> 8%
where the time goes in v4:
time: 144 us; the launch traced here: 143 us
  Pallas kernels  55.7 us (39%)
  starting transfers between devices  35.3 us (25%)
  waiting for transfers between devices  32.7 us (23%)
  local copies, waits for them, and re-layouts  11.3 us (8%)
  between operations  5.69 us (4%)
  other arithmetic  2.67 us (2%)
    pallas_call x1, Pallas kernels, attend_images(): return call(meta, q, direction, *state, *images)  40.8 us
    ppermute x19, starting transfers between devices, across(): return lax.ppermute(value, axis, [(i, i ^ mask) for i in range(size)])  28.5 us
    ppermute x19, waiting for transfers between devices, across(): return lax.ppermute(value, axis, [(i, i ^ mask) for i in range(size)])  21.9 us
    ppermute x6, waiting for transfers between devices, along_y(): return lax.ppermute(value, 'segment', pairs)  10.8 us
    unnamed x12, local copies, waits for them, and re-layouts  9.4 us
    pallas_call x1, Pallas kernels, attend_own(): return call(q, own_kv, own_kv)  9.2 us
    ppermute x6, starting transfers between devices, along_y(): return lax.ppermute(value, 'segment', pairs)  6.81 us
  transfers between devices with their start and end apart: 25, of which 17 were waited for; matrix products, arithmetic and copies ran while one was open for 4% of the time, Pallas kernels for 8%

profile of v4, /device:TPU:32, one launch (start us, length us, event | category | flops | bytes accessed | tf_op | source)
XLA Modules:
  0.0 143.3 jit_solution(12643813313315864380)
XLA Ops:
  0.6 3.1 %collective-permute-start.2 = (bf16[48,2048]{1,0:T(8,128)(2,1)}, bf16[48,2048]{1,0:T(8,128)(2,1)S(1)}, u32[]{:S(2)}, u32[]{:S(2)}) collective-permute-start(bf16[48,2048]{1,0:T(8,128)(2,1)} %bitcast.23), channel_id=1, source_target_pairs={{0,96},{32,0},{64,32},{96,64},{128,224},{160,128},{192,160},{224,1... | collective-permute-start | bytes 589832 | tf_op jit(solution)/shard_map/ppermute | solution.py:586
  3.7 0.6 collective-permute-start.1
  4.4 1.0 collective-permute-start
  6.0 1.4 copy.11.list_ref
  7.4 1.4 copy.12.order_ref
  8.7 0.6 pad_add_fusion.idx_ref
  9.4 1.9 %meta.1.meta_ref = s32[32]{0:T(128)} custom-call(s32[2]{0:T(128)} %pad_add_fusion.idx_ref, s32[32,8]{1,0:T(8,128)} %copy.11.list_ref, s32[256]{0:T(256)} %count_ref.1, s32[32,8]{1,0:T(8,128)} %copy.12.order_ref, s32[1]{0:T(128)S(6)} %copy.13.len_ref), custom_call_target="tpu_custom_call" | custom-call | tf_op jit(solution)/shard_map/meta/pallas_call | solution.py:77
  11.2 1.3 fusion
  14.3 1.7 %collective-permute-done = bf16[48,2048]{1,0:T(8,128)(2,1)S(1)} collective-permute-done((bf16[48,2048]{1,0:T(8,128)(2,1)}, bf16[48,2048]{1,0:T(8,128)(2,1)S(1)}, u32[]{:S(2)}, u32[]{:S(2)}) %collective-permute-start) | collective-permute-done | bytes 196640 | tf_op jit(solution)/shard_map/ppermute | solution.py:586
  16.0 1.0 select_select_fusion.1
  17.0 3.1 %collective-permute-start.3 = (bf16[48,2048]{1,0:T(8,128)(2,1)S(1)}, bf16[48,2048]{1,0:T(8,128)(2,1)S(1)}, u32[]{:S(2)}, u32[]{:S(2)}) collective-permute-start(bf16[48,2048]{1,0:T(8,128)(2,1)S(1)} %select_select_fusion.1), channel_id=1, source_target_pairs={{0,128},{32,160},{64,192},{96,224},{128,0},{160,32},{192,64},{224,... | collective-permute-start | bytes 589832 | tf_op jit(solution)/shard_map/ppermute | solution.py:591
  22.7 2.7 %collective-permute-done.3 = bf16[48,2048]{1,0:T(8,128)(2,1)S(1)} collective-permute-done((bf16[48,2048]{1,0:T(8,128)(2,1)S(1)}, bf16[48,2048]{1,0:T(8,128)(2,1)S(1)}, u32[]{:S(2)}, u32[]{:S(2)}) %collective-permute-start.3) | collective-permute-done | bytes 196640 | tf_op jit(solution)/shard_map/ppermute | solution.py:591
  25.4 1.0 select_select_fusion.rest_0_
  26.4 2.0 %collective-permute-start.6 = (bf16[48,2048]{1,0:T(8,128)(2,1)S(1)}, bf16[48,2048]{1,0:T(8,128)(2,1)S(1)}, u32[]{:S(2)}, u32[]{:S(2)}) collective-permute-start(bf16[48,2048]{1,0:T(8,128)(2,1)S(1)} %select_select_fusion.rest_0_), channel_id=1, source_target_pairs={{0,6},{1,7},{2,4},{3,5},{4,2},{5,3},{6,0},{7,1},{8,14},{9,15},{10,... | collective-permute-start | bytes 589832 | tf_op jit(solution)/shard_map/ppermute | solution.py:591
  28.4 1.5 %collective-permute-start.5 = (bf16[48,2048]{1,0:T(8,128)(2,1)S(1)}, bf16[48,2048]{1,0:T(8,128)(2,1)S(1)}, u32[]{:S(2)}, u32[]{:S(2)}) collective-permute-start(bf16[48,2048]{1,0:T(8,128)(2,1)S(1)} %select_select_fusion.rest_0_), channel_id=1, source_target_pairs={{0,4},{1,5},{2,6},{3,7},{4,0},{5,1},{6,2},{7,3},{8,12},{9,13},{10,... | collective-permute-start | bytes 589832 | tf_op jit(solution)/shard_map/ppermute | solution.py:591
  29.8 1.4 collective-permute-start.4
  31.2 2.2 %copy-done.2 = bf16[1,256,8192]{2,1,0:T(8,128)(2,1)S(1)} copy-done((bf16[1,256,8192]{2,1,0:T(8,128)(2,1)S(1)}, bf16[1,256,8192]{2,1,0:T(8,128)(2,1)}, u32[]{:S(2)}) %copy-start.2) | copy-done | bytes 4194328
  33.4 1.2 copy-done.3
  34.6 9.2 %attend_own.1 = (f32[8192,256]{1,0:T(8,128)S(1)}, f32[64,256]{1,0:T(8,128)S(1)}, f32[64,256]{1,0:T(8,128)S(1)}) custom-call(bf16[256,8192]{1,0:T(8,128)(2,1)S(1)} %bitcast.20, bf16[256,2048]{1,0:T(8,128)(2,1)S(1)} %bitcast.21, bf16[256,2048]{1,0:T(8,128)(2,1)S(1)} %bitcast.22), custom_call_target="tpu_custom_call" | custom-call | flops 2000000000 | bytes 16000000 | tf_op jit(solution)/shard_map/attend_own/pallas_call | solution.py:258
  43.8 3.3 %copy-done.4 = f32[8192,256]{1,0:T(8,128)} copy-done((f32[8192,256]{1,0:T(8,128)}, f32[8192,256]{1,0:T(8,128)S(1)}, u32[]{:S(2)}) %copy-start.4) | copy-done | bytes 8388632
  47.1 0.6 collective-permute-start.8
  49.4 40.8 %attend_images.1 = (bf16[4,48,2176]{2,1,0:T(8,128)(2,1)S(1)}, bf16[4,48,2176]{2,1,0:T(8,128)(2,1)S(1)}, f32[8,128]{1,0:T(8,128)S(1)}) custom-call(s32[32]{0:T(128)S(1)} %copy-done.1, bf16[256,8192]{1,0:T(8,128)(2,1)} %bitcast.19, f32[64,128]{1,0:T(8,128)S(1)} %bitcast.17, f32[8192,256]{1,0:T(8,128)} %copy-done.4, f32[64,256]{1,0:T(8,128)S(1)} %get-tuple-element.25.max_ref, ...), custom_call_target="tpu_custom_call" | custom-call | flops 8000000000 | bytes 18000000 | tf_op jit(solution)/shard_map/attend_images/pallas_call | solution.py:438
  90.9 1.8 %collective-permute-done.12 = f32[8,128]{1,0:T(8,128)S(1)} collective-permute-done((f32[8,128]{1,0:T(8,128)S(1)}, f32[8,128]{1,0:T(8,128)S(1)}, u32[]{:S(2)}, u32[]{:S(2)}) %collective-permute-start.12) | collective-permute-done | bytes 4128 | tf_op jit(solution)/shard_map/ppermute | solution.py:591
  92.8 1.5 %collective-permute-start.15 = (f32[8,128]{1,0:T(8,128)S(1)}, f32[8,128]{1,0:T(8,128)S(1)}, u32[]{:S(2)}, u32[]{:S(2)}) collective-permute-start(f32[8,128]{1,0:T(8,128)S(1)} %broadcast_select_fusion.rest_0_), channel_id=1, source_target_pairs={{0,6},{1,7},{2,4},{3,5},{4,2},{5,3},{6,0},{7,1},{8,14},{9,15},{10,... | collective-permute-start | bytes 12296 | tf_op jit(solution)/shard_map/ppermute | solution.py:591
  94.3 1.6 %collective-permute-start.14 = (f32[8,128]{1,0:T(8,128)S(1)}, f32[8,128]{1,0:T(8,128)S(1)}, u32[]{:S(2)}, u32[]{:S(2)}) collective-permute-start(f32[8,128]{1,0:T(8,128)S(1)} %broadcast_select_fusion.rest_0_), channel_id=1, source_target_pairs={{0,4},{1,5},{2,6},{3,7},{4,0},{5,1},{6,2},{7,3},{8,12},{9,13},{10,... | collective-permute-start | bytes 12296 | tf_op jit(solution)/shard_map/ppermute | solution.py:591
  95.8 1.4 collective-permute-start.13
  97.2 1.6 %collective-permute-done.14.rest_2_ = f32[8,128]{1,0:T(8,128)S(1)} collective-permute-done((f32[8,128]{1,0:T(8,128)S(1)}, f32[8,128]{1,0:T(8,128)S(1)}, u32[]{:S(2)}, u32[]{:S(2)}) %collective-permute-start.14) | collective-permute-done | bytes 4128 | tf_op jit(solution)/shard_map/ppermute | solution.py:591
  98.8 0.7 collective-permute-done.13.rest_1_
  99.4 1.2 scaled_sum.1
  100.7 2.4 %collective-permute-start.16 = (bf16[48,2176]{1,0:T(8,128)(2,1)S(1)}, bf16[48,2176]{1,0:T(8,128)(2,1)S(1)}, u32[]{:S(2)}, u32[]{:S(2)}) collective-permute-start(bf16[48,2176]{1,0:T(8,128)(2,1)S(1)} %get-tuple-element.34), channel_id=1, source_target_pairs={{0,2},{1,3},{2,0},{3,1},{4,6},{5,7},{6,4},{7,5},{8,10},{9,11},{10,... | collective-permute-start | bytes 626696 | tf_op jit(solution)/shard_map/ppermute | solution.py:591
  103.0 2.0 %collective-permute-start.17 = (bf16[48,2176]{1,0:T(8,128)(2,1)S(1)}, bf16[48,2176]{1,0:T(8,128)(2,1)S(1)}, u32[]{:S(2)}, u32[]{:S(2)}) collective-permute-start(bf16[48,2176]{1,0:T(8,128)(2,1)S(1)} %get-tuple-element.35), channel_id=1, source_target_pairs={{0,4},{1,5},{2,6},{3,7},{4,0},{5,1},{6,2},{7,3},{8,12},{9,13},{10,... | collective-permute-start | bytes 626696 | tf_op jit(solution)/shard_map/ppermute | solution.py:591
  105.0 1.5 %collective-permute-start.19 = (f32[8,128]{1,0:T(8,128)S(1)}, f32[8,128]{1,0:T(8,128)S(1)}, u32[]{:S(2)}, u32[]{:S(2)}) collective-permute-start(f32[8,128]{1,0:T(8,128)S(1)} %get-tuple-element.37), channel_id=1, source_target_pairs={{0,16},{1,17},{2,18},{3,19},{4,20},{5,21},{6,22},{7,23},{8,24},{9,... | collective-permute-start | bytes 12296 | tf_op jit(solution)/shard_map/ppermute | solution.py:591
  106.5 2.1 %collective-permute-done.19 = f32[8,128]{1,0:T(8,128)S(1)} collective-permute-done((f32[8,128]{1,0:T(8,128)S(1)}, f32[8,128]{1,0:T(8,128)S(1)}, u32[]{:S(2)}, u32[]{:S(2)}) %collective-permute-start.19) | collective-permute-done | bytes 4128 | tf_op jit(solution)/shard_map/ppermute | solution.py:591
  108.7 5.5 %collective-permute-start.20 = (f32[8,128]{1,0:T(8,128)S(1)}, f32[8,128]{1,0:T(8,128)S(1)}, u32[]{:S(2)}, u32[]{:S(2)}) collective-permute-start(f32[8,128]{1,0:T(8,128)S(1)} %add.8.l0_ref), channel_id=1, source_target_pairs={{0,8},{1,9},{2,10},{3,11},{4,12},{5,13},{6,14},{7,15},{8,0},{9,1},... | collective-permute-start | bytes 12296 | tf_op jit(solution)/shard_map/ppermute | solution.py:591
  114.1 2.1 %collective-permute-done.20.l1_ref = f32[8,128]{1,0:T(8,128)S(1)} collective-permute-done((f32[8,128]{1,0:T(8,128)S(1)}, f32[8,128]{1,0:T(8,128)S(1)}, u32[]{:S(2)}, u32[]{:S(2)}) %collective-permute-start.20) | collective-permute-done | bytes 4128 | tf_op jit(solution)/shard_map/ppermute | solution.py:591
  116.2 2.6 %collective-permute-done.17.b_ref = bf16[48,2176]{1,0:T(8,128)(2,1)S(1)} collective-permute-done((bf16[48,2176]{1,0:T(8,128)(2,1)S(1)}, bf16[48,2176]{1,0:T(8,128)(2,1)S(1)}, u32[]{:S(2)}, u32[]{:S(2)}) %collective-permute-start.17) | collective-permute-done | bytes 208928 | tf_op jit(solution)/shard_map/ppermute | solution.py:591
  118.9 3.3 %collective-permute-done.18.c_ref = bf16[48,2176]{1,0:T(8,128)(2,1)S(1)} collective-permute-done((bf16[48,2176]{1,0:T(8,128)(2,1)S(1)}, bf16[48,2176]{1,0:T(8,128)(2,1)S(1)}, u32[]{:S(2)}, u32[]{:S(2)}) %collective-permute-start.18) | collective-permute-done | bytes 208928 | tf_op jit(solution)/shard_map/ppermute | solution.py:591
  122.1 0.7 group_sum.1.s0
  122.9 1.2 collective-permute-start.22
  124.1 0.8 collective-permute-start.21
  124.9 5.2 %collective-permute-done.23.s3 = bf16[48,2176]{1,0:T(8,128)(2,1)S(1)} collective-permute-done((bf16[48,2176]{1,0:T(8,128)(2,1)S(1)}, bf16[48,2176]{1,0:T(8,128)(2,1)S(1)}, u32[]{:S(2)}, u32[]{:S(2)}) %collective-permute-start.23) | collective-permute-done | bytes 208928 | tf_op jit(solution)/shard_map/ppermute | solution.py:586
  130.1 1.7 %collective-permute-done.22.s2 = bf16[48,2176]{1,0:T(8,128)(2,1)S(1)} collective-permute-done((bf16[48,2176]{1,0:T(8,128)(2,1)S(1)}, bf16[48,2176]{1,0:T(8,128)(2,1)S(1)}, u32[]{:S(2)}, u32[]{:S(2)}) %collective-permute-start.22) | collective-permute-done | bytes 208928 | tf_op jit(solution)/shard_map/ppermute | solution.py:586
  131.8 2.2 %collective-permute-done.21.s1 = bf16[48,2176]{1,0:T(8,128)(2,1)S(1)} collective-permute-done((bf16[48,2176]{1,0:T(8,128)(2,1)S(1)}, bf16[48,2176]{1,0:T(8,128)(2,1)S(1)}, u32[]{:S(2)}, u32[]{:S(2)}) %collective-permute-start.21) | collective-permute-done | bytes 208928 | tf_op jit(solution)/shard_map/ppermute | solution.py:586
  134.0 1.1 sort_by_owner.1
  135.1 3.1 %collective-permute-start.24 = (bf16[48,2176]{1,0:T(8,128)(2,1)S(1)}, bf16[48,2176]{1,0:T(8,128)(2,1)S(1)}, u32[]{:S(2)}, u32[]{:S(2)}) collective-permute-start(bf16[48,2176]{1,0:T(8,128)(2,1)S(1)} %get-tuple-element.39), channel_id=1, source_target_pairs={{0,128},{32,160},{64,192},{96,224},{128,0},{160,32},{192,64},{224,... | collective-permute-start | bytes 626696 | tf_op jit(solution)/shard_map/ppermute | solution.py:591
  138.2 0.5 slice.11
  138.7 3.8 %collective-permute-done.24.recv_ref = bf16[48,2176]{1,0:T(8,128)(2,1)S(1)} collective-permute-done((bf16[48,2176]{1,0:T(8,128)(2,1)S(1)}, bf16[48,2176]{1,0:T(8,128)(2,1)S(1)}, u32[]{:S(2)}, u32[]{:S(2)}) %collective-permute-start.24) | collective-permute-done | bytes 208928 | tf_op jit(solution)/shard_map/ppermute | solution.py:591
  142.4 0.8 last_sum.1
  (29 shorter events, 2.5 us)
Async XLA Ops:
  0.6 48.8 %copy-start = (f32[8192]{0:T(1024)S(1)}, f32[8192]{0:T(1024)}, u32[]{:S(2)}) copy-start(f32[8192]{0:T(1024)} %param.15) | copy-start | bytes 98308
  0.6 13.6 %collective-permute-start.2 = (bf16[48,2048]{1,0:T(8,128)(2,1)}, bf16[48,2048]{1,0:T(8,128)(2,1)S(1)}, u32[]{:S(2)}, u32[]{:S(2)}) collective-permute-start(bf16[48,2048]{1,0:T(8,128)(2,1)} %bitcast.23), channel_id=1, source_target_pairs={{0,96},{32,0},{64,32},{96,64},{128,224},{160,128},{192,160},{224,1... | collective-permute-start | bytes 589832 | tf_op jit(solution)/shard_map/ppermute | solution.py:586
  3.7 10.5 %collective-permute-start.1 = (bf16[48,2048]{1,0:T(8,128)(2,1)}, bf16[48,2048]{1,0:T(8,128)(2,1)S(1)}, u32[]{:S(2)}, u32[]{:S(2)}) collective-permute-start(bf16[48,2048]{1,0:T(8,128)(2,1)} %bitcast.24), channel_id=1, source_target_pairs={{0,64},{32,96},{64,0},{96,32},{128,192},{160,224},{192,128},{224,1... | collective-permute-start | bytes 589832 | tf_op jit(solution)/shard_map/ppermute | solution.py:586
  4.4 11.7 %collective-permute-start = (bf16[48,2048]{1,0:T(8,128)(2,1)}, bf16[48,2048]{1,0:T(8,128)(2,1)S(1)}, u32[]{:S(2)}, u32[]{:S(2)}) collective-permute-start(bf16[48,2048]{1,0:T(8,128)(2,1)} %bitcast.25), channel_id=1, source_target_pairs={{0,32},{32,64},{64,96},{96,0},{128,160},{160,192},{192,224},{224,1... | collective-permute-start | bytes 589832 | tf_op jit(solution)/shard_map/ppermute | solution.py:586
  11.2 38.2 %copy-start.1 = (s32[32]{0:T(128)S(1)}, s32[32]{0:T(128)}, u32[]{:S(2)}) copy-start(s32[32]{0:T(128)} %meta.1.meta_ref) | copy-start | bytes 388
  17.0 8.4 %collective-permute-start.3 = (bf16[48,2048]{1,0:T(8,128)(2,1)S(1)}, bf16[48,2048]{1,0:T(8,128)(2,1)S(1)}, u32[]{:S(2)}, u32[]{:S(2)}) collective-permute-start(bf16[48,2048]{1,0:T(8,128)(2,1)S(1)} %select_select_fusion.1), channel_id=1, source_target_pairs={{0,128},{32,160},{64,192},{96,224},{128,0},{160,32},{192,64},{224,... | collective-permute-start | bytes 589832 | tf_op jit(solution)/shard_map/ppermute | solution.py:591
  26.4 20.7 %collective-permute-start.6 = (bf16[48,2048]{1,0:T(8,128)(2,1)S(1)}, bf16[48,2048]{1,0:T(8,128)(2,1)S(1)}, u32[]{:S(2)}, u32[]{:S(2)}) collective-permute-start(bf16[48,2048]{1,0:T(8,128)(2,1)S(1)} %select_select_fusion.rest_0_), channel_id=1, source_target_pairs={{0,6},{1,7},{2,4},{3,5},{4,2},{5,3},{6,0},{7,1},{8,14},{9,15},{10,... | collective-permute-start | bytes 589832 | tf_op jit(solution)/shard_map/ppermute | solution.py:591
  28.4 18.7 %collective-permute-start.5 = (bf16[48,2048]{1,0:T(8,128)(2,1)S(1)}, bf16[48,2048]{1,0:T(8,128)(2,1)S(1)}, u32[]{:S(2)}, u32[]{:S(2)}) collective-permute-start(bf16[48,2048]{1,0:T(8,128)(2,1)S(1)} %select_select_fusion.rest_0_), channel_id=1, source_target_pairs={{0,4},{1,5},{2,6},{3,7},{4,0},{5,1},{6,2},{7,3},{8,12},{9,13},{10,... | collective-permute-start | bytes 589832 | tf_op jit(solution)/shard_map/ppermute | solution.py:591
  29.8 17.3 %collective-permute-start.4 = (bf16[48,2048]{1,0:T(8,128)(2,1)S(1)}, bf16[48,2048]{1,0:T(8,128)(2,1)S(1)}, u32[]{:S(2)}, u32[]{:S(2)}) collective-permute-start(bf16[48,2048]{1,0:T(8,128)(2,1)S(1)} %select_select_fusion.rest_0_), channel_id=1, source_target_pairs={{0,2},{1,3},{2,0},{3,1},{4,6},{5,7},{6,4},{7,5},{8,10},{9,11},{10,... | collective-permute-start | bytes 589832 | tf_op jit(solution)/shard_map/ppermute | solution.py:591
  31.2 2.2 %copy-start.2 = (bf16[1,256,8192]{2,1,0:T(8,128)(2,1)S(1)}, bf16[1,256,8192]{2,1,0:T(8,128)(2,1)}, u32[]{:S(2)}) copy-start(bf16[1,256,8192]{2,1,0:T(8,128)(2,1)} %param.8) | copy-start | bytes 12582916
  33.4 1.2 copy-start.3
  43.8 3.3 %copy-start.4 = (f32[8192,256]{1,0:T(8,128)}, f32[8192,256]{1,0:T(8,128)S(1)}, u32[]{:S(2)}) copy-start(f32[8192,256]{1,0:T(8,128)S(1)} %get-tuple-element.23.acc_hbm) | copy-start | bytes 25165828
  47.1 1.4 %collective-permute-start.7 = (bf16[48,2048]{1,0:T(8,128)(2,1)S(1)}, bf16[48,2048]{1,0:T(8,128)(2,1)S(1)}, u32[]{:S(2)}, u32[]{:S(2)}) collective-permute-start(bf16[48,2048]{1,0:T(8,128)(2,1)S(1)} %select_select_fusion.rest_0_), channel_id=1, source_target_pairs={{0,1},{1,0},{2,3},{3,2},{4,5},{5,4},{6,7},{7,6},{8,9},{9,8},{10,11... | collective-permute-start | bytes 589832 | tf_op jit(solution)/shard_map/ppermute | solution.py:591
  47.1 1.7 %collective-permute-start.8 = (bf16[48,2048]{1,0:T(8,128)(2,1)S(1)}, bf16[48,2048]{1,0:T(8,128)(2,1)S(1)}, u32[]{:S(2)}, u32[]{:S(2)}) collective-permute-start(bf16[48,2048]{1,0:T(8,128)(2,1)S(1)} %collective-permute-done.4.rest_1_), channel_id=1, source_target_pairs={{0,1},{1,0},{2,3},{3,2},{4,5},{5,4},{6,7},{7,6},{8,9},{9,8},{10,11... | collective-permute-start | bytes 589832 | tf_op jit(solution)/shard_map/ppermute | solution.py:591
  47.7 1.4 %collective-permute-start.9 = (bf16[48,2048]{1,0:T(8,128)(2,1)S(1)}, bf16[48,2048]{1,0:T(8,128)(2,1)S(1)}, u32[]{:S(2)}, u32[]{:S(2)}) collective-permute-start(bf16[48,2048]{1,0:T(8,128)(2,1)S(1)} %collective-permute-done.5.rest_2_), channel_id=1, source_target_pairs={{0,1},{1,0},{2,3},{3,2},{4,5},{5,4},{6,7},{7,6},{8,9},{9,8},{10,11... | collective-permute-start | bytes 589832 | tf_op jit(solution)/shard_map/ppermute | solution.py:591
  47.8 1.6 %collective-permute-start.10 = (bf16[48,2048]{1,0:T(8,128)(2,1)S(1)}, bf16[48,2048]{1,0:T(8,128)(2,1)S(1)}, u32[]{:S(2)}, u32[]{:S(2)}) collective-permute-start(bf16[48,2048]{1,0:T(8,128)(2,1)S(1)} %collective-permute-done.6.rest_3_), channel_id=1, source_target_pairs={{0,1},{1,0},{2,3},{3,2},{4,5},{5,4},{6,7},{7,6},{8,9},{9,8},{10,11... | collective-permute-start | bytes 589832 | tf_op jit(solution)/shard_map/ppermute | solution.py:591
  90.3 9.2 %collective-permute-start.11 = (bf16[4,48,2176]{2,1,0:T(8,128)(2,1)S(1)}, bf16[4,48,2176]{2,1,0:T(8,128)(2,1)S(1)}, u32[]{:S(2)}, u32[]{:S(2)}) collective-permute-start(bf16[4,48,2176]{2,1,0:T(8,128)(2,1)S(1)} %get-tuple-element.31), channel_id=1, source_target_pairs={{0,1},{1,0},{2,3},{3,2},{4,5},{5,4},{6,7},{7,6},{8,9},{9,8},{10,11... | collective-permute-start | bytes 2506760 | tf_op jit(solution)/shard_map/ppermute | solution.py:591
  90.6 2.1 %collective-permute-start.12 = (f32[8,128]{1,0:T(8,128)S(1)}, f32[8,128]{1,0:T(8,128)S(1)}, u32[]{:S(2)}, u32[]{:S(2)}) collective-permute-start(f32[8,128]{1,0:T(8,128)S(1)} %get-tuple-element.32), channel_id=1, source_target_pairs={{0,1},{1,0},{2,3},{3,2},{4,5},{5,4},{6,7},{7,6},{8,9},{9,8},{10,11... | collective-permute-start | bytes 12296 | tf_op jit(solution)/shard_map/ppermute | solution.py:591
  92.8 4.4 %collective-permute-start.15 = (f32[8,128]{1,0:T(8,128)S(1)}, f32[8,128]{1,0:T(8,128)S(1)}, u32[]{:S(2)}, u32[]{:S(2)}) collective-permute-start(f32[8,128]{1,0:T(8,128)S(1)} %broadcast_select_fusion.rest_0_), channel_id=1, source_target_pairs={{0,6},{1,7},{2,4},{3,5},{4,2},{5,3},{6,0},{7,1},{8,14},{9,15},{10,... | collective-permute-start | bytes 12296 | tf_op jit(solution)/shard_map/ppermute | solution.py:591
  94.3 4.5 %collective-permute-start.14 = (f32[8,128]{1,0:T(8,128)S(1)}, f32[8,128]{1,0:T(8,128)S(1)}, u32[]{:S(2)}, u32[]{:S(2)}) collective-permute-start(f32[8,128]{1,0:T(8,128)S(1)} %broadcast_select_fusion.rest_0_), channel_id=1, source_target_pairs={{0,4},{1,5},{2,6},{3,7},{4,0},{5,1},{6,2},{7,3},{8,12},{9,13},{10,... | collective-permute-start | bytes 12296 | tf_op jit(solution)/shard_map/ppermute | solution.py:591
  95.8 3.6 %collective-permute-start.13 = (f32[8,128]{1,0:T(8,128)S(1)}, f32[8,128]{1,0:T(8,128)S(1)}, u32[]{:S(2)}, u32[]{:S(2)}) collective-permute-start(f32[8,128]{1,0:T(8,128)S(1)} %broadcast_select_fusion.rest_0_), channel_id=1, source_target_pairs={{0,2},{1,3},{2,0},{3,1},{4,6},{5,7},{6,4},{7,5},{8,10},{9,11},{10,... | collective-permute-start | bytes 12296 | tf_op jit(solution)/shard_map/ppermute | solution.py:591
  100.7 15.6 %collective-permute-start.16 = (bf16[48,2176]{1,0:T(8,128)(2,1)S(1)}, bf16[48,2176]{1,0:T(8,128)(2,1)S(1)}, u32[]{:S(2)}, u32[]{:S(2)}) collective-permute-start(bf16[48,2176]{1,0:T(8,128)(2,1)S(1)} %get-tuple-element.34), channel_id=1, source_target_pairs={{0,2},{1,3},{2,0},{3,1},{4,6},{5,7},{6,4},{7,5},{8,10},{9,11},{10,... | collective-permute-start | bytes 626696 | tf_op jit(solution)/shard_map/ppermute | solution.py:591
  103.0 15.8 %collective-permute-start.17 = (bf16[48,2176]{1,0:T(8,128)(2,1)S(1)}, bf16[48,2176]{1,0:T(8,128)(2,1)S(1)}, u32[]{:S(2)}, u32[]{:S(2)}) collective-permute-start(bf16[48,2176]{1,0:T(8,128)(2,1)S(1)} %get-tuple-element.35), channel_id=1, source_target_pairs={{0,4},{1,5},{2,6},{3,7},{4,0},{5,1},{6,2},{7,3},{8,12},{9,13},{10,... | collective-permute-start | bytes 626696 | tf_op jit(solution)/shard_map/ppermute | solution.py:591
  105.0 17.1 %collective-permute-start.18 = (bf16[48,2176]{1,0:T(8,128)(2,1)S(1)}, bf16[48,2176]{1,0:T(8,128)(2,1)S(1)}, u32[]{:S(2)}, u32[]{:S(2)}) collective-permute-start(bf16[48,2176]{1,0:T(8,128)(2,1)S(1)} %get-tuple-element.36), channel_id=1, source_target_pairs={{0,6},{1,7},{2,4},{3,5},{4,2},{5,3},{6,0},{7,1},{8,14},{9,15},{10,... | collective-permute-start | bytes 626696 | tf_op jit(solution)/shard_map/ppermute | solution.py:591
  105.0 3.6 %collective-permute-start.19 = (f32[8,128]{1,0:T(8,128)S(1)}, f32[8,128]{1,0:T(8,128)S(1)}, u32[]{:S(2)}, u32[]{:S(2)}) collective-permute-start(f32[8,128]{1,0:T(8,128)S(1)} %get-tuple-element.37), channel_id=1, source_target_pairs={{0,16},{1,17},{2,18},{3,19},{4,20},{5,21},{6,22},{7,23},{8,24},{9,... | collective-permute-start | bytes 12296 | tf_op jit(solution)/shard_map/ppermute | solution.py:591
  108.7 7.6 %collective-permute-start.20 = (f32[8,128]{1,0:T(8,128)S(1)}, f32[8,128]{1,0:T(8,128)S(1)}, u32[]{:S(2)}, u32[]{:S(2)}) collective-permute-start(f32[8,128]{1,0:T(8,128)S(1)} %add.8.l0_ref), channel_id=1, source_target_pairs={{0,8},{1,9},{2,10},{3,11},{4,12},{5,13},{6,14},{7,15},{8,0},{9,1},... | collective-permute-start | bytes 12296 | tf_op jit(solution)/shard_map/ppermute | solution.py:591
  122.8 7.3 %collective-permute-start.23 = (bf16[48,2176]{1,0:T(8,128)(2,1)S(1)}, bf16[48,2176]{1,0:T(8,128)(2,1)S(1)}, u32[]{:S(2)}, u32[]{:S(2)}) collective-permute-start(bf16[48,2176]{1,0:T(8,128)(2,1)S(1)} %group_sum.1.s0), channel_id=1, source_target_pairs={{0,96},{32,0},{64,32},{96,64},{128,224},{160,128},{192,160},{224,1... | collective-permute-start | bytes 626696 | tf_op jit(solution)/shard_map/ppermute | solution.py:586
  122.9 8.9 %collective-permute-start.22 = (bf16[48,2176]{1,0:T(8,128)(2,1)S(1)}, bf16[48,2176]{1,0:T(8,128)(2,1)S(1)}, u32[]{:S(2)}, u32[]{:S(2)}) collective-permute-start(bf16[48,2176]{1,0:T(8,128)(2,1)S(1)} %group_sum.1.s0), channel_id=1, source_target_pairs={{0,64},{32,96},{64,0},{96,32},{128,192},{160,224},{192,128},{224,1... | collective-permute-start | bytes 626696 | tf_op jit(solution)/shard_map/ppermute | solution.py:586
  124.1 9.9 %collective-permute-start.21 = (bf16[48,2176]{1,0:T(8,128)(2,1)S(1)}, bf16[48,2176]{1,0:T(8,128)(2,1)S(1)}, u32[]{:S(2)}, u32[]{:S(2)}) collective-permute-start(bf16[48,2176]{1,0:T(8,128)(2,1)S(1)} %group_sum.1.s0), channel_id=1, source_target_pairs={{0,32},{32,64},{64,96},{96,0},{128,160},{160,192},{192,224},{224,1... | collective-permute-start | bytes 626696 | tf_op jit(solution)/shard_map/ppermute | solution.py:586
  135.1 7.4 %collective-permute-start.24 = (bf16[48,2176]{1,0:T(8,128)(2,1)S(1)}, bf16[48,2176]{1,0:T(8,128)(2,1)S(1)}, u32[]{:S(2)}, u32[]{:S(2)}) collective-permute-start(bf16[48,2176]{1,0:T(8,128)(2,1)S(1)} %get-tuple-element.39), channel_id=1, source_target_pairs={{0,128},{32,160},{64,192},{96,224},{128,0},{160,32},{192,64},{224,... | collective-permute-start | bytes 626696 | tf_op jit(solution)/shard_map/ppermute | solution.py:591
